TPU v7x, 32 devices: a whole 2x2x4 slice. The times are simulated.
32 devices in a mesh: gx: 4 (over y, core), gy: 8 (over z, x).
Axes of the slice: x: 2, y: 2, z: 4, core: 2. Of those that a mesh axis runs over, the one named last changes fastest.
Arguments:
- near_tiles: bfloat16 [4, 8, 32, 20, 128, 128], P('gx', 'gy'), may hold values from -0.125 to 0.125
- block: bfloat16 [4, 8, 4096, 64], P('gx', 'gy'), may hold values from -7 to 7, as said below
- adjacency: int32 [4, 8, 32, 20], P('gx', 'gy'), may hold values from 0 to 1023, as said below
Outputs:
- basis: float32 [4, 8, 4096, 64], P('gx', 'gy')
- r_factor: float32 [64, 64], replicated
Inputs may be any that keep to these rules, and one draw needn't show every extreme that they name: `adjacency`: entry 0 of each row tile is the row tile itself; every entry names a tile of the device of its row tile or of a device whose gx and gy indices each differ by at most one, without wrapping. `block`: entries are real values of order one, within -7 to 7.
All inputs are finite; a program needn't handle non-finite values.
Results may differ from a plain program's by a relative error of at most 0.0003.
Values may be sent and summed in bfloat16 or wider, within the bound.
No kernel may reach another device: no remote copies, remote signals or barrier semaphores. Data moves between devices by JAX's collectives and lax.ppermute only.
A program may use at most 128 MiB of HBM per device.

v0:
```python
import jax
import jax.numpy as jnp
from jax import lax
from jax.sharding import PartitionSpec as P


def extended(shard, sides, width):
    for axis, dim in sides:
        size, length = (lax.axis_size(axis), shard.shape[dim])
        up = [(i, (i + 1) % size) for i in range(size - 1)]
        down = [(j, i) for i, j in up]
        last = lax.slice_in_dim(shard, length - width, length, axis=dim)
        initial = lax.slice_in_dim(shard, 0, width, axis=dim)
        before = lax.ppermute(last, axis, up)
        after = lax.ppermute(initial, axis, down)
        shard = jnp.concatenate([before, shard, after], axis=dim)
    return shard


def swapped(value, axis, stride):
    mask = 2**stride
    pairs = [(source, source ^ mask) for source in range(lax.axis_size(axis))]
    return lax.ppermute(value, axis, pairs)


def upper_cholesky(matrix):
    return jnp.linalg.cholesky(matrix).T


def gram_of(matrix):
    return jnp.dot(matrix.T, matrix, precision=lax.Precision.HIGHEST)


def right_solve(values, factor):
    return jax.scipy.linalg.solve_triangular(factor.T, values.T, lower=True).T


def shards(near_tiles, block, adjacency):
    tiles_dev = adjacency.shape[2]
    tile_rows = near_tiles.shape[4]
    columns = block.shape[3]
    gy_count = lax.axis_size("gy")
    neighbours = extended(block, (("gx", 0), ("gy", 1)), 1)
    flat_rows = neighbours.reshape(9 * tiles_dev, tile_rows, columns)
    links = adjacency[0, 0]
    owner = links // tiles_dev
    offset_x = owner // gy_count - lax.axis_index("gx") + 1
    offset_y = owner % gy_count - lax.axis_index("gy") + 1
    local_tile = (offset_x * 3 + offset_y) * tiles_dev + links % tiles_dev
    picked = flat_rows[local_tile]
    product = jnp.einsum(
        "rnij,rnjk->rik", near_tiles[0, 0], picked, preferred_element_type=jnp.float32
    )
    image = product.reshape(tiles_dev * tile_rows, columns)
    scale = jnp.sqrt(jnp.float32(image.shape[0] * lax.axis_size("gx") * gy_count))
    factor = upper_cholesky(gram_of(image))
    for level in range(gy_count.bit_length() - 1):
        partner = swapped(factor, "gy", level)
        factor = upper_cholesky(gram_of(factor) + gram_of(partner))
    for level in range(lax.axis_size("gx").bit_length() - 1):
        partner = swapped(factor, "gx", level)
        factor = upper_cholesky(gram_of(factor) + gram_of(partner))
    ortho = right_solve(image, factor)
    basis = (ortho * scale).reshape(1, 1, image.shape[0], columns)
    return (basis, factor / scale)


def solution(mesh):
    in_specs = (
        P("gx", "gy", None, None, None, None),
        P("gx", "gy", None, None),
        P("gx", "gy", None, None),
    )
    out_specs = (P("gx", "gy", None, None), P())
    return jax.shard_map(shards, mesh=mesh, in_specs=in_specs, out_specs=out_specs, check_vma=False)
```

profile of v0, /device:TPU:0, one launch (start us, length us, event | category | flops | bytes accessed | tf_op | source)
XLA Modules:
  0.0 218.2 jit_solution(101984643513786746)
XLA Ops:
  0.6 2.4 %collective-permute-start = (bf16[1,1,4096,64]{2,3,1,0:T(8,128)(2,1)}, bf16[1,1,4096,64]{2,3,1,0:T(8,128)(2,1)S(1)}, u32[]{:S(2)}, u32[]{:S(2)}) collective-permute-start(bf16[1,1,4096,64]{2,3,1,0:T(8,128)(2,1)} %param.5), channel_id=1, source_target_pairs={{0,8},{8,16},{16,24},{1,9},{9,17},{17,25},{2,10},{10,18},{18,26},{... | collective-permute-start | bytes 1572872 | tf_op jit(solution)/shard_map/ppermute | solution.py:14
  3.0 1.3 collective-permute-start.1
  4.8 1.1 constant_dynamic-update-slice_fusion.1
  5.8 3.3 %collective-permute-done.1 = bf16[1,1,4096,64]{2,3,1,0:T(8,128)(2,1)S(1)} collective-permute-done((bf16[1,1,4096,64]{2,3,1,0:T(8,128)(2,1)}, bf16[1,1,4096,64]{2,3,1,0:T(8,128)(2,1)S(1)}, u32[]{:S(2)}, u32[]{:S(2)}) %collective-permute-start.1) | collective-permute-done | bytes 524320 | tf_op jit(solution)/shard_map/ppermute | solution.py:15
  9.2 1.3 collective-permute-start.3
  10.5 5.7 %collective-permute-start.2 = (bf16[3,1,4096,64]{2,3,1,0:T(8,128)(2,1)S(1)}, bf16[3,1,4096,64]{2,3,1,0:T(8,128)(2,1)}, u32[]{:S(2)}, u32[]{:S(2)}) collective-permute-start(bf16[3,1,4096,64]{2,3,1,0:T(8,128)(2,1)S(1)} %constant_dynamic-update-slice_fusion), channel_id=1, source_target_pairs={{0,1},{1,2},{2,3},{3,4},{4,5},{5,6},{6,7},{8,9},{9,10},{10,11},{11... | collective-permute-start | bytes 4718600 | tf_op jit(solution)/shard_map/ppermute | solution.py:14
  16.2 0.9 compare_select_fusion
  17.3 24.5 %collective-permute-done.3 = bf16[3,1,4096,64]{2,3,1,0:T(8,128)(2,1)S(1)} collective-permute-done((bf16[3,1,4096,64]{2,3,1,0:T(8,128)(2,1)S(1)}, bf16[3,1,4096,64]{2,3,1,0:T(8,128)(2,1)S(1)}, u32[]{:S(2)}, u32[]{:S(2)}) %collective-permute-start.3) | collective-permute-done | bytes 1572896 | tf_op jit(solution)/shard_map/ppermute | solution.py:15
  41.8 40.1 %collective-permute-done.2 = bf16[3,1,4096,64]{2,3,1,0:T(8,128)(2,1)} collective-permute-done((bf16[3,1,4096,64]{2,3,1,0:T(8,128)(2,1)S(1)}, bf16[3,1,4096,64]{2,3,1,0:T(8,128)(2,1)}, u32[]{:S(2)}, u32[]{:S(2)}) %collective-permute-start.2) | collective-permute-done | bytes 1572896 | tf_op jit(solution)/shard_map/ppermute | solution.py:14
  81.9 1.7 pad_maximum_fusion
  83.6 6.7 %copy.22 = bf16[3,3,4096,64]{2,1,0,3:T(4,128)(2,1)} copy(bf16[3,3,4096,64]{2,3,1,0:T(8,128)(2,1)S(1)} %pad_maximum_fusion) | data formatting | bytes 9437184 | tf_op jit(solution)/shard_map/concatenate | solution.py:16
  90.3 13.5 %reshape.214 = bf16[288,128,64]{1,0,2:T(8,128)(2,1)} reshape(bf16[3,3,4096,64]{2,1,0,3:T(4,128)(2,1)} %copy.22) | data formatting | bytes 9437184 | tf_op jit(solution)/shard_map/reshape | solution.py:44
  103.8 6.4 %copy.24 = bf16[288,128,64]{1,2,0:T(8,128)(2,1)} copy(bf16[288,128,64]{1,0,2:T(8,128)(2,1)} %reshape.214) | data formatting | bytes 9437184 | tf_op jit(solution)/shard_map/reshape | solution.py:44
  110.2 22.2 %gather_fusion = bf16[640,128,64]{1,2,0:T(8,128)(2,1)} fusion(bf16[288,128,64]{1,2,0:T(8,128)(2,1)} %copy.24, s32[1024]{0:T(1024)S(1)} %pad_clamp_fusion), kind=kCustom, calls=%fused_computation | custom fusion | bytes 20974080 | tf_op jit(solution)/shard_map/gather | solution.py:50
  132.3 13.9 %fusion = f32[32,64,128,1]{2,1,3,0:T(8,128)S(1)} fusion(bf16[32,20,128,64]{2,3,1,0:T(8,128)(2,1)} %bitcast.92, bf16[1,1,32,20,128,128]{5,4,3,2,1,0:T(8,128)(2,1)} %param.4), kind=kOutput, calls=%fused_computation.1 | convolution fusion | flops 1342177280 | bytes 32505856 | tf_op jit(solution)/shard_map/rnij,rnjk->rik/dot_general | solution.py:51
  146.3 1.0 convolution_bitcast_fusion
  147.4 5.8 %cholesky.104 = f32[64,64]{1,0:T(8,128)S(1)} custom-call(f32[64,64]{1,0:T(8,128)S(1)} %fusion.12), custom_call_target="Cholesky" | custom-call | tf_op jit(solution)/shard_map/jit(cholesky)/cholesky | solution.py:27
  154.5 2.7 %collective-permute-start.4 = (f32[64,64]{0,1:T(8,128)S(1)}, f32[64,64]{0,1:T(8,128)S(1)}, u32[]{:S(2)}, u32[]{:S(2)}) collective-permute-start(f32[64,64]{0,1:T(8,128)S(1)} %fusion.23), channel_id=1, source_target_pairs={{0,1},{1,0},{2,3},{3,2},{4,5},{5,4},{6,7},{7,6},{8,9},{9,8},{10,11... | collective-permute-start | bytes 49160 | tf_op jit(solution)/shard_map/ppermute | solution.py:23
  158.0 1.1 collective-permute-done.4
  159.4 5.8 %cholesky.115 = f32[64,64]{1,0:T(8,128)S(1)} custom-call(f32[64,64]{1,0:T(8,128)S(1)} %fusion.11), custom_call_target="Cholesky" | custom-call | tf_op jit(solution)/shard_map/jit(cholesky)/cholesky | solution.py:27
  166.6 1.6 collective-permute-start.5
  169.0 1.5 collective-permute-done.5
  170.8 5.8 %cholesky.126 = f32[64,64]{1,0:T(8,128)S(1)} custom-call(f32[64,64]{1,0:T(8,128)S(1)} %fusion.10), custom_call_target="Cholesky" | custom-call | tf_op jit(solution)/shard_map/jit(cholesky)/cholesky | solution.py:27
  178.0 2.7 %collective-permute-start.6 = (f32[64,64]{0,1:T(8,128)S(1)}, f32[64,64]{0,1:T(8,128)S(1)}, u32[]{:S(2)}, u32[]{:S(2)}) collective-permute-start(f32[64,64]{0,1:T(8,128)S(1)} %fusion.27), channel_id=1, source_target_pairs={{0,4},{1,5},{2,6},{3,7},{4,0},{5,1},{6,2},{7,3},{8,12},{9,13},{10,... | collective-permute-start | bytes 49160 | tf_op jit(solution)/shard_map/ppermute | solution.py:23
  181.5 1.4 collective-permute-done.6
  183.2 5.8 %cholesky.137 = f32[64,64]{1,0:T(8,128)S(1)} custom-call(f32[64,64]{1,0:T(8,128)S(1)} %fusion.9), custom_call_target="Cholesky" | custom-call | tf_op jit(solution)/shard_map/jit(cholesky)/cholesky | solution.py:27
  191.9 5.8 %cholesky.148 = f32[64,64]{1,0:T(8,128)S(1)} custom-call(f32[64,64]{1,0:T(8,128)S(1)} %fusion.8), custom_call_target="Cholesky" | custom-call | tf_op jit(solution)/shard_map/jit(cholesky)/cholesky | solution.py:27
  199.2 0.8 fusion.32
  200.0 3.1 %collective-permute-done.8 = f32[64,64]{0,1:T(8,128)S(1)} collective-permute-done((f32[64,64]{0,1:T(8,128)S(1)}, f32[64,64]{0,1:T(8,128)S(1)}, u32[]{:S(2)}, u32[]{:S(2)}) %collective-permute-start.8) | collective-permute-done | bytes 16416 | tf_op jit(solution)/shard_map/ppermute | solution.py:23
  203.4 5.8 %cholesky.159 = f32[64,64]{1,0:T(8,128)S(1)} custom-call(f32[64,64]{1,0:T(8,128)S(1)} %fusion.7), custom_call_target="Cholesky" | custom-call | tf_op jit(solution)/shard_map/jit(cholesky)/cholesky | solution.py:27
  211.3 4.9 %custom-call.6 = f32[1,64,64]{1,2,0:T(8,128)S(1)} custom-call(f32[1,64,64]{2,1,0:T(8,128)S(1)} %get-tuple-element.8), custom_call_target="InvertDiagBlocksLowerTriangular" | custom-call | tf_op jit(solution)/shard_map/jit(_solve_triangular)/triangular_solve | solution.py:35
  216.2 2.0 fusion.2
  (49 shorter events, 14.5 us)
Async XLA Ops:
  0.6 4.1 %collective-permute-start = (bf16[1,1,4096,64]{2,3,1,0:T(8,128)(2,1)}, bf16[1,1,4096,64]{2,3,1,0:T(8,128)(2,1)S(1)}, u32[]{:S(2)}, u32[]{:S(2)}) collective-permute-start(bf16[1,1,4096,64]{2,3,1,0:T(8,128)(2,1)} %param.5), channel_id=1, source_target_pairs={{0,8},{8,16},{16,24},{1,9},{9,17},{17,25},{2,10},{10,18},{18,26},{... | collective-permute-start | bytes 1572872 | tf_op jit(solution)/shard_map/ppermute | solution.py:14
  3.0 6.1 %collective-permute-start.1 = (bf16[1,1,4096,64]{2,3,1,0:T(8,128)(2,1)}, bf16[1,1,4096,64]{2,3,1,0:T(8,128)(2,1)S(1)}, u32[]{:S(2)}, u32[]{:S(2)}) collective-permute-start(bf16[1,1,4096,64]{2,3,1,0:T(8,128)(2,1)} %param.5), channel_id=1, source_target_pairs={{8,0},{16,8},{24,16},{9,1},{17,9},{25,17},{10,2},{18,10},{26,18},{... | collective-permute-start | bytes 1572872 | tf_op jit(solution)/shard_map/ppermute | solution.py:15
  9.2 32.6 %collective-permute-start.3 = (bf16[3,1,4096,64]{2,3,1,0:T(8,128)(2,1)S(1)}, bf16[3,1,4096,64]{2,3,1,0:T(8,128)(2,1)S(1)}, u32[]{:S(2)}, u32[]{:S(2)}) collective-permute-start(bf16[3,1,4096,64]{2,3,1,0:T(8,128)(2,1)S(1)} %constant_dynamic-update-slice_fusion), channel_id=1, source_target_pairs={{1,0},{2,1},{3,2},{4,3},{5,4},{6,5},{7,6},{9,8},{10,9},{11,10},{12... | collective-permute-start | bytes 4718600 | tf_op jit(solution)/shard_map/ppermute | solution.py:15
  10.5 71.4 %collective-permute-start.2 = (bf16[3,1,4096,64]{2,3,1,0:T(8,128)(2,1)S(1)}, bf16[3,1,4096,64]{2,3,1,0:T(8,128)(2,1)}, u32[]{:S(2)}, u32[]{:S(2)}) collective-permute-start(bf16[3,1,4096,64]{2,3,1,0:T(8,128)(2,1)S(1)} %constant_dynamic-update-slice_fusion), channel_id=1, source_target_pairs={{0,1},{1,2},{2,3},{3,4},{4,5},{5,6},{6,7},{8,9},{9,10},{10,11},{11... | collective-permute-start | bytes 4718600 | tf_op jit(solution)/shard_map/ppermute | solution.py:14
  154.5 4.6 %collective-permute-start.4 = (f32[64,64]{0,1:T(8,128)S(1)}, f32[64,64]{0,1:T(8,128)S(1)}, u32[]{:S(2)}, u32[]{:S(2)}) collective-permute-start(f32[64,64]{0,1:T(8,128)S(1)} %fusion.23), channel_id=1, source_target_pairs={{0,1},{1,0},{2,3},{3,2},{4,5},{5,4},{6,7},{7,6},{8,9},{9,8},{10,11... | collective-permute-start | bytes 49160 | tf_op jit(solution)/shard_map/ppermute | solution.py:23
  166.6 4.0 %collective-permute-start.5 = (f32[64,64]{0,1:T(8,128)S(1)}, f32[64,64]{0,1:T(8,128)S(1)}, u32[]{:S(2)}, u32[]{:S(2)}) collective-permute-start(f32[64,64]{0,1:T(8,128)S(1)} %fusion.25), channel_id=1, source_target_pairs={{0,2},{1,3},{2,0},{3,1},{4,6},{5,7},{6,4},{7,5},{8,10},{9,11},{10,... | collective-permute-start | bytes 49160 | tf_op jit(solution)/shard_map/ppermute | solution.py:23
  178.0 4.9 %collective-permute-start.6 = (f32[64,64]{0,1:T(8,128)S(1)}, f32[64,64]{0,1:T(8,128)S(1)}, u32[]{:S(2)}, u32[]{:S(2)}) collective-permute-start(f32[64,64]{0,1:T(8,128)S(1)} %fusion.27), channel_id=1, source_target_pairs={{0,4},{1,5},{2,6},{3,7},{4,0},{5,1},{6,2},{7,3},{8,12},{9,13},{10,... | collective-permute-start | bytes 49160 | tf_op jit(solution)/shard_map/ppermute | solution.py:23
  190.4 1.3 collective-permute-start.7
  199.1 4.0 %collective-permute-start.8 = (f32[64,64]{0,1:T(8,128)S(1)}, f32[64,64]{0,1:T(8,128)S(1)}, u32[]{:S(2)}, u32[]{:S(2)}) collective-permute-start(f32[64,64]{0,1:T(8,128)S(1)} %fusion.31), channel_id=1, source_target_pairs={{0,16},{8,24},{16,0},{24,8},{1,17},{9,25},{17,1},{25,9},{2,18},{10... | collective-permute-start | bytes 49160 | tf_op jit(solution)/shard_map/ppermute | solution.py:23
where the time goes:
time: 219 us; the launch traced here: 218 us
  waiting for transfers between devices  75.6 us (35%)
  local copies, waits for them, and re-layouts  51.3 us (23%)
  other arithmetic  50.6 us (23%)
  matrix products  22 us (10%)
  starting transfers between devices  17.8 us (8%)
    ppermute x2, waiting for transfers between devices, extended(): before = lax.ppermute(last, axis, up)  40.5 us
    another operation x18, other arithmetic, upper_cholesky(): return jnp.linalg.cholesky(matrix).T  39.1 us
    ppermute x2, waiting for transfers between devices, extended(): after = lax.ppermute(initial, axis, down)  27.8 us
    gather x1, local copies, waits for them, and re-layouts, shards(): picked = flat_rows[local_tile]  22.2 us
    reshape x2, local copies, waits for them, and re-layouts, shards(): flat_rows = neighbours.reshape(9 * tiles_dev, tile_rows, columns)  19.9 us
    dot_general x1, matrix products, shards(): jnp.einsum('rnij,rnjk->rik', near_tiles[0, 0], picked, preferred_element_...  13.9 us
    ppermute x2, starting transfers between devices, extended(): before = lax.ppermute(last, axis, up)  8.1 us
    ppermute x5, waiting for transfers between devices, swapped(): return lax.ppermute(value, axis, pairs)  7.35 us
  transfers between devices with their start and end apart: 9, of which 9 were waited for; matrix products, arithmetic and copies ran while one was open for 3% of the time, Pallas kernels for 0%

commit v1 on v0

v1 whole, which is shorter than its diff:
```python
import functools

import jax
import jax.numpy as jnp
from jax import lax
from jax.experimental import pallas as pl
from jax.experimental.pallas import tpu as pltpu
from jax.sharding import PartitionSpec as P

UNROLL = 32
ROW_BY_ROW = (((1,), (1,)), ((), ()))
VMEM_LIMIT = 24 * 2**20


def pair_swap(value, axis):
    size = lax.axis_size(axis)
    return lax.ppermute(value, axis, [(i, i ^ 1) for i in range(size)])


def between_pairs(value, axis):
    size = lax.axis_size(axis)
    pairs = []
    for i in range(1, size - 1, 2):
        pairs += [(i, i + 1), (i + 1, i)]
    return lax.ppermute(value, axis, pairs)


def pass_on(value, axis):
    size = lax.axis_size(axis)
    pairs = [(i, i + 2) for i in range(0, size - 2, 2)]
    pairs += [(i, i - 2) for i in range(3, size, 2)]
    return lax.ppermute(value, axis, pairs)


def slot_of(owner, own):
    return jnp.where(owner == own, 0, jnp.where(owner == (own ^ 1), 1, 2))


def work_lists(links, tiles_dev, gy_count):
    count = links.size
    flat = links.T.reshape(-1)
    order = jnp.arange(count, dtype=jnp.int32)
    entry = (order % tiles_dev) * links.shape[1] + order // tiles_dev
    owner = flat // tiles_dev
    across = slot_of(owner // gy_count, lax.axis_index("gx"))
    phase = slot_of(owner % gy_count, lax.axis_index("gy"))
    zero_tile = 3 * tiles_dev
    code = entry * 128 + across * tiles_dev + flat % tiles_dev
    counts = jnp.stack([jnp.sum((phase == p).astype(jnp.int32)) for p in range(3)])
    steps = (counts + UNROLL - 1) // UNROLL
    starts = jnp.stack([0 * steps[0], steps[0], steps[0] + steps[1]])
    key = phase * count + order
    before = jnp.sum((key[None, :] < key[:, None]).astype(jnp.int32), axis=1)
    skipped = jnp.where(phase == 0, 0, jnp.where(phase == 1, counts[0], counts[0] + counts[1]))
    begin = jnp.where(phase == 0, starts[0], jnp.where(phase == 1, starts[1], starts[2]))
    place = before - skipped + begin * UNROLL
    length = count + 3 * UNROLL
    hits = place[None, :] == jnp.arange(length, dtype=jnp.int32)[:, None]
    listed = zero_tile + jnp.sum(jnp.where(hits, code[None, :] - zero_tile, 0), axis=1)
    return listed.astype(jnp.int32), jnp.concatenate([starts, steps]).astype(jnp.int32)


def accumulate(phase, listed, ranges, near, sources, acc, rows):
    tiles_dev, _, columns = acc.shape
    width = near.shape[-1]
    blocks = near.shape[0] // tiles_dev
    for slot, source in enumerate(sources):
        for tile in range(tiles_dev):
            rows[slot * tiles_dev + tile] = source[:, tile * width:(tile + 1) * width]
    rows[3 * tiles_dev] = jnp.zeros(rows.shape[1:], rows.dtype)
    start = ranges[phase]

    def step(index, carry):
        products = []
        for lane in range(UNROLL):
            code = listed[(start + index) * UNROLL + lane]
            entry = lax.shift_right_logical(code, 7)
            tile = rows[code & 127]
            product = lax.dot_general(near[entry], tile, ROW_BY_ROW, preferred_element_type=jnp.float32)
            products.append((lax.div(entry, blocks), product))
        for target, product in products:
            acc[target] += product
        return carry

    lax.fori_loop(0, ranges[3 + phase], step, 0)


def first_kernel(listed, ranges, near, own, core, outer, acc, rows):
    acc[...] = jnp.zeros(acc.shape, acc.dtype)
    accumulate(0, listed, ranges, near, (own, core, outer), acc, rows)


def next_kernel(phase, listed, ranges, near, own, core, outer, acc_in, acc, rows):
    accumulate(phase, listed, ranges, near, (own, core, outer), acc, rows)


def last_kernel(listed, ranges, near, own, core, outer, acc_in, split, gram, rows, acc):
    tiles_dev, width, columns = acc.shape
    acc[...] = acc_in[...]
    accumulate(2, listed, ranges, near, (own, core, outer), acc, rows)
    for tile in range(tiles_dev):
        image = acc[tile].T
        high = image.astype(jnp.bfloat16)
        low = (image - high.astype(jnp.float32)).astype(jnp.bfloat16)
        split[:, tile * width:(tile + 1) * width] = jnp.concatenate([high, low], axis=0)
    both = split[...]
    full = lax.dot_general(both, both, ROW_BY_ROW, preferred_element_type=jnp.float32)
    top = full[:columns, :columns] + full[columns:, columns:]
    side = full[:columns, columns:] + full[columns:, :columns]
    gram[...] = top + side


def finish_kernel(scale, gram, split, basis, factor):
    columns = gram.shape[0]
    row = lax.broadcasted_iota(jnp.int32, (columns, columns), 0)
    column = lax.broadcasted_iota(jnp.int32, (columns, columns), 1)
    unit = jnp.where(row == column, 1.0, 0.0)
    work = jnp.concatenate([gram[...], unit], axis=1)
    wide_row = lax.broadcasted_iota(jnp.int32, work.shape, 0)
    for k in range(columns - 1):
        begin = k // 8 * 8
        live = work[begin:]
        pivot_row = work[k:k + 1]
        pivot = pivot_row[:, k:k + 1]
        ratio = live[:, k:k + 1] * (1.0 / pivot)
        ratio = jnp.where(wide_row[begin:] > k, ratio, 0.0)
        live = live - ratio * pivot_row
        work = live if begin == 0 else jnp.concatenate([work[:begin], live], axis=0)
    left, right = work[:, :columns], work[:, columns:]
    diagonal = jnp.sum(jnp.where(row == column, left, 0.0), axis=1, keepdims=True)
    root = lax.rsqrt(diagonal)
    upper = jnp.where(row <= column, left, 0.0) * root
    factor[...] = upper * (1.0 / scale)
    weight = right * (root * scale)
    high = weight.astype(jnp.bfloat16)
    low = (weight - high.astype(jnp.float32)).astype(jnp.bfloat16)
    high_rows = split[:columns]
    stacked = jnp.concatenate([high, high, low], axis=1)
    values = jnp.concatenate([split[...], high_rows], axis=0)
    basis[...] = jnp.dot(stacked, values, preferred_element_type=jnp.float32)


def in_vmem():
    return pl.BlockSpec(memory_space=pltpu.VMEM)


def in_smem():
    return pl.BlockSpec(memory_space=pltpu.SMEM)


def sum_over_all(value):
    gx_count, gy_count = lax.axis_size("gx"), lax.axis_size("gy")
    total = gx_count * gy_count
    bits = [gy_count * 2**i for i in range(1, gx_count.bit_length() - 1)]
    bits = bits[:1] + [2**i for i in range(gy_count.bit_length() - 1)] + bits[1:]

    def from_other(mask):
        return lax.ppermute(value, ("gx", "gy"), [(i, i ^ mask) for i in range(total)])

    value = value + from_other(gy_count)
    while bits:
        taken, bits = bits[:2], bits[2:]
        near = value + from_other(taken[0])
        if len(taken) == 2:
            near = near + (from_other(taken[1]) + from_other(taken[0] ^ taken[1]))
        value = near
    return value


def shards(near_tiles, block, adjacency):
    tiles_dev, blocks = adjacency.shape[2:]
    width = near_tiles.shape[4]
    rows, columns = block.shape[2:]
    gx_count, gy_count = lax.axis_size("gx"), lax.axis_size("gy")
    scale = float(rows * gx_count * gy_count) ** 0.5

    beside = pair_swap(block, "gy")
    outer = between_pairs(block, "gx")
    core = pair_swap(block, "gx")
    beyond = pass_on(beside, "gy")
    beside_outer = between_pairs(beside, "gx")
    beside_core = pair_swap(beside, "gx")
    beyond_outer = between_pairs(beyond, "gx")
    beyond_core = pair_swap(beyond, "gx")

    listed, ranges = work_lists(adjacency[0, 0], tiles_dev, gy_count)
    near = near_tiles.reshape(tiles_dev * blocks, width, width)
    near = pltpu.with_memory_space_constraint(near, pltpu.VMEM)
    params = pltpu.CompilerParams(vmem_limit_bytes=VMEM_LIMIT)
    acc_shape = jax.ShapeDtypeStruct((tiles_dev, width, columns), jnp.float32)
    tile_rows = pltpu.VMEM((3 * tiles_dev + 1, columns, width), jnp.bfloat16)
    lists = [in_smem(), in_smem()]
    flat = lambda value: value[0, 0].T

    acc = pl.pallas_call(
        first_kernel, out_shape=acc_shape, in_specs=lists + [in_vmem()] * 4, out_specs=in_vmem(),
        scratch_shapes=[tile_rows], compiler_params=params, name="own_rows",
    )(listed, ranges, near, flat(block), flat(core), flat(outer))
    acc = pl.pallas_call(
        functools.partial(next_kernel, 1), out_shape=acc_shape, in_specs=lists + [in_vmem()] * 5, out_specs=in_vmem(),
        scratch_shapes=[tile_rows], compiler_params=params, name="beside_rows", input_output_aliases={6: 0},
    )(listed, ranges, near, flat(beside), flat(beside_core), flat(beside_outer), acc)
    split, gram = pl.pallas_call(
        last_kernel,
        out_shape=(
            jax.ShapeDtypeStruct((2 * columns, rows), jnp.bfloat16),
            jax.ShapeDtypeStruct((columns, columns), jnp.float32),
        ),
        in_specs=lists + [in_vmem()] * 5, out_specs=(in_vmem(), in_vmem()),
        scratch_shapes=[tile_rows, pltpu.VMEM(acc_shape.shape, jnp.float32)], compiler_params=params, name="beyond_rows",
    )(listed, ranges, near, flat(beyond), flat(beyond_core), flat(beyond_outer), acc)

    gram = sum_over_all(gram)
    basis, factor = pl.pallas_call(
        functools.partial(finish_kernel, scale),
        out_shape=(
            jax.ShapeDtypeStruct((columns, rows), jnp.float32),
            jax.ShapeDtypeStruct((columns, columns), jnp.float32),
        ),
        in_specs=[in_vmem()] * 2, out_specs=(in_vmem(), in_vmem()), compiler_params=params, name="orthonormalize",
    )(gram, split)
    return basis.T.reshape(1, 1, rows, columns), factor


def solution(mesh):
    in_specs = (
        P("gx", "gy", None, None, None, None),
        P("gx", "gy", None, None),
        P("gx", "gy", None, None),
    )
    out_specs = (P("gx", "gy", None, None), P())
    return jax.shard_map(shards, mesh=mesh, in_specs=in_specs, out_specs=out_specs, check_vma=False)
```

time: 219 us -> 84.1 us (0.38)
  waiting for transfers between devices: 75.6 us -> 22.4 us
  other arithmetic: 50.6 us -> 6.06 us
  local copies, waits for them, and re-layouts: 51.3 us -> 9.36 us
  matrix products: 22 us -> 0 us
  Pallas kernels: 0 us -> 20.2 us
  starting transfers between devices: 17.8 us -> 22.3 us
  between operations: 0.95 us -> 3.36 us
    ppermute x9 -> x15, waiting for transfers between devices: 75.6 us -> 22.4 us  [the longest x7 10.2 us: from_other(): lax.ppermute(value, ('gx', 'gy'), [(i, i ^ mask) for i in range(total)])]
    another operation x19 -> x0, other arithmetic: 44 us -> none  [the longest x18 39.1 us: upper_cholesky(): return jnp.linalg.cholesky(matrix).T]
    gather x1 -> x0, local copies, waits for them, and re-layouts: 22.2 us -> none  [shards(): picked = flat_rows[local_tile]]
    pallas_call x0 -> x4, Pallas kernels: none -> 20.2 us  [the longest x1 7.37 us: shards(): pl.pallas_call(first_kernel, out_shape=acc_shape, in_specs=lists + [in_vm...]
    dot_general x12 -> x0, matrix products: 20 us -> none  [the longest x1 13.9 us: shards(): jnp.einsum('rnij,rnjk->rik', near_tiles[0, 0], picked, preferred_element_...]
    reshape x2 -> x1, local copies, waits for them, and re-layouts: 19.9 us -> 0.07 us  [work_lists(): flat = links.T.reshape(-1)]
    unnamed x3 -> x5, local copies, waits for them, and re-layouts: 1.81 us -> 8.7 us
    concatenate x2 -> x0, local copies, waits for them, and re-layouts: 6.76 us -> none  [extended(): shard = jnp.concatenate([before, shard, after], axis=dim)]
  transfers between devices with their start and end apart: 9 -> 15, of which waited for: 9 -> 8; matrix products, arithmetic and copies ran while one was open for 3% -> 9% of each run, Pallas kernels for 0% -> 14%
where the time goes in v1:
time: 84.1 us; the launch traced here: 83.7 us
  waiting for transfers between devices  22.4 us (27%)
  starting transfers between devices  22.3 us (27%)
  Pallas kernels  20.2 us (24%)
  local copies, waits for them, and re-layouts  9.36 us (11%)
  other arithmetic  6.06 us (7%)
  between operations  3.36 us (4%)
    ppermute x7, starting transfers between devices, from_other(): lax.ppermute(value, ('gx', 'gy'), [(i, i ^ mask) for i in range(total)])  10.3 us
    ppermute x7, waiting for transfers between devices, from_other(): lax.ppermute(value, ('gx', 'gy'), [(i, i ^ mask) for i in range(total)])  10.2 us
    ppermute x1, waiting for transfers between devices, pass_on(): return lax.ppermute(value, axis, pairs)  8.9 us
    unnamed x5, local copies, waits for them, and re-layouts  8.7 us
    pallas_call x1, Pallas kernels, shards(): pl.pallas_call(first_kernel, out_shape=acc_shape, in_specs=lists + [in_vm...  7.37 us
    pallas_call x1, Pallas kernels, shards(): pl.pallas_call(functools.partial(finish_kernel, scale), out_shape=(jax.Sh...  6.77 us
    ppermute x4, starting transfers between devices, pair_swap(): return lax.ppermute(value, axis, [(i, i ^ 1) for i in range(size)])  5.53 us
    ppermute x1, starting transfers between devices, pass_on(): return lax.ppermute(value, axis, pairs)  4.39 us
  transfers between devices with their start and end apart: 15, of which 8 were waited for; matrix products, arithmetic and copies ran while one was open for 9% of the time, Pallas kernels for 14%

profile of v1, /device:TPU:0, one launch (start us, length us, event | category | flops | bytes accessed | tf_op | source)
XLA Modules:
  0.0 83.7 jit_solution(13456893543341812477)
XLA Ops:
  1.1 0.7 collective-permute-start.7
  1.8 2.6 %collective-permute-start = (bf16[1,1,4096,64]{2,3,1,0:T(8,128)(2,1)}, bf16[1,1,4096,64]{2,3,1,0:T(8,128)(2,1)S(1)}, u32[]{:S(2)}, u32[]{:S(2)}) collective-permute-start(bf16[1,1,4096,64]{2,3,1,0:T(8,128)(2,1)} %param.4), channel_id=1, source_target_pairs={{0,1},{1,0},{2,3},{3,2},{4,5},{5,4},{6,7},{7,6},{8,9},{9,8},{10,11... | collective-permute-start | bytes 1572872 | tf_op jit(solution)/shard_map/ppermute | solution.py:17
  4.4 0.7 copy.11
  5.2 0.7 broadcast_compare_fusion
  5.9 0.7 convert_reduce_fusion.3
  7.9 2.0 %and_select_fusion = s32[3]{0:T(128)S(1)} fusion(s32[1]{0:T(128)} %bitcast.3, s32[1]{0:T(128)} %bitcast.2, s32[1]{0:T(128)} %bitcast.1), kind=kLoop, calls=%fused_computation.67 | loop fusion | flops 54 | bytes 24 | tf_op jit(solution)/shard_map/jit(floor_divide)/jit(_where)/select_n | solution.py:50
  9.9 0.6 fusion.25
  11.8 3.3 %collective-permute-done = bf16[1,1,4096,64]{2,3,1,0:T(8,128)(2,1)S(1)} collective-permute-done((bf16[1,1,4096,64]{2,3,1,0:T(8,128)(2,1)}, bf16[1,1,4096,64]{2,3,1,0:T(8,128)(2,1)S(1)}, u32[]{:S(2)}, u32[]{:S(2)}) %collective-permute-start) | collective-permute-done | bytes 524320 | tf_op jit(solution)/shard_map/ppermute | solution.py:17
  15.1 4.4 %collective-permute-start.1 = (bf16[1,1,4096,64]{2,3,1,0:T(8,128)(2,1)S(1)}, bf16[1,1,4096,64]{2,3,1,0:T(8,128)(2,1)S(1)}, u32[]{:S(2)}, u32[]{:S(2)}) collective-permute-start(bf16[1,1,4096,64]{2,3,1,0:T(8,128)(2,1)S(1)} %collective-permute-done), channel_id=1, source_target_pairs={{0,2},{2,4},{4,6},{3,1},{5,3},{7,5},{8,10},{10,12},{12,14},{11,9},... | collective-permute-start | bytes 1572872 | tf_op jit(solution)/shard_map/ppermute | solution.py:32
  19.9 1.6 %collective-permute-start.4 = (bf16[1,1,4096,64]{2,3,1,0:T(8,128)(2,1)S(1)}, bf16[1,1,4096,64]{2,3,1,0:T(8,128)(2,1)S(1)}, u32[]{:S(2)}, u32[]{:S(2)}) collective-permute-start(bf16[1,1,4096,64]{2,3,1,0:T(8,128)(2,1)S(1)} %collective-permute-done), channel_id=1, source_target_pairs={{0,8},{8,0},{16,24},{24,16},{1,9},{9,1},{17,25},{25,17},{2,10},{10... | collective-permute-start | bytes 1572872 | tf_op jit(solution)/shard_map/ppermute | solution.py:17
  21.4 0.7 collective-permute-start.5
  22.1 8.9 %collective-permute-done.1 = bf16[1,1,4096,64]{2,3,1,0:T(8,128)(2,1)S(1)} collective-permute-done((bf16[1,1,4096,64]{2,3,1,0:T(8,128)(2,1)S(1)}, bf16[1,1,4096,64]{2,3,1,0:T(8,128)(2,1)S(1)}, u32[]{:S(2)}, u32[]{:S(2)}) %collective-permute-start.1) | collective-permute-done | bytes 524320 | tf_op jit(solution)/shard_map/ppermute | solution.py:32
  31.0 0.9 %collective-permute-start.2 = (bf16[1,1,4096,64]{2,3,1,0:T(8,128)(2,1)S(1)}, bf16[1,1,4096,64]{2,3,1,0:T(8,128)(2,1)S(1)}, u32[]{:S(2)}, u32[]{:S(2)}) collective-permute-start(bf16[1,1,4096,64]{2,3,1,0:T(8,128)(2,1)S(1)} %collective-permute-done.1), channel_id=1, source_target_pairs={{0,8},{8,0},{16,24},{24,16},{1,9},{9,1},{17,25},{25,17},{2,10},{10... | collective-permute-start | bytes 1572872 | tf_op jit(solution)/shard_map/ppermute | solution.py:17
  31.9 0.7 collective-permute-start.3
  32.6 1.3 %multiply_add_fusion = s32[640]{0:T(1024)S(1)} fusion(s32[640]{0:T(1024)S(1)} %convert_reduce_fusion, pred[640]{0:T(1024)(128)(4,1)S(1)} %get-tuple-element.17, pred[640]{0:T(1024)(128)(4,1)S(1)} %get-tuple-element.16, s32[]{:T(128)} %add.153, s32[]{:T(128)} %bitcast.4, s32[]{:T(128)S(6)} %add.152, s32[]{:T(128)} %get-tuple-element.10), kind=kLoop, calls=%fused_computation.54 | loop fusion | flops 7040 | bytes 6416 | tf_op jit(solution)/shard_map/add | solution.py:56
  33.9 0.7 pad_add_fusion.ranges
  34.9 7.0 %copy-done = bf16[1,1,32,20,128,128]{5,4,3,2,1,0:T(8,128)(2,1)S(1)} copy-done((bf16[1,1,32,20,128,128]{5,4,3,2,1,0:T(8,128)(2,1)S(1)}, bf16[1,1,32,20,128,128]{5,4,3,2,1,0:T(8,128)(2,1)}, u32[]{:S(2)}) %copy-start) | copy-done | bytes 20971544
  41.8 1.0 %copy-done.1 = bf16[1,1,4096,64]{2,3,1,0:T(8,128)(2,1)S(1)} copy-done((bf16[1,1,4096,64]{2,3,1,0:T(8,128)(2,1)S(1)}, bf16[1,1,4096,64]{2,3,1,0:T(8,128)(2,1)}, u32[]{:S(2)}) %copy-start.1) | copy-done | bytes 524312
  42.9 7.4 %own_rows.1.acc_in = f32[32,128,64]{2,1,0:T(8,128)S(1)} custom-call(s32[736]{0:T(1024)S(1)} %broadcast_add_fusion.listed, s32[6]{0:T(128)S(1)} %pad_add_fusion.ranges, bf16[640,128,128]{2,1,0:T(8,128)(2,1)S(1)} %bitcast.45, bf16[64,4096]{1,0:T(8,128)(2,1)S(1)} %bitcast.48, bf16[64,4096]{1,0:T(8,128)(2,1)S(1)} %bitcast.50, bf16[64,4096]{1,0:T(8,128)(2,1)S(1)} %bitcast.51), custom_call_target="tpu_custom_call" | custom-call | tf_op jit(solution)/shard_map/own_rows/pallas_call | solution.py:195
  50.3 4.1 %beside_rows.1.acc_in = f32[32,128,64]{2,1,0:T(8,128)S(1)} custom-call(s32[736]{0:T(1024)S(1)} %broadcast_add_fusion.listed, s32[6]{0:T(128)S(1)} %pad_add_fusion.ranges, bf16[640,128,128]{2,1,0:T(8,128)(2,1)S(1)} %bitcast.46, bf16[64,4096]{1,0:T(8,128)(2,1)S(1)} %bitcast.49, bf16[64,4096]{1,0:T(8,128)(2,1)S(1)} %bitcast.54, ...), custom_call_target="tpu_custom_call", output_to_operand_aliasing={{}: (6, {})} | custom-call | tf_op jit(solution)/shard_map/beside_rows/pallas_call | solution.py:199
  54.3 2.0 %beyond_rows.1 = (bf16[128,4096]{1,0:T(8,128)(2,1)S(1)}, f32[64,64]{1,0:T(8,128)S(1)}) custom-call(s32[736]{0:T(1024)S(1)} %broadcast_add_fusion.listed, s32[6]{0:T(128)S(1)} %pad_add_fusion.ranges, bf16[640,128,128]{2,1,0:T(8,128)(2,1)S(1)} %bitcast.47, bf16[64,4096]{1,0:T(8,128)(2,1)S(1)} %bitcast.52, bf16[64,4096]{1,0:T(8,128)(2,1)S(1)} %bitcast.53, ...), custom_call_target="tpu_custom_call" | custom-call | tf_op jit(solution)/shard_map/beyond_rows/pallas_call | solution.py:203
  56.4 1.3 %collective-permute-start.8 = (f32[64,64]{1,0:T(8,128)S(1)}, f32[64,64]{1,0:T(8,128)S(1)}, u32[]{:S(2)}, u32[]{:S(2)}) collective-permute-start(f32[64,64]{1,0:T(8,128)S(1)} %get-tuple-element.6), channel_id=1, source_target_pairs={{0,8},{1,9},{2,10},{3,11},{4,12},{5,13},{6,14},{7,15},{8,0},{9,1},... | collective-permute-start | bytes 49160 | tf_op jit(solution)/shard_map/ppermute | solution.py:158
  57.7 0.9 %collective-permute-done.8 = f32[64,64]{1,0:T(8,128)S(1)} collective-permute-done((f32[64,64]{1,0:T(8,128)S(1)}, f32[64,64]{1,0:T(8,128)S(1)}, u32[]{:S(2)}, u32[]{:S(2)}) %collective-permute-start.8) | collective-permute-done | bytes 16416 | tf_op jit(solution)/shard_map/ppermute | solution.py:158
  58.5 2.6 %collective-permute-start.10 = (f32[64,64]{1,0:T(8,128)S(1)}, f32[64,64]{1,0:T(8,128)S(1)}, u32[]{:S(2)}, u32[]{:S(2)}) collective-permute-start(f32[64,64]{1,0:T(8,128)S(1)} %add.162), channel_id=1, source_target_pairs={{0,1},{1,0},{2,3},{3,2},{4,5},{5,4},{6,7},{7,6},{8,9},{9,8},{10,11... | collective-permute-start | bytes 49160 | tf_op jit(solution)/shard_map/ppermute | solution.py:158
  61.1 1.0 %collective-permute-start.11 = (f32[64,64]{1,0:T(8,128)S(1)}, f32[64,64]{1,0:T(8,128)S(1)}, u32[]{:S(2)}, u32[]{:S(2)}) collective-permute-start(f32[64,64]{1,0:T(8,128)S(1)} %add.162), channel_id=1, source_target_pairs={{0,17},{1,16},{2,19},{3,18},{4,21},{5,20},{6,23},{7,22},{8,25},{9,... | collective-permute-start | bytes 49160 | tf_op jit(solution)/shard_map/ppermute | solution.py:158
  62.1 0.6 collective-permute-start.9
  63.0 2.9 %collective-permute-done.11 = f32[64,64]{1,0:T(8,128)S(1)} collective-permute-done((f32[64,64]{1,0:T(8,128)S(1)}, f32[64,64]{1,0:T(8,128)S(1)}, u32[]{:S(2)}, u32[]{:S(2)}) %collective-permute-start.11) | collective-permute-done | bytes 16416 | tf_op jit(solution)/shard_map/ppermute | solution.py:158
  66.3 2.3 %collective-permute-start.12 = (f32[64,64]{1,0:T(8,128)S(1)}, f32[64,64]{1,0:T(8,128)S(1)}, u32[]{:S(2)}, u32[]{:S(2)}) collective-permute-start(f32[64,64]{1,0:T(8,128)S(1)} %add_add_fusion.1), channel_id=1, source_target_pairs={{0,2},{1,3},{2,0},{3,1},{4,6},{5,7},{6,4},{7,5},{8,10},{9,11},{10,... | collective-permute-start | bytes 49160 | tf_op jit(solution)/shard_map/ppermute | solution.py:158
  68.6 2.6 %collective-permute-start.13 = (f32[64,64]{1,0:T(8,128)S(1)}, f32[64,64]{1,0:T(8,128)S(1)}, u32[]{:S(2)}, u32[]{:S(2)}) collective-permute-start(f32[64,64]{1,0:T(8,128)S(1)} %add_add_fusion.1), channel_id=1, source_target_pairs={{0,4},{1,5},{2,6},{3,7},{4,0},{5,1},{6,2},{7,3},{8,12},{9,13},{10,... | collective-permute-start | bytes 49160 | tf_op jit(solution)/shard_map/ppermute | solution.py:158
  71.2 2.2 %collective-permute-done.13 = f32[64,64]{1,0:T(8,128)S(1)} collective-permute-done((f32[64,64]{1,0:T(8,128)S(1)}, f32[64,64]{1,0:T(8,128)S(1)}, u32[]{:S(2)}, u32[]{:S(2)}) %collective-permute-start.13) | collective-permute-done | bytes 16416 | tf_op jit(solution)/shard_map/ppermute | solution.py:158
  73.4 3.5 %collective-permute-done.14 = f32[64,64]{1,0:T(8,128)S(1)} collective-permute-done((f32[64,64]{1,0:T(8,128)S(1)}, f32[64,64]{1,0:T(8,128)S(1)}, u32[]{:S(2)}, u32[]{:S(2)}) %collective-permute-start.14) | collective-permute-done | bytes 16416 | tf_op jit(solution)/shard_map/ppermute | solution.py:158
  76.9 6.8 %orthonormalize.1 = (f32[64,4096]{1,0:T(8,128)}, f32[64,64]{1,0:T(8,128)}) custom-call(f32[64,64]{1,0:T(8,128)S(1)} %add_add_fusion.gram, bf16[128,4096]{1,0:T(8,128)(2,1)S(1)} %get-tuple-element.7.split), custom_call_target="tpu_custom_call" | custom-call | tf_op jit(solution)/shard_map/orthonormalize/pallas_call | solution.py:214
  (22 shorter events, 1.9 us)
Async XLA Ops:
  0.6 31.3 %collective-permute-start.6 = (bf16[1,1,4096,64]{2,3,1,0:T(8,128)(2,1)}, bf16[1,1,4096,64]{2,3,1,0:T(8,128)(2,1)S(1)}, u32[]{:S(2)}, u32[]{:S(2)}) collective-permute-start(bf16[1,1,4096,64]{2,3,1,0:T(8,128)(2,1)} %param.4), channel_id=1, source_target_pairs={{0,8},{8,0},{16,24},{24,16},{1,9},{9,1},{17,25},{25,17},{2,10},{10... | collective-permute-start | bytes 1572872 | tf_op jit(solution)/shard_map/ppermute | solution.py:17
  1.1 33.7 %collective-permute-start.7 = (bf16[1,1,4096,64]{2,3,1,0:T(8,128)(2,1)}, bf16[1,1,4096,64]{2,3,1,0:T(8,128)(2,1)S(1)}, u32[]{:S(2)}, u32[]{:S(2)}) collective-permute-start(bf16[1,1,4096,64]{2,3,1,0:T(8,128)(2,1)} %param.4), channel_id=1, source_target_pairs={{8,16},{16,8},{9,17},{17,9},{10,18},{18,10},{11,19},{19,11},{12,20... | collective-permute-start | bytes 1572872 | tf_op jit(solution)/shard_map/ppermute | solution.py:25
  1.8 13.3 %collective-permute-start = (bf16[1,1,4096,64]{2,3,1,0:T(8,128)(2,1)}, bf16[1,1,4096,64]{2,3,1,0:T(8,128)(2,1)S(1)}, u32[]{:S(2)}, u32[]{:S(2)}) collective-permute-start(bf16[1,1,4096,64]{2,3,1,0:T(8,128)(2,1)} %param.4), channel_id=1, source_target_pairs={{0,1},{1,0},{2,3},{3,2},{4,5},{5,4},{6,7},{7,6},{8,9},{9,8},{10,11... | collective-permute-start | bytes 1572872 | tf_op jit(solution)/shard_map/ppermute | solution.py:17
  15.1 15.9 %collective-permute-start.1 = (bf16[1,1,4096,64]{2,3,1,0:T(8,128)(2,1)S(1)}, bf16[1,1,4096,64]{2,3,1,0:T(8,128)(2,1)S(1)}, u32[]{:S(2)}, u32[]{:S(2)}) collective-permute-start(bf16[1,1,4096,64]{2,3,1,0:T(8,128)(2,1)S(1)} %collective-permute-done), channel_id=1, source_target_pairs={{0,2},{2,4},{4,6},{3,1},{5,3},{7,5},{8,10},{10,12},{12,14},{11,9},... | collective-permute-start | bytes 1572872 | tf_op jit(solution)/shard_map/ppermute | solution.py:32
  19.9 30.4 %collective-permute-start.4 = (bf16[1,1,4096,64]{2,3,1,0:T(8,128)(2,1)S(1)}, bf16[1,1,4096,64]{2,3,1,0:T(8,128)(2,1)S(1)}, u32[]{:S(2)}, u32[]{:S(2)}) collective-permute-start(bf16[1,1,4096,64]{2,3,1,0:T(8,128)(2,1)S(1)} %collective-permute-done), channel_id=1, source_target_pairs={{0,8},{8,0},{16,24},{24,16},{1,9},{9,1},{17,25},{25,17},{2,10},{10... | collective-permute-start | bytes 1572872 | tf_op jit(solution)/shard_map/ppermute | solution.py:17
  21.4 28.8 %collective-permute-start.5 = (bf16[1,1,4096,64]{2,3,1,0:T(8,128)(2,1)S(1)}, bf16[1,1,4096,64]{2,3,1,0:T(8,128)(2,1)S(1)}, u32[]{:S(2)}, u32[]{:S(2)}) collective-permute-start(bf16[1,1,4096,64]{2,3,1,0:T(8,128)(2,1)S(1)} %collective-permute-done), channel_id=1, source_target_pairs={{8,16},{16,8},{9,17},{17,9},{10,18},{18,10},{11,19},{19,11},{12,20... | collective-permute-start | bytes 1572872 | tf_op jit(solution)/shard_map/ppermute | solution.py:25
  31.0 23.3 %collective-permute-start.2 = (bf16[1,1,4096,64]{2,3,1,0:T(8,128)(2,1)S(1)}, bf16[1,1,4096,64]{2,3,1,0:T(8,128)(2,1)S(1)}, u32[]{:S(2)}, u32[]{:S(2)}) collective-permute-start(bf16[1,1,4096,64]{2,3,1,0:T(8,128)(2,1)S(1)} %collective-permute-done.1), channel_id=1, source_target_pairs={{0,8},{8,0},{16,24},{24,16},{1,9},{9,1},{17,25},{25,17},{2,10},{10... | collective-permute-start | bytes 1572872 | tf_op jit(solution)/shard_map/ppermute | solution.py:17
  31.9 22.5 %collective-permute-start.3 = (bf16[1,1,4096,64]{2,3,1,0:T(8,128)(2,1)S(1)}, bf16[1,1,4096,64]{2,3,1,0:T(8,128)(2,1)S(1)}, u32[]{:S(2)}, u32[]{:S(2)}) collective-permute-start(bf16[1,1,4096,64]{2,3,1,0:T(8,128)(2,1)S(1)} %collective-permute-done.1), channel_id=1, source_target_pairs={{8,16},{16,8},{9,17},{17,9},{10,18},{18,10},{11,19},{19,11},{12,20... | collective-permute-start | bytes 1572872 | tf_op jit(solution)/shard_map/ppermute | solution.py:25
  34.9 7.0 %copy-start = (bf16[1,1,32,20,128,128]{5,4,3,2,1,0:T(8,128)(2,1)S(1)}, bf16[1,1,32,20,128,128]{5,4,3,2,1,0:T(8,128)(2,1)}, u32[]{:S(2)}) copy-start(bf16[1,1,32,20,128,128]{5,4,3,2,1,0:T(8,128)(2,1)} %param.3) | copy-start | bytes 62914564
  41.8 1.0 %copy-start.1 = (bf16[1,1,4096,64]{2,3,1,0:T(8,128)(2,1)S(1)}, bf16[1,1,4096,64]{2,3,1,0:T(8,128)(2,1)}, u32[]{:S(2)}) copy-start(bf16[1,1,4096,64]{2,3,1,0:T(8,128)(2,1)} %param.4) | copy-start | bytes 1572868
  56.4 2.2 %collective-permute-start.8 = (f32[64,64]{1,0:T(8,128)S(1)}, f32[64,64]{1,0:T(8,128)S(1)}, u32[]{:S(2)}, u32[]{:S(2)}) collective-permute-start(f32[64,64]{1,0:T(8,128)S(1)} %get-tuple-element.6), channel_id=1, source_target_pairs={{0,8},{1,9},{2,10},{3,11},{4,12},{5,13},{6,14},{7,15},{8,0},{9,1},... | collective-permute-start | bytes 49160 | tf_op jit(solution)/shard_map/ppermute | solution.py:158
  58.5 4.5 %collective-permute-start.10 = (f32[64,64]{1,0:T(8,128)S(1)}, f32[64,64]{1,0:T(8,128)S(1)}, u32[]{:S(2)}, u32[]{:S(2)}) collective-permute-start(f32[64,64]{1,0:T(8,128)S(1)} %add.162), channel_id=1, source_target_pairs={{0,1},{1,0},{2,3},{3,2},{4,5},{5,4},{6,7},{7,6},{8,9},{9,8},{10,11... | collective-permute-start | bytes 49160 | tf_op jit(solution)/shard_map/ppermute | solution.py:158
  61.1 4.8 %collective-permute-start.11 = (f32[64,64]{1,0:T(8,128)S(1)}, f32[64,64]{1,0:T(8,128)S(1)}, u32[]{:S(2)}, u32[]{:S(2)}) collective-permute-start(f32[64,64]{1,0:T(8,128)S(1)} %add.162), channel_id=1, source_target_pairs={{0,17},{1,16},{2,19},{3,18},{4,21},{5,20},{6,23},{7,22},{8,25},{9,... | collective-permute-start | bytes 49160 | tf_op jit(solution)/shard_map/ppermute | solution.py:158
  62.1 4.2 %collective-permute-start.9 = (f32[64,64]{1,0:T(8,128)S(1)}, f32[64,64]{1,0:T(8,128)S(1)}, u32[]{:S(2)}, u32[]{:S(2)}) collective-permute-start(f32[64,64]{1,0:T(8,128)S(1)} %add.162), channel_id=1, source_target_pairs={{0,16},{1,17},{2,18},{3,19},{4,20},{5,21},{6,22},{7,23},{8,24},{9,... | collective-permute-start | bytes 49160 | tf_op jit(solution)/shard_map/ppermute | solution.py:158
  66.3 4.9 %collective-permute-start.12 = (f32[64,64]{1,0:T(8,128)S(1)}, f32[64,64]{1,0:T(8,128)S(1)}, u32[]{:S(2)}, u32[]{:S(2)}) collective-permute-start(f32[64,64]{1,0:T(8,128)S(1)} %add_add_fusion.1), channel_id=1, source_target_pairs={{0,2},{1,3},{2,0},{3,1},{4,6},{5,7},{6,4},{7,5},{8,10},{9,11},{10,... | collective-permute-start | bytes 49160 | tf_op jit(solution)/shard_map/ppermute | solution.py:158
  68.6 4.8 %collective-permute-start.13 = (f32[64,64]{1,0:T(8,128)S(1)}, f32[64,64]{1,0:T(8,128)S(1)}, u32[]{:S(2)}, u32[]{:S(2)}) collective-permute-start(f32[64,64]{1,0:T(8,128)S(1)} %add_add_fusion.1), channel_id=1, source_target_pairs={{0,4},{1,5},{2,6},{3,7},{4,0},{5,1},{6,2},{7,3},{8,12},{9,13},{10,... | collective-permute-start | bytes 49160 | tf_op jit(solution)/shard_map/ppermute | solution.py:158
  71.2 5.7 %collective-permute-start.14 = (f32[64,64]{1,0:T(8,128)S(1)}, f32[64,64]{1,0:T(8,128)S(1)}, u32[]{:S(2)}, u32[]{:S(2)}) collective-permute-start(f32[64,64]{1,0:T(8,128)S(1)} %add_add_fusion.1), channel_id=1, source_target_pairs={{0,6},{1,7},{2,4},{3,5},{4,2},{5,3},{6,0},{7,1},{8,14},{9,15},{10,... | collective-permute-start | bytes 49160 | tf_op jit(solution)/shard_map/ppermute | solution.py:158

commit v2 on v1

v2 whole, which is shorter than its diff:
```python
import functools

import jax
import jax.numpy as jnp
from jax import lax
from jax.experimental import pallas as pl
from jax.experimental.pallas import tpu as pltpu
from jax.sharding import PartitionSpec as P

UNROLL = 32
PARTS = 4
LIST_ROWS = 6
PART_OF = (0, 1, 1, 1, 1, 2, 2, 3, 2)
SLOT_OF = (0, 0, 1, 2, 3, 0, 1, 0, 2)
ROW_BY_ROW = (((1,), (1,)), ((), ()))
VMEM_LIMIT = 8 * 2**20


def pair_swap(value, axis):
    size = lax.axis_size(axis)
    return lax.ppermute(value, axis, [(i, i ^ 1) for i in range(size)])


def between_pairs(value, axis):
    return lax.ppermute(value, axis, outside(lax.axis_size(axis)))


def outside(size):
    return [(i, i + 1) for i in range(1, size - 1, 2)] + [(i + 1, i) for i in range(1, size - 1, 2)]


def across_both(value):
    gx_count, gy_count = lax.axis_size("gx"), lax.axis_size("gy")
    pairs = [
        (from_x * gy_count + (from_y ^ 1), to_x * gy_count + to_y)
        for from_x, to_x in outside(gx_count)
        for from_y, to_y in outside(gy_count)
    ]
    return lax.ppermute(value, ("gx", "gy"), pairs)


def two_back(value, axis):
    size = lax.axis_size(axis)
    pairs = [(i, i - 2) for i in range(2, size, 2)]
    pairs += [(i, i + 2) for i in range(1, size - 2, 2)]
    return lax.ppermute(value, axis, pairs)


def exact_log2(value):
    assert value & (value - 1) == 0
    return value.bit_length() - 1


def look_up(table, index):
    packed = sum(value << (2 * place) for place, value in enumerate(table))
    return lax.shift_right_logical(jnp.full(index.shape, packed, jnp.int32), 2 * index) & 3


def build_lists(links, work, tiles_dev, blocks, gy_count):
    own_x, own_y = lax.axis_index("gx"), lax.axis_index("gy")
    count = links.shape[1]
    tile_bits, gy_bits = exact_log2(tiles_dev), exact_log2(gy_count)
    link = links[...]
    place = lax.broadcasted_iota(jnp.int32, link.shape, 1)
    owner = lax.shift_right_logical(link, tile_bits)
    owner_x, owner_y = lax.shift_right_logical(owner, gy_bits), owner & (gy_count - 1)
    across = jnp.where(owner_x == own_x, 0, jnp.where(owner_x == (own_x ^ 1), 1, 2))
    own_row, beside = owner_y == own_y, owner_y == (own_y ^ 1)
    kind = across + jnp.where(own_row, 0, jnp.where(beside, 3, 6))
    part, slot = look_up(PART_OF, kind), look_up(SLOT_OF, kind)
    entry = (place & (tiles_dev - 1)) * blocks + lax.shift_right_logical(place, tile_bits)
    code = entry * 512 + slot * tiles_dev + (link & (tiles_dev - 1)) + 1

    def ones_where(hit):
        return jnp.where(hit, 1.0, 0.0).astype(jnp.bfloat16)

    def iota(rows, dim):
        return lax.broadcasted_iota(jnp.int32, (rows, count), dim)

    is_part = iota(128, 0) == part
    earlier = ones_where(lax.broadcasted_iota(jnp.int32, (count, count), 0) < lax.broadcasted_iota(jnp.int32, (count, count), 1))
    before = jnp.dot(ones_where(is_part[:16]), earlier, preferred_element_type=jnp.float32)
    rank = jnp.sum(jnp.where(is_part[:16], before, 0.0), axis=0, keepdims=True).astype(jnp.int32)
    row = part * LIST_ROWS + lax.shift_right_logical(rank, 7)
    column_hits = ones_where(iota(128, 0) == (rank & 127))
    row_hits = iota(PARTS * LIST_ROWS + 2, 0) == row
    listed = jnp.zeros((PARTS * LIST_ROWS + 2, 128), jnp.float32)
    for shift in (16, 8, 0):
        digit = (lax.shift_right_logical(code, shift) & 255).astype(jnp.float32)
        values = jnp.where(row_hits, digit, 0.0).astype(jnp.bfloat16)
        listed = listed * 256.0 + lax.dot_general(values, column_hits, ROW_BY_ROW, preferred_element_type=jnp.float32)
    ones = jnp.ones((PARTS * LIST_ROWS + 2, count), jnp.bfloat16)
    lengths = lax.dot_general(ones, ones_where(is_part), ROW_BY_ROW, preferred_element_type=jnp.float32)
    line = lax.broadcasted_iota(jnp.int32, listed.shape, 0)
    work[...] = jnp.where(line == PARTS * LIST_ROWS + 1, lengths, listed).astype(jnp.int32)


def lay_out(sources, rows, tiles_dev):
    width = rows.shape[-1]
    rows[0] = jnp.zeros(rows.shape[1:], rows.dtype)
    for slot, source in enumerate(sources):
        for tile in range(tiles_dev):
            rows[1 + slot * tiles_dev + tile] = source[:, tile * width:(tile + 1) * width]


def accumulate(part, work, near, acc, rows):
    tiles_dev = acc.shape[0]
    blocks = near.shape[0] // tiles_dev
    groups = 128 // UNROLL

    def step(index, carry):
        line = part * LIST_ROWS + lax.div(index, groups)
        begin = lax.rem(index, groups) * UNROLL
        products = []
        for lane in range(UNROLL):
            code = work[line, begin + lane]
            entry = lax.shift_right_logical(code, 9)
            product = lax.dot_general(
                near[entry], rows[code & 511], ROW_BY_ROW, preferred_element_type=jnp.float32
            )
            products.append((lax.div(entry, blocks), product))
        for target, product in products:
            acc[target] += product
        return carry

    length = work[PARTS * LIST_ROWS + 1, part]
    lax.fori_loop(0, lax.div(length + (UNROLL - 1), UNROLL), step, 0)


def own_kernel(gy_count, links, near_hbm, own, acc, work, rows, near, work_smem, sems, work_sem):
    tiles_dev = acc.shape[0]
    chunks = sems.shape[0]
    length = near.shape[0] // chunks
    copies = [
        pltpu.make_async_copy(
            near_hbm.at[pl.ds(c * length, length)], near.at[pl.ds(c * length, length)], sems.at[c]
        )
        for c in range(chunks)
    ]
    for copy in copies:
        copy.start()
    build_lists(links, work, tiles_dev, near.shape[0] // tiles_dev, gy_count)
    work_copy = pltpu.make_async_copy(work, work_smem, work_sem)
    work_copy.start()
    lay_out((own,), rows, tiles_dev)
    acc[...] = jnp.zeros(acc.shape, acc.dtype)
    work_copy.wait()
    for copy in copies:
        copy.wait()
    accumulate(0, work_smem, near, acc, rows)


def middle_kernel(part, work, near, *refs):
    acc, rows = refs[-2:]
    lay_out(refs[:-3], rows, acc.shape[0])
    accumulate(part, work, near, acc, rows)


def last_kernel(work, near, source, acc_in, split, gram, rows, acc):
    tiles_dev, width, columns = acc.shape
    lay_out((source,), rows, tiles_dev)
    acc[...] = acc_in[...]
    accumulate(3, work, near, acc, rows)
    for tile in range(tiles_dev):
        image = acc[tile].T
        high = image.astype(jnp.bfloat16)
        low = (image - high.astype(jnp.float32)).astype(jnp.bfloat16)
        split[:, tile * width:(tile + 1) * width] = jnp.concatenate([high, low], axis=0)
    both = split[...]
    full = lax.dot_general(both, both, ROW_BY_ROW, preferred_element_type=jnp.float32)
    top = full[:columns, :columns] + full[columns:, columns:]
    side = full[:columns, columns:] + full[columns:, :columns]
    gram[...] = top + side


def finish_kernel(scale, gram, split, basis, factor):
    columns = gram.shape[0]
    row = lax.broadcasted_iota(jnp.int32, (columns, columns), 0)
    column = lax.broadcasted_iota(jnp.int32, (columns, columns), 1)
    unit = jnp.where(row == column, 1.0, 0.0)
    work = jnp.concatenate([gram[...], unit], axis=1)
    wide_row = lax.broadcasted_iota(jnp.int32, work.shape, 0)
    for k in range(columns - 1):
        begin = k // 8 * 8
        live = work[begin:]
        pivot_row = work[k:k + 1]
        pivot = pivot_row[:, k:k + 1]
        ratio = live[:, k:k + 1] * (1.0 / pivot)
        ratio = jnp.where(wide_row[begin:] > k, ratio, 0.0)
        live = live - ratio * pivot_row
        work = live if begin == 0 else jnp.concatenate([work[:begin], live], axis=0)
    left, right = work[:, :columns], work[:, columns:]
    diagonal = jnp.sum(jnp.where(row == column, left, 0.0), axis=1, keepdims=True)
    root = lax.rsqrt(diagonal)
    upper = jnp.where(row <= column, left, 0.0) * root
    factor[...] = upper * (1.0 / scale)
    weight = right * (root * scale)
    high = weight.astype(jnp.bfloat16)
    low = (weight - high.astype(jnp.float32)).astype(jnp.bfloat16)
    high_rows = split[:columns]
    stacked = jnp.concatenate([high, high, low], axis=1)
    values = jnp.concatenate([split[...], high_rows], axis=0)
    basis[...] = jnp.dot(stacked, values, preferred_element_type=jnp.float32)


def in_vmem():
    return pl.BlockSpec(memory_space=pltpu.VMEM)


def in_smem():
    return pl.BlockSpec(memory_space=pltpu.SMEM)


def sum_over_all(value):
    gx_count, gy_count = lax.axis_size("gx"), lax.axis_size("gy")
    total = gx_count * gy_count
    bits = [gy_count * 2**i for i in range(1, gx_count.bit_length() - 1)]
    bits = bits[:1] + [2**i for i in range(gy_count.bit_length() - 1)] + bits[1:]

    def from_other(mask):
        return lax.ppermute(value, ("gx", "gy"), [(i, i ^ mask) for i in range(total)])

    value = value + from_other(gy_count)
    while bits:
        taken, bits = bits[:2], bits[2:]
        near = value + from_other(taken[0])
        if len(taken) == 2:
            near = near + (from_other(taken[1]) + from_other(taken[0] ^ taken[1]))
        value = near
    return value


def shards(near_tiles, block, adjacency):
    tiles_dev, blocks = adjacency.shape[2:]
    width = near_tiles.shape[4]
    rows, columns = block.shape[2:]
    gx_count, gy_count = lax.axis_size("gx"), lax.axis_size("gy")
    scale = float(rows * gx_count * gy_count) ** 0.5

    beside = pair_swap(block, "gy")
    two_off = two_back(block, "gy")
    outer = between_pairs(block, "gx")
    core = pair_swap(block, "gx")

    count = tiles_dev * blocks
    links = adjacency[0, 0].T.reshape(1, -1)
    near = near_tiles.reshape(count, width, width)
    acc_shape = jax.ShapeDtypeStruct((tiles_dev, width, columns), jnp.float32)
    flat = lambda value: value[0, 0].T

    def tile_rows(sources):
        return pltpu.VMEM((sources * tiles_dev + 1, columns, width), jnp.bfloat16)

    def params(limit=VMEM_LIMIT):
        return dict(
            compiler_params=pltpu.CompilerParams(vmem_limit_bytes=limit),
        )

    acc, work = pl.pallas_call(
        functools.partial(own_kernel, gy_count),
        out_shape=(acc_shape, jax.ShapeDtypeStruct((PARTS * LIST_ROWS + 2, 128), jnp.int32)),
        in_specs=[in_vmem(), pl.BlockSpec(memory_space=pltpu.HBM), in_vmem()],
        out_specs=(in_vmem(), in_vmem()),
        scratch_shapes=[
            tile_rows(1),
            pltpu.VMEM(near.shape, near.dtype),
            pltpu.SMEM((PARTS * LIST_ROWS + 2, 128), jnp.int32),
            pltpu.SemaphoreType.DMA((8,)),
            pltpu.SemaphoreType.DMA,
        ],
        name="own_rows", **params(46 * 2**20),
    )(links, near, flat(block))
    near = pltpu.with_memory_space_constraint(near, pltpu.VMEM)

    def add(part, acc, *sources):
        return pl.pallas_call(
            functools.partial(middle_kernel, part), out_shape=acc_shape, out_specs=in_vmem(),
            in_specs=[in_smem()] + [in_vmem()] * (2 + len(sources)), scratch_shapes=[tile_rows(len(sources))],
            name=f"rows_{part}", input_output_aliases={2 + len(sources): 0}, **params(),
        )(work, near, *(flat(source) for source in sources), acc)

    beside, two_off, outer, core, acc = lax.optimization_barrier((beside, two_off, outer, core, acc))
    beyond = pair_swap(two_off, "gy")
    beside_outer = between_pairs(beside, "gx")
    beyond_outer = across_both(beside)
    beside_core = pair_swap(beside, "gx")
    acc = add(1, acc, core, outer, beside, beside_core)
    beyond, beside_outer, beyond_outer, acc = lax.optimization_barrier((beyond, beside_outer, beyond_outer, acc))
    beyond_core = pair_swap(beyond, "gx")
    acc = add(2, acc, beside_outer, beyond, beyond_outer)
    split, gram = pl.pallas_call(
        last_kernel,
        out_shape=(
            jax.ShapeDtypeStruct((2 * columns, rows), jnp.bfloat16),
            jax.ShapeDtypeStruct((columns, columns), jnp.float32),
        ),
        in_specs=[in_smem()] + [in_vmem()] * 3, out_specs=(in_vmem(), in_vmem()),
        scratch_shapes=[tile_rows(1), pltpu.VMEM(acc_shape.shape, jnp.float32)], name="rows_3_and_gram", **params(),
    )(work, near, flat(beyond_core), acc)

    gram = sum_over_all(gram)
    basis, factor = pl.pallas_call(
        functools.partial(finish_kernel, scale),
        out_shape=(
            jax.ShapeDtypeStruct((columns, rows), jnp.float32),
            jax.ShapeDtypeStruct((columns, columns), jnp.float32),
        ),
        in_specs=[in_vmem()] * 2, out_specs=(in_vmem(), in_vmem()), name="orthonormalize", **params(),
    )(gram, split)
    return basis.T.reshape(1, 1, rows, columns), factor


def solution(mesh):
    in_specs = (
        P("gx", "gy", None, None, None, None),
        P("gx", "gy", None, None),
        P("gx", "gy", None, None),
    )
    out_specs = (P("gx", "gy", None, None), P())
    return jax.shard_map(shards, mesh=mesh, in_specs=in_specs, out_specs=out_specs, check_vma=False)
```

time: 84.1 us -> 71.1 us (0.85)
  waiting for transfers between devices: 22.4 us -> 8.45 us
  Pallas kernels: 20.2 us -> 28.8 us
  other arithmetic: 6.06 us -> 0.02 us
  between operations: 3.36 us -> 0.77 us
  starting transfers between devices: 22.3 us -> 23.8 us
    ppermute x4, waiting for transfers between devices: 8.91 us -> 0.01 us  [the longest x2 0.01 us: between_pairs(): return lax.ppermute(value, axis, outside(lax.axis_size(axis)))]
    pallas_call x2 -> x3, Pallas kernels: 11.4 us -> 20 us  [the longest x1 12.8 us: shards(): pl.pallas_call(functools.partial(own_kernel, gy_count), out_shape=(acc_sh...]
    ppermute x4 -> x5, starting transfers between devices: 5.53 us -> 10.6 us  [pair_swap(): return lax.ppermute(value, axis, [(i, i ^ 1) for i in range(size)])]
    ppermute x4, starting transfers between devices: 6.43 us -> 3.36 us  [the longest x2 1.38 us: between_pairs(): return lax.ppermute(value, axis, outside(lax.axis_size(axis)))]
    ppermute x7, waiting for transfers between devices: 10.2 us -> 7.56 us  [from_other(): lax.ppermute(value, ('gx', 'gy'), [(i, i ^ mask) for i in range(total)])]
    ppermute x4 -> x5, waiting for transfers between devices: 3.3 us -> 0.88 us  [pair_swap(): return lax.ppermute(value, axis, [(i, i ^ 1) for i in range(size)])]
    select_n x2 -> x0, other arithmetic: 2.03 us -> none  [the longest x1 2 us: work_lists(): steps = (counts + UNROLL - 1) // UNROLL]
    reduce_sum x3 -> x0, other arithmetic: 1.3 us -> none  [the longest x1 0.72 us: work_lists(): jnp.sum((phase == p).astype(jnp.int32))]
  transfers between devices with their start and end apart: 15 -> 16, of which waited for: 8 -> 8; matrix products, arithmetic and copies ran while one was open for 9% -> 1% of each run, Pallas kernels for 14% -> 28%
where the time goes in v2:
time: 71.1 us; the launch traced here: 70.7 us
  Pallas kernels  28.8 us (41%)
  starting transfers between devices  23.8 us (33%)
  local copies, waits for them, and re-layouts  8.79 us (12%)
  waiting for transfers between devices  8.45 us (12%)
  between operations  0.77 us (1%)
    pallas_call x1, Pallas kernels, shards(): pl.pallas_call(functools.partial(own_kernel, gy_count), out_shape=(acc_sh...  12.8 us
    ppermute x5, starting transfers between devices, pair_swap(): return lax.ppermute(value, axis, [(i, i ^ 1) for i in range(size)])  10.6 us
    ppermute x7, starting transfers between devices, from_other(): lax.ppermute(value, ('gx', 'gy'), [(i, i ^ mask) for i in range(total)])  9.79 us
    unnamed x5, local copies, waits for them, and re-layouts  8.71 us
    ppermute x7, waiting for transfers between devices, from_other(): lax.ppermute(value, ('gx', 'gy'), [(i, i ^ mask) for i in range(total)])  7.56 us
    pallas_call x2, Pallas kernels, add(): pl.pallas_call(functools.partial(middle_kernel, part), out_shape=acc_shap...  7.2 us
    pallas_call x1, Pallas kernels, shards(): pl.pallas_call(functools.partial(finish_kernel, scale), out_shape=(jax.Sh...  6.77 us
    pallas_call x1, Pallas kernels, shards(): pl.pallas_call(last_kernel, out_shape=(jax.ShapeDtypeStruct((2 * columns,...  2.05 us
  transfers between devices with their start and end apart: 16, of which 8 were waited for; matrix products, arithmetic and copies ran while one was open for 1% of the time, Pallas kernels for 28%

profile of v2, /device:TPU:0, one launch (start us, length us, event | category | flops | bytes accessed | tf_op | source)
XLA Modules:
  0.0 70.7 jit_solution(9899791670656122177)
XLA Ops:
  0.6 1.3 %collective-permute-start.1 = (bf16[1,1,4096,64]{2,3,1,0:T(8,128)(2,1)}, bf16[1,1,4096,64]{2,3,1,0:T(8,128)(2,1)S(1)}, u32[]{:S(2)}, u32[]{:S(2)}) collective-permute-start(bf16[1,1,4096,64]{2,3,1,0:T(8,128)(2,1)} %param.4), channel_id=1, source_target_pairs={{2,0},{4,2},{6,4},{1,3},{3,5},{5,7},{10,8},{12,10},{14,12},{9,11},... | collective-permute-start | bytes 1572872 | tf_op jit(solution)/shard_map/ppermute | solution.py:46
  1.9 5.2 %collective-permute-start = (bf16[1,1,4096,64]{2,3,1,0:T(8,128)(2,1)}, bf16[1,1,4096,64]{2,3,1,0:T(8,128)(2,1)S(1)}, u32[]{:S(2)}, u32[]{:S(2)}) collective-permute-start(bf16[1,1,4096,64]{2,3,1,0:T(8,128)(2,1)} %param.4), channel_id=1, source_target_pairs={{0,1},{1,0},{2,3},{3,2},{4,5},{5,4},{6,7},{7,6},{8,9},{9,8},{10,11... | collective-permute-start | bytes 1572872 | tf_op jit(solution)/shard_map/ppermute | solution.py:21
  7.2 0.0 collective-permute-start.3
  7.2 0.7 collective-permute-start.2
  7.8 0.7 copy.9
  8.6 0.1 reshape.13.links
  8.6 1.0 %copy-done.1 = bf16[1,1,4096,64]{2,3,1,0:T(8,128)(2,1)S(1)} copy-done((bf16[1,1,4096,64]{2,3,1,0:T(8,128)(2,1)S(1)}, bf16[1,1,4096,64]{2,3,1,0:T(8,128)(2,1)}, u32[]{:S(2)}) %copy-start.1) | copy-done | bytes 524312
  9.7 12.8 %own_rows.1 = (f32[32,128,64]{2,1,0:T(8,128)S(1)}, s32[26,128]{1,0:T(8,128)S(1)}) custom-call(s32[1,640]{1,0:T(1,128)S(1)} %reshape.13.links, bf16[640,128,128]{2,1,0:T(8,128)(2,1)} %bitcast.36, bf16[64,4096]{1,0:T(8,128)(2,1)S(1)} %bitcast.40), custom_call_target="tpu_custom_call" | custom-call | tf_op jit(solution)/shard_map/own_rows/pallas_call | solution.py:259
  22.5 0.1 collective-permute-start.7
  22.7 0.0 collective-permute-start.4
  22.7 0.7 collective-permute-start.6
  23.4 0.7 collective-permute-start.5
  24.1 0.4 collective-permute-done.7
  24.5 7.0 %copy-done = bf16[1,1,32,20,128,128]{5,4,3,2,1,0:T(8,128)(2,1)S(1)} copy-done((bf16[1,1,32,20,128,128]{5,4,3,2,1,0:T(8,128)(2,1)S(1)}, bf16[1,1,32,20,128,128]{5,4,3,2,1,0:T(8,128)(2,1)}, u32[]{:S(2)}) %copy-start) | copy-done | bytes 20971544
  31.5 6.1 %rows_1.1.refs_3_ = f32[32,128,64]{2,1,0:T(8,128)S(1)} custom-call(s32[26,128]{1,0:T(8,128)S(1)} %get-tuple-element.17.work, bf16[640,128,128]{2,1,0:T(8,128)(2,1)S(1)} %bitcast.37, bf16[64,4096]{1,0:T(8,128)(2,1)S(1)} %bitcast.42, bf16[64,4096]{1,0:T(8,128)(2,1)S(1)} %bitcast.43, bf16[64,4096]{1,0:T(8,128)(2,1)S(1)} %bitcast.41, ...), custom_call_target="tpu_custom_call", output_to_operand_aliasing={{}: (6, {})} | custom-call | tf_op jit(solution)/shard_map/rows_1/pallas_call | solution.py:276
  37.6 5.3 %collective-permute-start.8 = (bf16[1,1,4096,64]{2,3,1,0:T(8,128)(2,1)S(1)}, bf16[1,1,4096,64]{2,3,1,0:T(8,128)(2,1)S(1)}, u32[]{:S(2)}, u32[]{:S(2)}) collective-permute-start(bf16[1,1,4096,64]{2,3,1,0:T(8,128)(2,1)S(1)} %collective-permute-done.4), channel_id=1, source_target_pairs={{0,8},{8,0},{16,24},{24,16},{1,9},{9,1},{17,25},{25,17},{2,10},{10... | collective-permute-start | bytes 1572872 | tf_op jit(solution)/shard_map/ppermute | solution.py:21
  42.9 1.1 %rows_2.1.acc_in = f32[32,128,64]{2,1,0:T(8,128)S(1)} custom-call(s32[26,128]{1,0:T(8,128)S(1)} %get-tuple-element.17.work, bf16[640,128,128]{2,1,0:T(8,128)(2,1)S(1)} %bitcast.38, bf16[64,4096]{1,0:T(8,128)(2,1)S(1)} %bitcast.46, bf16[64,4096]{1,0:T(8,128)(2,1)S(1)} %bitcast.44, bf16[64,4096]{1,0:T(8,128)(2,1)S(1)} %bitcast.45, ...), custom_call_target="tpu_custom_call", output_to_operand_aliasing={{}: (5, {})} | custom-call | tf_op jit(solution)/shard_map/rows_2/pallas_call | solution.py:276
  44.0 0.5 collective-permute-done.8
  44.4 2.1 %rows_3_and_gram.1 = (bf16[128,4096]{1,0:T(8,128)(2,1)S(1)}, f32[64,64]{1,0:T(8,128)S(1)}) custom-call(s32[26,128]{1,0:T(8,128)S(1)} %get-tuple-element.17.work, bf16[640,128,128]{2,1,0:T(8,128)(2,1)S(1)} %bitcast.39, bf16[64,4096]{1,0:T(8,128)(2,1)S(1)} %bitcast.48, f32[32,128,64]{2,1,0:T(8,128)S(1)} %rows_2.1.acc_in), custom_call_target="tpu_custom_call" | custom-call | tf_op jit(solution)/shard_map/rows_3_and_gram/pallas_call | solution.py:291
  46.5 1.0 %collective-permute-start.9 = (f32[64,64]{1,0:T(8,128)S(1)}, f32[64,64]{1,0:T(8,128)S(1)}, u32[]{:S(2)}, u32[]{:S(2)}) collective-permute-start(f32[64,64]{1,0:T(8,128)S(1)} %get-tuple-element.28), channel_id=1, source_target_pairs={{0,8},{1,9},{2,10},{3,11},{4,12},{5,13},{6,14},{7,15},{8,0},{9,1},... | collective-permute-start | bytes 49160 | tf_op jit(solution)/shard_map/ppermute | solution.py:221
  47.5 0.9 %collective-permute-done.9 = f32[64,64]{1,0:T(8,128)S(1)} collective-permute-done((f32[64,64]{1,0:T(8,128)S(1)}, f32[64,64]{1,0:T(8,128)S(1)}, u32[]{:S(2)}, u32[]{:S(2)}) %collective-permute-start.9) | collective-permute-done | bytes 16416 | tf_op jit(solution)/shard_map/ppermute | solution.py:221
  48.3 3.7 %collective-permute-start.12 = (f32[64,64]{1,0:T(8,128)S(1)}, f32[64,64]{1,0:T(8,128)S(1)}, u32[]{:S(2)}, u32[]{:S(2)}) collective-permute-start(f32[64,64]{1,0:T(8,128)S(1)} %add.21), channel_id=1, source_target_pairs={{0,17},{1,16},{2,19},{3,18},{4,21},{5,20},{6,23},{7,22},{8,25},{9,... | collective-permute-start | bytes 49160 | tf_op jit(solution)/shard_map/ppermute | solution.py:221
  52.0 0.6 collective-permute-start.10
  52.7 1.3 %collective-permute-done.12 = f32[64,64]{1,0:T(8,128)S(1)} collective-permute-done((f32[64,64]{1,0:T(8,128)S(1)}, f32[64,64]{1,0:T(8,128)S(1)}, u32[]{:S(2)}, u32[]{:S(2)}) %collective-permute-start.12) | collective-permute-done | bytes 16416 | tf_op jit(solution)/shard_map/ppermute | solution.py:221
  53.9 2.0 %collective-permute-done.11 = f32[64,64]{1,0:T(8,128)S(1)} collective-permute-done((f32[64,64]{1,0:T(8,128)S(1)}, f32[64,64]{1,0:T(8,128)S(1)}, u32[]{:S(2)}, u32[]{:S(2)}) %collective-permute-start.11) | collective-permute-done | bytes 16416 | tf_op jit(solution)/shard_map/ppermute | solution.py:221
  55.9 2.6 %collective-permute-start.15 = (f32[64,64]{1,0:T(8,128)S(1)}, f32[64,64]{1,0:T(8,128)S(1)}, u32[]{:S(2)}, u32[]{:S(2)}) collective-permute-start(f32[64,64]{1,0:T(8,128)S(1)} %add_add_fusion.1), channel_id=1, source_target_pairs={{0,6},{1,7},{2,4},{3,5},{4,2},{5,3},{6,0},{7,1},{8,14},{9,15},{10,... | collective-permute-start | bytes 49160 | tf_op jit(solution)/shard_map/ppermute | solution.py:221
  58.6 1.4 %collective-permute-start.14 = (f32[64,64]{1,0:T(8,128)S(1)}, f32[64,64]{1,0:T(8,128)S(1)}, u32[]{:S(2)}, u32[]{:S(2)}) collective-permute-start(f32[64,64]{1,0:T(8,128)S(1)} %add_add_fusion.1), channel_id=1, source_target_pairs={{0,4},{1,5},{2,6},{3,7},{4,0},{5,1},{6,2},{7,3},{8,12},{9,13},{10,... | collective-permute-start | bytes 49160 | tf_op jit(solution)/shard_map/ppermute | solution.py:221
  60.0 0.5 collective-permute-start.13
  60.4 1.5 %collective-permute-done.15 = f32[64,64]{1,0:T(8,128)S(1)} collective-permute-done((f32[64,64]{1,0:T(8,128)S(1)}, f32[64,64]{1,0:T(8,128)S(1)}, u32[]{:S(2)}, u32[]{:S(2)}) %collective-permute-start.15) | collective-permute-done | bytes 16416 | tf_op jit(solution)/shard_map/ppermute | solution.py:221
  61.9 1.4 %collective-permute-done.14 = f32[64,64]{1,0:T(8,128)S(1)} collective-permute-done((f32[64,64]{1,0:T(8,128)S(1)}, f32[64,64]{1,0:T(8,128)S(1)}, u32[]{:S(2)}, u32[]{:S(2)}) %collective-permute-start.14) | collective-permute-done | bytes 16416 | tf_op jit(solution)/shard_map/ppermute | solution.py:221
  63.4 0.5 collective-permute-done.13
  63.9 6.8 %orthonormalize.1 = (f32[64,4096]{1,0:T(8,128)}, f32[64,64]{1,0:T(8,128)}) custom-call(f32[64,64]{1,0:T(8,128)S(1)} %add_add_fusion.gram, bf16[128,4096]{1,0:T(8,128)(2,1)S(1)} %get-tuple-element.29.split), custom_call_target="tpu_custom_call" | custom-call | tf_op jit(solution)/shard_map/orthonormalize/pallas_call | solution.py:302
  (14 shorter events, 0.1 us)
Async XLA Ops:
  0.6 21.9 %collective-permute-start.1 = (bf16[1,1,4096,64]{2,3,1,0:T(8,128)(2,1)}, bf16[1,1,4096,64]{2,3,1,0:T(8,128)(2,1)S(1)}, u32[]{:S(2)}, u32[]{:S(2)}) collective-permute-start(bf16[1,1,4096,64]{2,3,1,0:T(8,128)(2,1)} %param.4), channel_id=1, source_target_pairs={{2,0},{4,2},{6,4},{1,3},{3,5},{5,7},{10,8},{12,10},{14,12},{9,11},... | collective-permute-start | bytes 1572872 | tf_op jit(solution)/shard_map/ppermute | solution.py:46
  1.9 20.6 %collective-permute-start = (bf16[1,1,4096,64]{2,3,1,0:T(8,128)(2,1)}, bf16[1,1,4096,64]{2,3,1,0:T(8,128)(2,1)S(1)}, u32[]{:S(2)}, u32[]{:S(2)}) collective-permute-start(bf16[1,1,4096,64]{2,3,1,0:T(8,128)(2,1)} %param.4), channel_id=1, source_target_pairs={{0,1},{1,0},{2,3},{3,2},{4,5},{5,4},{6,7},{7,6},{8,9},{9,8},{10,11... | collective-permute-start | bytes 1572872 | tf_op jit(solution)/shard_map/ppermute | solution.py:21
  7.2 15.4 %collective-permute-start.3 = (bf16[1,1,4096,64]{2,3,1,0:T(8,128)(2,1)}, bf16[1,1,4096,64]{2,3,1,0:T(8,128)(2,1)S(1)}, u32[]{:S(2)}, u32[]{:S(2)}) collective-permute-start(bf16[1,1,4096,64]{2,3,1,0:T(8,128)(2,1)} %param.4), channel_id=1, source_target_pairs={{0,8},{8,0},{16,24},{24,16},{1,9},{9,1},{17,25},{25,17},{2,10},{10... | collective-permute-start | bytes 1572872 | tf_op jit(solution)/shard_map/ppermute | solution.py:21
  7.2 15.4 %collective-permute-start.2 = (bf16[1,1,4096,64]{2,3,1,0:T(8,128)(2,1)}, bf16[1,1,4096,64]{2,3,1,0:T(8,128)(2,1)S(1)}, u32[]{:S(2)}, u32[]{:S(2)}) collective-permute-start(bf16[1,1,4096,64]{2,3,1,0:T(8,128)(2,1)} %param.4), channel_id=1, source_target_pairs={{8,16},{16,8},{9,17},{17,9},{10,18},{18,10},{11,19},{19,11},{12,20... | collective-permute-start | bytes 1572872 | tf_op jit(solution)/shard_map/ppermute | solution.py:25
  8.6 1.0 %copy-start.1 = (bf16[1,1,4096,64]{2,3,1,0:T(8,128)(2,1)S(1)}, bf16[1,1,4096,64]{2,3,1,0:T(8,128)(2,1)}, u32[]{:S(2)}) copy-start(bf16[1,1,4096,64]{2,3,1,0:T(8,128)(2,1)} %param.4) | copy-start | bytes 1572868
  22.5 2.0 %collective-permute-start.7 = (bf16[1,1,4096,64]{2,3,1,0:T(8,128)(2,1)S(1)}, bf16[1,1,4096,64]{2,3,1,0:T(8,128)(2,1)S(1)}, u32[]{:S(2)}, u32[]{:S(2)}) collective-permute-start(bf16[1,1,4096,64]{2,3,1,0:T(8,128)(2,1)S(1)} %collective-permute-done), channel_id=1, source_target_pairs={{0,8},{8,0},{16,24},{24,16},{1,9},{9,1},{17,25},{25,17},{2,10},{10... | collective-permute-start | bytes 1572872 | tf_op jit(solution)/shard_map/ppermute | solution.py:21
  22.7 14.9 %collective-permute-start.4 = (bf16[1,1,4096,64]{2,3,1,0:T(8,128)(2,1)S(1)}, bf16[1,1,4096,64]{2,3,1,0:T(8,128)(2,1)S(1)}, u32[]{:S(2)}, u32[]{:S(2)}) collective-permute-start(bf16[1,1,4096,64]{2,3,1,0:T(8,128)(2,1)S(1)} %collective-permute-done.1), channel_id=1, source_target_pairs={{0,1},{1,0},{2,3},{3,2},{4,5},{5,4},{6,7},{7,6},{8,9},{9,8},{10,11... | collective-permute-start | bytes 1572872 | tf_op jit(solution)/shard_map/ppermute | solution.py:21
  22.7 14.9 %collective-permute-start.6 = (bf16[1,1,4096,64]{2,3,1,0:T(8,128)(2,1)S(1)}, bf16[1,1,4096,64]{2,3,1,0:T(8,128)(2,1)S(1)}, u32[]{:S(2)}, u32[]{:S(2)}) collective-permute-start(bf16[1,1,4096,64]{2,3,1,0:T(8,128)(2,1)S(1)} %collective-permute-done), channel_id=1, source_target_pairs={{8,18},{10,20},{12,22},{11,17},{13,19},{15,21},{16,10},{18,12},{20... | collective-permute-start | bytes 1572872 | tf_op jit(solution)/shard_map/ppermute | solution.py:39
  23.4 14.2 %collective-permute-start.5 = (bf16[1,1,4096,64]{2,3,1,0:T(8,128)(2,1)S(1)}, bf16[1,1,4096,64]{2,3,1,0:T(8,128)(2,1)S(1)}, u32[]{:S(2)}, u32[]{:S(2)}) collective-permute-start(bf16[1,1,4096,64]{2,3,1,0:T(8,128)(2,1)S(1)} %collective-permute-done), channel_id=1, source_target_pairs={{8,16},{16,8},{9,17},{17,9},{10,18},{18,10},{11,19},{19,11},{12,20... | collective-permute-start | bytes 1572872 | tf_op jit(solution)/shard_map/ppermute | solution.py:25
  24.5 7.0 %copy-start = (bf16[1,1,32,20,128,128]{5,4,3,2,1,0:T(8,128)(2,1)S(1)}, bf16[1,1,32,20,128,128]{5,4,3,2,1,0:T(8,128)(2,1)}, u32[]{:S(2)}) copy-start(bf16[1,1,32,20,128,128]{5,4,3,2,1,0:T(8,128)(2,1)} %param.3) | copy-start | bytes 62914564
  37.6 6.8 %collective-permute-start.8 = (bf16[1,1,4096,64]{2,3,1,0:T(8,128)(2,1)S(1)}, bf16[1,1,4096,64]{2,3,1,0:T(8,128)(2,1)S(1)}, u32[]{:S(2)}, u32[]{:S(2)}) collective-permute-start(bf16[1,1,4096,64]{2,3,1,0:T(8,128)(2,1)S(1)} %collective-permute-done.4), channel_id=1, source_target_pairs={{0,8},{8,0},{16,24},{24,16},{1,9},{9,1},{17,25},{25,17},{2,10},{10... | collective-permute-start | bytes 1572872 | tf_op jit(solution)/shard_map/ppermute | solution.py:21
  46.5 1.9 %collective-permute-start.9 = (f32[64,64]{1,0:T(8,128)S(1)}, f32[64,64]{1,0:T(8,128)S(1)}, u32[]{:S(2)}, u32[]{:S(2)}) collective-permute-start(f32[64,64]{1,0:T(8,128)S(1)} %get-tuple-element.28), channel_id=1, source_target_pairs={{0,8},{1,9},{2,10},{3,11},{4,12},{5,13},{6,14},{7,15},{8,0},{9,1},... | collective-permute-start | bytes 49160 | tf_op jit(solution)/shard_map/ppermute | solution.py:221
  48.3 5.6 %collective-permute-start.12 = (f32[64,64]{1,0:T(8,128)S(1)}, f32[64,64]{1,0:T(8,128)S(1)}, u32[]{:S(2)}, u32[]{:S(2)}) collective-permute-start(f32[64,64]{1,0:T(8,128)S(1)} %add.21), channel_id=1, source_target_pairs={{0,17},{1,16},{2,19},{3,18},{4,21},{5,20},{6,23},{7,22},{8,25},{9,... | collective-permute-start | bytes 49160 | tf_op jit(solution)/shard_map/ppermute | solution.py:221
  52.0 3.9 %collective-permute-start.11 = (f32[64,64]{1,0:T(8,128)S(1)}, f32[64,64]{1,0:T(8,128)S(1)}, u32[]{:S(2)}, u32[]{:S(2)}) collective-permute-start(f32[64,64]{1,0:T(8,128)S(1)} %add.21), channel_id=1, source_target_pairs={{0,1},{1,0},{2,3},{3,2},{4,5},{5,4},{6,7},{7,6},{8,9},{9,8},{10,11... | collective-permute-start | bytes 49160 | tf_op jit(solution)/shard_map/ppermute | solution.py:221
  52.0 3.9 %collective-permute-start.10 = (f32[64,64]{1,0:T(8,128)S(1)}, f32[64,64]{1,0:T(8,128)S(1)}, u32[]{:S(2)}, u32[]{:S(2)}) collective-permute-start(f32[64,64]{1,0:T(8,128)S(1)} %add.21), channel_id=1, source_target_pairs={{0,16},{1,17},{2,18},{3,19},{4,20},{5,21},{6,22},{7,23},{8,24},{9,... | collective-permute-start | bytes 49160 | tf_op jit(solution)/shard_map/ppermute | solution.py:221
  55.9 6.0 %collective-permute-start.15 = (f32[64,64]{1,0:T(8,128)S(1)}, f32[64,64]{1,0:T(8,128)S(1)}, u32[]{:S(2)}, u32[]{:S(2)}) collective-permute-start(f32[64,64]{1,0:T(8,128)S(1)} %add_add_fusion.1), channel_id=1, source_target_pairs={{0,6},{1,7},{2,4},{3,5},{4,2},{5,3},{6,0},{7,1},{8,14},{9,15},{10,... | collective-permute-start | bytes 49160 | tf_op jit(solution)/shard_map/ppermute | solution.py:221
  58.6 4.8 %collective-permute-start.14 = (f32[64,64]{1,0:T(8,128)S(1)}, f32[64,64]{1,0:T(8,128)S(1)}, u32[]{:S(2)}, u32[]{:S(2)}) collective-permute-start(f32[64,64]{1,0:T(8,128)S(1)} %add_add_fusion.1), channel_id=1, source_target_pairs={{0,4},{1,5},{2,6},{3,7},{4,0},{5,1},{6,2},{7,3},{8,12},{9,13},{10,... | collective-permute-start | bytes 49160 | tf_op jit(solution)/shard_map/ppermute | solution.py:221
  60.0 3.9 %collective-permute-start.13 = (f32[64,64]{1,0:T(8,128)S(1)}, f32[64,64]{1,0:T(8,128)S(1)}, u32[]{:S(2)}, u32[]{:S(2)}) collective-permute-start(f32[64,64]{1,0:T(8,128)S(1)} %add_add_fusion.1), channel_id=1, source_target_pairs={{0,2},{1,3},{2,0},{3,1},{4,6},{5,7},{6,4},{7,5},{8,10},{9,11},{10,... | collective-permute-start | bytes 49160 | tf_op jit(solution)/shard_map/ppermute | solution.py:221

commit v3 on v2

--- a/solution.py
+++ b/solution.py
@@ -8,6 +8,8 @@
 from jax.sharding import PartitionSpec as P
 
 UNROLL = 32
+EARLY = 3
+CHUNKS = 8
 PARTS = 4
 LIST_ROWS = 6
 PART_OF = (0, 1, 1, 1, 1, 2, 2, 3, 2)
@@ -68,31 +70,44 @@
     own_row, beside = owner_y == own_y, owner_y == (own_y ^ 1)
     kind = across + jnp.where(own_row, 0, jnp.where(beside, 3, 6))
     part, slot = look_up(PART_OF, kind), look_up(SLOT_OF, kind)
-    entry = (place & (tiles_dev - 1)) * blocks + lax.shift_right_logical(place, tile_bits)
-    code = entry * 512 + slot * tiles_dev + (link & (tiles_dev - 1)) + 1
+    code = place * 512 + slot * tiles_dev + (link & (tiles_dev - 1)) + 1
 
     def ones_where(hit):
         return jnp.where(hit, 1.0, 0.0).astype(jnp.bfloat16)
 
-    def iota(rows, dim):
-        return lax.broadcasted_iota(jnp.int32, (rows, count), dim)
-
-    is_part = iota(128, 0) == part
-    earlier = ones_where(lax.broadcasted_iota(jnp.int32, (count, count), 0) < lax.broadcasted_iota(jnp.int32, (count, count), 1))
-    before = jnp.dot(ones_where(is_part[:16]), earlier, preferred_element_type=jnp.float32)
-    rank = jnp.sum(jnp.where(is_part[:16], before, 0.0), axis=0, keepdims=True).astype(jnp.int32)
+    def iota(shape, dim):
+        return lax.broadcasted_iota(jnp.int32, shape, dim)
+
+    def dot(left, right):
+        return jnp.dot(left, right, preferred_element_type=jnp.float32)
+
+    def row_dot(left, right):
+        return lax.dot_general(left, right, ROW_BY_ROW, preferred_element_type=jnp.float32)
+
+    def to_even(length):
+        return ((length.astype(jnp.int32) + 1) & -2).astype(jnp.float32).astype(jnp.bfloat16)
+
+    groups, lines = PARTS * tiles_dev, PARTS * LIST_ROWS + 2
+    group = part * tiles_dev + lax.div(place, blocks)
+    in_group = iota((groups, count), 0) == group
+    members = ones_where(in_group)
+    before = dot(members, ones_where(iota((count, count), 0) < iota((count, count), 1)))
+    lengths = dot(members, jnp.ones((count, 128), jnp.bfloat16))
+    first, second = iota((groups, groups), 0), iota((groups, groups), 1)
+    same_part = lax.shift_right_logical(first, tile_bits) == lax.shift_right_logical(second, tile_bits)
+    starts = dot(ones_where(same_part & (second < first)), to_even(lengths))
+    rank = jnp.sum(jnp.where(in_group, before + starts[:, :1], 0.0), axis=0, keepdims=True).astype(jnp.int32)
     row = part * LIST_ROWS + lax.shift_right_logical(rank, 7)
-    column_hits = ones_where(iota(128, 0) == (rank & 127))
-    row_hits = iota(PARTS * LIST_ROWS + 2, 0) == row
-    listed = jnp.zeros((PARTS * LIST_ROWS + 2, 128), jnp.float32)
+    column_hits = ones_where(iota((128, count), 0) == (rank & 127))
+    row_hits = iota((lines, count), 0) == row
+    listed = jnp.zeros((lines, 128), jnp.float32)
     for shift in (16, 8, 0):
         digit = (lax.shift_right_logical(code, shift) & 255).astype(jnp.float32)
-        values = jnp.where(row_hits, digit, 0.0).astype(jnp.bfloat16)
-        listed = listed * 256.0 + lax.dot_general(values, column_hits, ROW_BY_ROW, preferred_element_type=jnp.float32)
-    ones = jnp.ones((PARTS * LIST_ROWS + 2, count), jnp.bfloat16)
-    lengths = lax.dot_general(ones, ones_where(is_part), ROW_BY_ROW, preferred_element_type=jnp.float32)
-    line = lax.broadcasted_iota(jnp.int32, listed.shape, 0)
-    work[...] = jnp.where(line == PARTS * LIST_ROWS + 1, lengths, listed).astype(jnp.int32)
+        listed = listed * 256.0 + row_dot(jnp.where(row_hits, digit, 0.0).astype(jnp.bfloat16), column_hits)
+    by_group = to_even(row_dot(jnp.ones((lines, count), jnp.bfloat16), members))
+    of_part = iota((128, groups), 0) == lax.shift_right_logical(iota((128, groups), 1), tile_bits)
+    totals = row_dot(by_group, ones_where(of_part))
+    work[...] = jnp.where(iota((lines, 128), 0) == lines - 1, totals, listed).astype(jnp.int32)
 
 
 def lay_out(sources, rows, tiles_dev):
@@ -103,57 +118,107 @@
             rows[1 + slot * tiles_dev + tile] = source[:, tile * width:(tile + 1) * width]
 
 
-def accumulate(part, work, near, acc, rows):
+def batches(part, work):
+    return lax.div(work[PARTS * LIST_ROWS + 1, part] + (UNROLL - 1), UNROLL)
+
+
+def code_at(part, work, index, lane):
+    groups = 128 // UNROLL
+    return work[part * LIST_ROWS + lax.div(index, groups), lax.rem(index, groups) * UNROLL + lane]
+
+
+def entry_of(code):
+    return lax.shift_right_logical(code, 9)
+
+
+def add_batch(part, work, index, tile_of, blocks, acc, rows):
+    products = []
+    for lane in range(0, UNROLL, 2):
+        codes = [code_at(part, work, index, lane + i) for i in range(2)]
+        entries = [entry_of(code) for code in codes]
+        left = jnp.concatenate([tile_of(entry, lane + i) for i, entry in enumerate(entries)], axis=1)
+        right = jnp.concatenate([rows[code & 511] for code in codes], axis=1)
+        product = lax.dot_general(left, right, ROW_BY_ROW, preferred_element_type=jnp.float32)
+        products.append((lax.div(entries[0], blocks), product))
+    for target, product in products:
+        acc[target] += product
+
+
+def accumulate(part, work, near, acc, rows, first=0):
+    blocks = near.shape[0] // acc.shape[0]
+
+    def step(index, carry):
+        add_batch(part, work, index, lambda entry, lane: near[entry], blocks, acc, rows)
+        return carry
+
+    lax.fori_loop(first, batches(part, work), step, 0)
+
+
+def own_kernel(gy_count, links, near_hbm, own, acc, work, rows, tiles, work_smem, sems, work_sem):
     tiles_dev = acc.shape[0]
-    blocks = near.shape[0] // tiles_dev
-    groups = 128 // UNROLL
-
-    def step(index, carry):
-        line = part * LIST_ROWS + lax.div(index, groups)
-        begin = lax.rem(index, groups) * UNROLL
-        products = []
-        for lane in range(UNROLL):
-            code = work[line, begin + lane]
-            entry = lax.shift_right_logical(code, 9)
-            product = lax.dot_general(
-                near[entry], rows[code & 511], ROW_BY_ROW, preferred_element_type=jnp.float32
-            )
-            products.append((lax.div(entry, blocks), product))
-        for target, product in products:
-            acc[target] += product
-        return carry
-
-    length = work[PARTS * LIST_ROWS + 1, part]
-    lax.fori_loop(0, lax.div(length + (UNROLL - 1), UNROLL), step, 0)
-
-
-def own_kernel(gy_count, links, near_hbm, own, acc, work, rows, near, work_smem, sems, work_sem):
-    tiles_dev = acc.shape[0]
-    chunks = sems.shape[0]
-    length = near.shape[0] // chunks
-    copies = [
-        pltpu.make_async_copy(
-            near_hbm.at[pl.ds(c * length, length)], near.at[pl.ds(c * length, length)], sems.at[c]
-        )
-        for c in range(chunks)
-    ]
-    for copy in copies:
-        copy.start()
-    build_lists(links, work, tiles_dev, near.shape[0] // tiles_dev, gy_count)
+    blocks = near_hbm.shape[0] // tiles_dev
+    build_lists(links, work, tiles_dev, blocks, gy_count)
     work_copy = pltpu.make_async_copy(work, work_smem, work_sem)
     work_copy.start()
     lay_out((own,), rows, tiles_dev)
     acc[...] = jnp.zeros(acc.shape, acc.dtype)
     work_copy.wait()
-    for copy in copies:
-        copy.wait()
-    accumulate(0, work_smem, near, acc, rows)
+    count = jnp.minimum(batches(0, work_smem), EARLY)
+
+    def fetch(index, carry):
+        for lane in range(UNROLL):
+            entry = entry_of(code_at(0, work_smem, index, lane))
+            pltpu.make_async_copy(near_hbm.at[entry], tiles.at[index * UNROLL + lane], sems.at[index]).start()
+        return carry
+
+    def step(index, carry):
+        held = tiles.at[pl.ds(index * UNROLL, UNROLL)]
+        pltpu.make_async_copy(near_hbm.at[pl.ds(0, UNROLL)], held, sems.at[index]).wait()
+        add_batch(0, work_smem, index, lambda entry, lane: held[lane], blocks, acc, rows)
+        return carry
+
+    lax.fori_loop(0, count, fetch, 0)
+    lax.fori_loop(0, count, step, 0)
 
 
 def middle_kernel(part, work, near, *refs):
     acc, rows = refs[-2:]
     lay_out(refs[:-3], rows, acc.shape[0])
     accumulate(part, work, near, acc, rows)
+
+
+def loading_kernel(work, near_hbm, *refs):
+    near, acc, rows, own_rows, sems = refs[-5:]
+    sources = refs[:-6]
+    tiles_dev = acc.shape[0]
+    blocks = near.shape[0] // tiles_dev
+    chunks = sems.shape[0]
+    length = near.shape[0] // chunks
+
+    def load(chunk):
+        held = pl.ds(chunk * length, length)
+        return pltpu.make_async_copy(near_hbm.at[held], near.at[held], sems.at[chunk])
+
+    for chunk in range(chunks):
+        load(chunk).start()
+    lay_out(sources[1:], rows, tiles_dev)
+    count = batches(1, work)
+
+    def wait(chunk, carry):
+        load(chunk).wait()
+        return carry
+
+    def step(index, there):
+        last = lax.div(entry_of(code_at(1, work, index, UNROLL - 2)), length)
+        needed = jnp.where(index == count - 1, chunks, last + 1)
+        lax.fori_loop(there, needed, wait, 0)
+        add_batch(1, work, index, lambda entry, lane: near[entry], blocks, acc, rows)
+        return jnp.maximum(there, needed)
+
+    there = lax.fori_loop(0, count, step, jnp.int32(0))
+    lax.fori_loop(there, chunks, wait, 0)
+    lay_out(sources[:1], own_rows, tiles_dev)
+    accumulate(0, work, near, acc, own_rows, EARLY)
 
 
 def last_kernel(work, near, source, acc_in, split, gram, rows, acc):
@@ -175,31 +240,40 @@
 
 def finish_kernel(scale, gram, split, basis, factor):
     columns = gram.shape[0]
-    row = lax.broadcasted_iota(jnp.int32, (columns, columns), 0)
-    column = lax.broadcasted_iota(jnp.int32, (columns, columns), 1)
-    unit = jnp.where(row == column, 1.0, 0.0)
-    work = jnp.concatenate([gram[...], unit], axis=1)
-    wide_row = lax.broadcasted_iota(jnp.int32, work.shape, 0)
-    for k in range(columns - 1):
-        begin = k // 8 * 8
-        live = work[begin:]
-        pivot_row = work[k:k + 1]
-        pivot = pivot_row[:, k:k + 1]
-        ratio = live[:, k:k + 1] * (1.0 / pivot)
-        ratio = jnp.where(wide_row[begin:] > k, ratio, 0.0)
-        live = live - ratio * pivot_row
-        work = live if begin == 0 else jnp.concatenate([work[:begin], live], axis=0)
-    left, right = work[:, :columns], work[:, columns:]
-    diagonal = jnp.sum(jnp.where(row == column, left, 0.0), axis=1, keepdims=True)
-    root = lax.rsqrt(diagonal)
-    upper = jnp.where(row <= column, left, 0.0) * root
-    factor[...] = upper * (1.0 / scale)
-    weight = right * (root * scale)
+    shape = (8, 2 * columns)
+    row = lax.broadcasted_iota(jnp.int32, shape, 0)
+    lane = lax.broadcasted_iota(jnp.int32, shape, 1)
+    groups = columns // 8
+    live = []
+    for g in range(groups):
+        unit = jnp.where(lane == row + (columns + 8 * g), 1.0, 0.0)
+        live.append(jnp.concatenate([gram[8 * g:8 * g + 8, :], unit[:, columns:]], axis=1))
+    done = []
+    for g in range(groups):
+        cols = [[jnp.broadcast_to(part[:, 8 * g + j:8 * g + j + 1], shape) for part in live] for j in range(8)]
+        pivots = jnp.ones(shape, jnp.float32)
+        for j in range(8):
+            pivot = jnp.broadcast_to(cols[j][0][j:j+1], shape)
+            pivots = jnp.where(row == j, pivot, pivots)
+            inverse = 1.0 / pivot
+            ratios = [part * inverse for part in cols[j]]
+            ratios[0] = jnp.where(row > j, ratios[0], 0.0)
+            for i in range(j + 1, 8):
+                pick = jnp.broadcast_to(cols[i][0][j:j+1], shape)
+                cols[i] = [part - ratio * pick for part, ratio in zip(cols[i], ratios)]
+            pick = jnp.broadcast_to(live[0][j:j+1], shape)
+            live = [part - ratio * pick for part, ratio in zip(live, ratios)]
+        done.append(live[0] * lax.rsqrt(pivots))
+        live = live[1:]
+    whole = jnp.concatenate(done, axis=0)
+    left, right = whole[:, :columns], whole[:, columns:]
+    on_or_above = lax.broadcasted_iota(jnp.int32, left.shape, 0) <= lax.broadcasted_iota(jnp.int32, left.shape, 1)
+    factor[...] = jnp.where(on_or_above, left, 0.0) * (1.0 / scale)
+    weight = right * scale
     high = weight.astype(jnp.bfloat16)
     low = (weight - high.astype(jnp.float32)).astype(jnp.bfloat16)
-    high_rows = split[:columns]
     stacked = jnp.concatenate([high, high, low], axis=1)
-    values = jnp.concatenate([split[...], high_rows], axis=0)
+    values = jnp.concatenate([split[...], split[:columns]], axis=0)
     basis[...] = jnp.dot(stacked, values, preferred_element_type=jnp.float32)
 
 
@@ -243,7 +317,7 @@
     core = pair_swap(block, "gx")
 
     count = tiles_dev * blocks
-    links = adjacency[0, 0].T.reshape(1, -1)
+    links = adjacency[0, 0].reshape(1, -1)
     near = near_tiles.reshape(count, width, width)
     acc_shape = jax.ShapeDtypeStruct((tiles_dev, width, columns), jnp.float32)
     flat = lambda value: value[0, 0].T
@@ -263,14 +337,13 @@
         out_specs=(in_vmem(), in_vmem()),
         scratch_shapes=[
             tile_rows(1),
-            pltpu.VMEM(near.shape, near.dtype),
+            pltpu.VMEM((EARLY * UNROLL, width, width), near.dtype),
             pltpu.SMEM((PARTS * LIST_ROWS + 2, 128), jnp.int32),
-            pltpu.SemaphoreType.DMA((8,)),
+            pltpu.SemaphoreType.DMA((EARLY,)),
             pltpu.SemaphoreType.DMA,
         ],
         name="own_rows", **params(46 * 2**20),
     )(links, near, flat(block))
-    near = pltpu.with_memory_space_constraint(near, pltpu.VMEM)
 
     def add(part, acc, *sources):
         return pl.pallas_call(
@@ -284,7 +357,14 @@
     beside_outer = between_pairs(beside, "gx")
     beyond_outer = across_both(beside)
     beside_core = pair_swap(beside, "gx")
-    acc = add(1, acc, core, outer, beside, beside_core)
+    near, acc = pl.pallas_call(
+        loading_kernel,
+        out_shape=(pltpu.VMEM(near.shape, near.dtype), acc_shape),
+        in_specs=[in_smem(), pl.BlockSpec(memory_space=pltpu.HBM)] + [in_vmem()] * 6,
+        out_specs=(in_vmem(), in_vmem()),
+        scratch_shapes=[tile_rows(4), tile_rows(1), pltpu.SemaphoreType.DMA((CHUNKS,))],
+        name="rows_1", input_output_aliases={7: 1}, **params(24 * 2**20),
+    )(work, near, *(flat(source) for source in (block, core, outer, beside, beside_core)), acc)
     beyond, beside_outer, beyond_outer, acc = lax.optimization_barrier((beyond, beside_outer, beyond_outer, acc))
     beyond_core = pair_swap(beyond, "gx")
     acc = add(2, acc, beside_outer, beyond, beyond_outer)

time: 71.1 us -> 63.6 us (0.89)
  local copies, waits for them, and re-layouts: 8.79 us -> 1.92 us
  Pallas kernels: 28.8 us -> 22.6 us
  waiting for transfers between devices: 8.45 us -> 13.5 us
    pallas_call x0 -> x1, Pallas kernels: none -> 11.9 us  [shards(): pl.pallas_call(loading_kernel, out_shape=(pltpu.VMEM(near.shape, near.dty...]
    pallas_call x1, Pallas kernels: 12.8 us -> 4.37 us  [shards(): pl.pallas_call(functools.partial(own_kernel, gy_count), out_shape=(acc_sh...]
    unnamed x5, local copies, waits for them, and re-layouts: 8.71 us -> 1.82 us
    pallas_call x2 -> x1, Pallas kernels: 7.2 us -> 1.07 us  [add(): pl.pallas_call(functools.partial(middle_kernel, part), out_shape=acc_shap...]
    pallas_call x1, Pallas kernels: 6.77 us -> 3.14 us  [shards(): pl.pallas_call(functools.partial(finish_kernel, scale), out_shape=(jax.Sh...]
    ppermute x1, waiting for transfers between devices: 0.01 us -> 3.34 us  [two_back(): return lax.ppermute(value, axis, pairs)]
    ppermute x5, waiting for transfers between devices: 0.88 us -> 1.79 us  [pair_swap(): return lax.ppermute(value, axis, [(i, i ^ 1) for i in range(size)])]
    ppermute x7, waiting for transfers between devices: 7.56 us -> 8.37 us  [from_other(): lax.ppermute(value, ('gx', 'gy'), [(i, i ^ mask) for i in range(total)])]
  transfers between devices with their start and end apart: 16 -> 16, of which waited for: 8 -> 9; matrix products, arithmetic and copies ran while one was open for 1% -> 1% of each run, Pallas kernels for 28% -> 28%
where the time goes in v3:
time: 63.6 us; the launch traced here: 63 us
  starting transfers between devices  24.2 us (38%)
  Pallas kernels  22.6 us (36%)
  waiting for transfers between devices  13.5 us (21%)
  local copies, waits for them, and re-layouts  1.92 us (3%)
  between operations  0.76 us (1%)
    pallas_call x1, Pallas kernels, shards(): pl.pallas_call(loading_kernel, out_shape=(pltpu.VMEM(near.shape, near.dty...  11.9 us
    ppermute x5, starting transfers between devices, pair_swap(): return lax.ppermute(value, axis, [(i, i ^ 1) for i in range(size)])  10.5 us
    ppermute x7, starting transfers between devices, from_other(): lax.ppermute(value, ('gx', 'gy'), [(i, i ^ mask) for i in range(total)])  10.3 us
    ppermute x7, waiting for transfers between devices, from_other(): lax.ppermute(value, ('gx', 'gy'), [(i, i ^ mask) for i in range(total)])  8.37 us
    pallas_call x1, Pallas kernels, shards(): pl.pallas_call(functools.partial(own_kernel, gy_count), out_shape=(acc_sh...  4.37 us
    ppermute x1, waiting for transfers between devices, two_back(): return lax.ppermute(value, axis, pairs)  3.34 us
    pallas_call x1, Pallas kernels, shards(): pl.pallas_call(functools.partial(finish_kernel, scale), out_shape=(jax.Sh...  3.14 us
    pallas_call x1, Pallas kernels, shards(): pl.pallas_call(last_kernel, out_shape=(jax.ShapeDtypeStruct((2 * columns,...  2.05 us
  transfers between devices with their start and end apart: 16, of which 9 were waited for; matrix products, arithmetic and copies ran while one was open for 1% of the time, Pallas kernels for 28%

profile of v3, /device:TPU:0, one launch (start us, length us, event | category | flops | bytes accessed | tf_op | source)
XLA Modules:
  0.0 63.0 jit_solution(3610708272901655998)
XLA Ops:
  0.6 3.0 %collective-permute-start = (bf16[1,1,4096,64]{2,3,1,0:T(8,128)(2,1)}, bf16[1,1,4096,64]{2,3,1,0:T(8,128)(2,1)S(1)}, u32[]{:S(2)}, u32[]{:S(2)}) collective-permute-start(bf16[1,1,4096,64]{2,3,1,0:T(8,128)(2,1)} %param.4), channel_id=1, source_target_pairs={{0,1},{1,0},{2,3},{3,2},{4,5},{5,4},{6,7},{7,6},{8,9},{9,8},{10,11... | collective-permute-start | bytes 1572872 | tf_op jit(solution)/shard_map/ppermute | solution.py:23
  3.6 1.3 %collective-permute-start.1 = (bf16[1,1,4096,64]{2,3,1,0:T(8,128)(2,1)}, bf16[1,1,4096,64]{2,3,1,0:T(8,128)(2,1)S(1)}, u32[]{:S(2)}, u32[]{:S(2)}) collective-permute-start(bf16[1,1,4096,64]{2,3,1,0:T(8,128)(2,1)} %param.4), channel_id=1, source_target_pairs={{2,0},{4,2},{6,4},{1,3},{3,5},{5,7},{10,8},{12,10},{14,12},{9,11},... | collective-permute-start | bytes 1572872 | tf_op jit(solution)/shard_map/ppermute | solution.py:48
  4.9 0.7 %collective-permute-start.2 = (bf16[1,1,4096,64]{2,3,1,0:T(8,128)(2,1)}, bf16[1,1,4096,64]{2,3,1,0:T(8,128)(2,1)S(1)}, u32[]{:S(2)}, u32[]{:S(2)}) collective-permute-start(bf16[1,1,4096,64]{2,3,1,0:T(8,128)(2,1)} %param.4), channel_id=1, source_target_pairs={{8,16},{16,8},{9,17},{17,9},{10,18},{18,10},{11,19},{19,11},{12,20... | collective-permute-start | bytes 1572872 | tf_op jit(solution)/shard_map/ppermute | solution.py:27
  5.6 2.9 %collective-permute-start.3 = (bf16[1,1,4096,64]{2,3,1,0:T(8,128)(2,1)}, bf16[1,1,4096,64]{2,3,1,0:T(8,128)(2,1)S(1)}, u32[]{:S(2)}, u32[]{:S(2)}) collective-permute-start(bf16[1,1,4096,64]{2,3,1,0:T(8,128)(2,1)} %param.4), channel_id=1, source_target_pairs={{0,8},{8,0},{16,24},{24,16},{1,9},{9,1},{17,25},{25,17},{2,10},{10... | collective-permute-start | bytes 1572872 | tf_op jit(solution)/shard_map/ppermute | solution.py:23
  8.5 0.8 %copy.8 = s32[1,1,32,20]{3,2,1,0:T(8,128)S(1)} copy(s32[1,1,32,20]{2,1,3,0:T(1,128)} %param.5) | data formatting | bytes 5120 | tf_op args[2]
  9.3 0.1 reshape_squeeze.3.links
  9.4 0.0 copy-start
  9.4 1.0 %copy-done = bf16[1,1,4096,64]{2,3,1,0:T(8,128)(2,1)S(1)} copy-done((bf16[1,1,4096,64]{2,3,1,0:T(8,128)(2,1)S(1)}, bf16[1,1,4096,64]{2,3,1,0:T(8,128)(2,1)}, u32[]{:S(2)}) %copy-start) | copy-done | bytes 524312
  10.5 4.4 %own_rows.1 = (f32[32,128,64]{2,1,0:T(8,128)S(1)}, s32[26,128]{1,0:T(8,128)S(1)}) custom-call(s32[1,640]{1,0:T(1,128)S(1)} %reshape_squeeze.3.links, bf16[640,128,128]{2,1,0:T(8,128)(2,1)} %bitcast.43, bf16[64,4096]{1,0:T(8,128)(2,1)S(1)} %bitcast.33), custom_call_target="tpu_custom_call" | custom-call | tf_op jit(solution)/shard_map/own_rows/pallas_call | solution.py:333
  14.9 0.9 %collective-permute-done = bf16[1,1,4096,64]{2,3,1,0:T(8,128)(2,1)S(1)} collective-permute-done((bf16[1,1,4096,64]{2,3,1,0:T(8,128)(2,1)}, bf16[1,1,4096,64]{2,3,1,0:T(8,128)(2,1)S(1)}, u32[]{:S(2)}, u32[]{:S(2)}) %collective-permute-start) | collective-permute-done | bytes 524320 | tf_op jit(solution)/shard_map/ppermute | solution.py:23
  15.8 3.3 %collective-permute-done.1 = bf16[1,1,4096,64]{2,3,1,0:T(8,128)(2,1)S(1)} collective-permute-done((bf16[1,1,4096,64]{2,3,1,0:T(8,128)(2,1)}, bf16[1,1,4096,64]{2,3,1,0:T(8,128)(2,1)S(1)}, u32[]{:S(2)}, u32[]{:S(2)}) %collective-permute-start.1) | collective-permute-done | bytes 524320 | tf_op jit(solution)/shard_map/ppermute | solution.py:48
  19.1 0.7 %collective-permute-start.6 = (bf16[1,1,4096,64]{2,3,1,0:T(8,128)(2,1)S(1)}, bf16[1,1,4096,64]{2,3,1,0:T(8,128)(2,1)S(1)}, u32[]{:S(2)}, u32[]{:S(2)}) collective-permute-start(bf16[1,1,4096,64]{2,3,1,0:T(8,128)(2,1)S(1)} %collective-permute-done), channel_id=1, source_target_pairs={{8,16},{16,8},{9,17},{17,9},{10,18},{18,10},{11,19},{19,11},{12,20... | collective-permute-start | bytes 1572872 | tf_op jit(solution)/shard_map/ppermute | solution.py:27
  19.8 0.7 %collective-permute-start.7 = (bf16[1,1,4096,64]{2,3,1,0:T(8,128)(2,1)S(1)}, bf16[1,1,4096,64]{2,3,1,0:T(8,128)(2,1)S(1)}, u32[]{:S(2)}, u32[]{:S(2)}) collective-permute-start(bf16[1,1,4096,64]{2,3,1,0:T(8,128)(2,1)S(1)} %collective-permute-done), channel_id=1, source_target_pairs={{8,18},{10,20},{12,22},{11,17},{13,19},{15,21},{16,10},{18,12},{20... | collective-permute-start | bytes 1572872 | tf_op jit(solution)/shard_map/ppermute | solution.py:41
  20.5 0.1 collective-permute-start.5
  20.6 0.4 collective-permute-done.4
  21.0 11.9 %rows_1.1 = (bf16[640,128,128]{2,1,0:T(8,128)(2,1)S(1)}, f32[32,128,64]{2,1,0:T(8,128)S(1)}) custom-call(s32[26,128]{1,0:T(8,128)S(1)} %get-tuple-element.19.work, bf16[640,128,128]{2,1,0:T(8,128)(2,1)} %bitcast.44, bf16[64,4096]{1,0:T(8,128)(2,1)S(1)} %bitcast.34, bf16[64,4096]{1,0:T(8,128)(2,1)S(1)} %bitcast.37, ...), custom_call_target="tpu_custom_call", output_to_operand_aliasing={{1}: (7, {})} | custom-call | tf_op jit(solution)/shard_map/rows_1/pallas_call | solution.py:360
  33.0 4.5 %collective-permute-start.8 = (bf16[1,1,4096,64]{2,3,1,0:T(8,128)(2,1)S(1)}, bf16[1,1,4096,64]{2,3,1,0:T(8,128)(2,1)S(1)}, u32[]{:S(2)}, u32[]{:S(2)}) collective-permute-start(bf16[1,1,4096,64]{2,3,1,0:T(8,128)(2,1)S(1)} %collective-permute-done.5), channel_id=1, source_target_pairs={{0,8},{8,0},{16,24},{24,16},{1,9},{9,1},{17,25},{25,17},{2,10},{10... | collective-permute-start | bytes 1572872 | tf_op jit(solution)/shard_map/ppermute | solution.py:23
  37.5 1.1 %rows_2.1.acc_in = f32[32,128,64]{2,1,0:T(8,128)S(1)} custom-call(s32[26,128]{1,0:T(8,128)S(1)} %get-tuple-element.19.work, bf16[640,128,128]{2,1,0:T(8,128)(2,1)S(1)} %get-tuple-element.25.near, bf16[64,4096]{1,0:T(8,128)(2,1)S(1)} %bitcast.38, bf16[64,4096]{1,0:T(8,128)(2,1)S(1)} %bitcast.40, ...), custom_call_target="tpu_custom_call", output_to_operand_aliasing={{}: (5, {})} | custom-call | tf_op jit(solution)/shard_map/rows_2/pallas_call | solution.py:349
  38.6 0.5 collective-permute-done.8
  39.1 2.1 %rows_3_and_gram.1 = (bf16[128,4096]{1,0:T(8,128)(2,1)S(1)}, f32[64,64]{1,0:T(8,128)S(1)}) custom-call(s32[26,128]{1,0:T(8,128)S(1)} %get-tuple-element.19.work, bf16[640,128,128]{2,1,0:T(8,128)(2,1)S(1)} %get-tuple-element.25.near, bf16[64,4096]{1,0:T(8,128)(2,1)S(1)} %bitcast.42, f32[32,128,64]{2,1,0:T(8,128)S(1)} %rows_2.1.acc_in), custom_call_target="tpu_custom_call" | custom-call | tf_op jit(solution)/shard_map/rows_3_and_gram/pallas_call | solution.py:371
  41.1 1.4 %collective-permute-start.9 = (f32[64,64]{1,0:T(8,128)S(1)}, f32[64,64]{1,0:T(8,128)S(1)}, u32[]{:S(2)}, u32[]{:S(2)}) collective-permute-start(f32[64,64]{1,0:T(8,128)S(1)} %get-tuple-element.32), channel_id=1, source_target_pairs={{0,8},{1,9},{2,10},{3,11},{4,12},{5,13},{6,14},{7,15},{8,0},{9,1},... | collective-permute-start | bytes 49160 | tf_op jit(solution)/shard_map/ppermute | solution.py:295
  42.5 0.9 %collective-permute-done.9 = f32[64,64]{1,0:T(8,128)S(1)} collective-permute-done((f32[64,64]{1,0:T(8,128)S(1)}, f32[64,64]{1,0:T(8,128)S(1)}, u32[]{:S(2)}, u32[]{:S(2)}) %collective-permute-start.9) | collective-permute-done | bytes 16416 | tf_op jit(solution)/shard_map/ppermute | solution.py:295
  43.4 0.4 collective-permute-start.10
  43.8 3.8 %collective-permute-start.11 = (f32[64,64]{1,0:T(8,128)S(1)}, f32[64,64]{1,0:T(8,128)S(1)}, u32[]{:S(2)}, u32[]{:S(2)}) collective-permute-start(f32[64,64]{1,0:T(8,128)S(1)} %add.21), channel_id=1, source_target_pairs={{0,1},{1,0},{2,3},{3,2},{4,5},{5,4},{6,7},{7,6},{8,9},{9,8},{10,11... | collective-permute-start | bytes 49160 | tf_op jit(solution)/shard_map/ppermute | solution.py:295
  47.6 0.2 collective-permute-start.12
  47.8 1.6 %collective-permute-done.11 = f32[64,64]{1,0:T(8,128)S(1)} collective-permute-done((f32[64,64]{1,0:T(8,128)S(1)}, f32[64,64]{1,0:T(8,128)S(1)}, u32[]{:S(2)}, u32[]{:S(2)}) %collective-permute-start.11) | collective-permute-done | bytes 16416 | tf_op jit(solution)/shard_map/ppermute | solution.py:295
  49.5 2.9 %collective-permute-done.12 = f32[64,64]{1,0:T(8,128)S(1)} collective-permute-done((f32[64,64]{1,0:T(8,128)S(1)}, f32[64,64]{1,0:T(8,128)S(1)}, u32[]{:S(2)}, u32[]{:S(2)}) %collective-permute-start.12) | collective-permute-done | bytes 16416 | tf_op jit(solution)/shard_map/ppermute | solution.py:295
  52.4 1.6 %collective-permute-start.13 = (f32[64,64]{1,0:T(8,128)S(1)}, f32[64,64]{1,0:T(8,128)S(1)}, u32[]{:S(2)}, u32[]{:S(2)}) collective-permute-start(f32[64,64]{1,0:T(8,128)S(1)} %add_add_fusion.1), channel_id=1, source_target_pairs={{0,2},{1,3},{2,0},{3,1},{4,6},{5,7},{6,4},{7,5},{8,10},{9,11},{10,... | collective-permute-start | bytes 49160 | tf_op jit(solution)/shard_map/ppermute | solution.py:295
  54.0 2.8 %collective-permute-start.15 = (f32[64,64]{1,0:T(8,128)S(1)}, f32[64,64]{1,0:T(8,128)S(1)}, u32[]{:S(2)}, u32[]{:S(2)}) collective-permute-start(f32[64,64]{1,0:T(8,128)S(1)} %add_add_fusion.1), channel_id=1, source_target_pairs={{0,6},{1,7},{2,4},{3,5},{4,2},{5,3},{6,0},{7,1},{8,14},{9,15},{10,... | collective-permute-start | bytes 49160 | tf_op jit(solution)/shard_map/ppermute | solution.py:295
  56.9 2.2 %collective-permute-done.14 = f32[64,64]{1,0:T(8,128)S(1)} collective-permute-done((f32[64,64]{1,0:T(8,128)S(1)}, f32[64,64]{1,0:T(8,128)S(1)}, u32[]{:S(2)}, u32[]{:S(2)}) %collective-permute-start.14) | collective-permute-done | bytes 16416 | tf_op jit(solution)/shard_map/ppermute | solution.py:295
  59.1 0.7 %collective-permute-done.15 = f32[64,64]{1,0:T(8,128)S(1)} collective-permute-done((f32[64,64]{1,0:T(8,128)S(1)}, f32[64,64]{1,0:T(8,128)S(1)}, u32[]{:S(2)}, u32[]{:S(2)}) %collective-permute-start.15) | collective-permute-done | bytes 16416 | tf_op jit(solution)/shard_map/ppermute | solution.py:295
  59.8 3.1 %orthonormalize.1 = (f32[64,4096]{1,0:T(8,128)}, f32[64,64]{1,0:T(8,128)}) custom-call(f32[64,64]{1,0:T(8,128)S(1)} %add_add_fusion.gram, bf16[128,4096]{1,0:T(8,128)(2,1)S(1)} %get-tuple-element.33.split), custom_call_target="tpu_custom_call" | custom-call | tf_op jit(solution)/shard_map/orthonormalize/pallas_call | solution.py:382
  (14 shorter events, 0.1 us)
Async XLA Ops:
  0.6 15.1 %collective-permute-start = (bf16[1,1,4096,64]{2,3,1,0:T(8,128)(2,1)}, bf16[1,1,4096,64]{2,3,1,0:T(8,128)(2,1)S(1)}, u32[]{:S(2)}, u32[]{:S(2)}) collective-permute-start(bf16[1,1,4096,64]{2,3,1,0:T(8,128)(2,1)} %param.4), channel_id=1, source_target_pairs={{0,1},{1,0},{2,3},{3,2},{4,5},{5,4},{6,7},{7,6},{8,9},{9,8},{10,11... | collective-permute-start | bytes 1572872 | tf_op jit(solution)/shard_map/ppermute | solution.py:23
  3.6 15.5 %collective-permute-start.1 = (bf16[1,1,4096,64]{2,3,1,0:T(8,128)(2,1)}, bf16[1,1,4096,64]{2,3,1,0:T(8,128)(2,1)S(1)}, u32[]{:S(2)}, u32[]{:S(2)}) collective-permute-start(bf16[1,1,4096,64]{2,3,1,0:T(8,128)(2,1)} %param.4), channel_id=1, source_target_pairs={{2,0},{4,2},{6,4},{1,3},{3,5},{5,7},{10,8},{12,10},{14,12},{9,11},... | collective-permute-start | bytes 1572872 | tf_op jit(solution)/shard_map/ppermute | solution.py:48
  4.9 14.2 %collective-permute-start.2 = (bf16[1,1,4096,64]{2,3,1,0:T(8,128)(2,1)}, bf16[1,1,4096,64]{2,3,1,0:T(8,128)(2,1)S(1)}, u32[]{:S(2)}, u32[]{:S(2)}) collective-permute-start(bf16[1,1,4096,64]{2,3,1,0:T(8,128)(2,1)} %param.4), channel_id=1, source_target_pairs={{8,16},{16,8},{9,17},{17,9},{10,18},{18,10},{11,19},{19,11},{12,20... | collective-permute-start | bytes 1572872 | tf_op jit(solution)/shard_map/ppermute | solution.py:27
  5.6 13.5 %collective-permute-start.3 = (bf16[1,1,4096,64]{2,3,1,0:T(8,128)(2,1)}, bf16[1,1,4096,64]{2,3,1,0:T(8,128)(2,1)S(1)}, u32[]{:S(2)}, u32[]{:S(2)}) collective-permute-start(bf16[1,1,4096,64]{2,3,1,0:T(8,128)(2,1)} %param.4), channel_id=1, source_target_pairs={{0,8},{8,0},{16,24},{24,16},{1,9},{9,1},{17,25},{25,17},{2,10},{10... | collective-permute-start | bytes 1572872 | tf_op jit(solution)/shard_map/ppermute | solution.py:23
  9.4 1.0 %copy-start = (bf16[1,1,4096,64]{2,3,1,0:T(8,128)(2,1)S(1)}, bf16[1,1,4096,64]{2,3,1,0:T(8,128)(2,1)}, u32[]{:S(2)}) copy-start(bf16[1,1,4096,64]{2,3,1,0:T(8,128)(2,1)} %param.4) | copy-start | bytes 1572868
  10.5 10.6 %copy-start.1 = (bf16[1,1,4096,64]{2,3,1,0:T(8,128)(2,1)S(1)}, bf16[1,1,4096,64]{2,3,1,0:T(8,128)(2,1)}, u32[]{:S(2)}) copy-start(bf16[1,1,4096,64]{2,3,1,0:T(8,128)(2,1)} %param.4) | copy-start | bytes 1572868
  19.1 1.9 %collective-permute-start.4 = (bf16[1,1,4096,64]{2,3,1,0:T(8,128)(2,1)S(1)}, bf16[1,1,4096,64]{2,3,1,0:T(8,128)(2,1)S(1)}, u32[]{:S(2)}, u32[]{:S(2)}) collective-permute-start(bf16[1,1,4096,64]{2,3,1,0:T(8,128)(2,1)S(1)} %collective-permute-done), channel_id=1, source_target_pairs={{0,8},{8,0},{16,24},{24,16},{1,9},{9,1},{17,25},{25,17},{2,10},{10... | collective-permute-start | bytes 1572872 | tf_op jit(solution)/shard_map/ppermute | solution.py:23
  19.1 13.8 %collective-permute-start.6 = (bf16[1,1,4096,64]{2,3,1,0:T(8,128)(2,1)S(1)}, bf16[1,1,4096,64]{2,3,1,0:T(8,128)(2,1)S(1)}, u32[]{:S(2)}, u32[]{:S(2)}) collective-permute-start(bf16[1,1,4096,64]{2,3,1,0:T(8,128)(2,1)S(1)} %collective-permute-done), channel_id=1, source_target_pairs={{8,16},{16,8},{9,17},{17,9},{10,18},{18,10},{11,19},{19,11},{12,20... | collective-permute-start | bytes 1572872 | tf_op jit(solution)/shard_map/ppermute | solution.py:27
  19.8 13.2 %collective-permute-start.7 = (bf16[1,1,4096,64]{2,3,1,0:T(8,128)(2,1)S(1)}, bf16[1,1,4096,64]{2,3,1,0:T(8,128)(2,1)S(1)}, u32[]{:S(2)}, u32[]{:S(2)}) collective-permute-start(bf16[1,1,4096,64]{2,3,1,0:T(8,128)(2,1)S(1)} %collective-permute-done), channel_id=1, source_target_pairs={{8,18},{10,20},{12,22},{11,17},{13,19},{15,21},{16,10},{18,12},{20... | collective-permute-start | bytes 1572872 | tf_op jit(solution)/shard_map/ppermute | solution.py:41
  20.5 12.5 %collective-permute-start.5 = (bf16[1,1,4096,64]{2,3,1,0:T(8,128)(2,1)S(1)}, bf16[1,1,4096,64]{2,3,1,0:T(8,128)(2,1)S(1)}, u32[]{:S(2)}, u32[]{:S(2)}) collective-permute-start(bf16[1,1,4096,64]{2,3,1,0:T(8,128)(2,1)S(1)} %collective-permute-done.1), channel_id=1, source_target_pairs={{0,1},{1,0},{2,3},{3,2},{4,5},{5,4},{6,7},{7,6},{8,9},{9,8},{10,11... | collective-permute-start | bytes 1572872 | tf_op jit(solution)/shard_map/ppermute | solution.py:23
  33.0 6.1 %collective-permute-start.8 = (bf16[1,1,4096,64]{2,3,1,0:T(8,128)(2,1)S(1)}, bf16[1,1,4096,64]{2,3,1,0:T(8,128)(2,1)S(1)}, u32[]{:S(2)}, u32[]{:S(2)}) collective-permute-start(bf16[1,1,4096,64]{2,3,1,0:T(8,128)(2,1)S(1)} %collective-permute-done.5), channel_id=1, source_target_pairs={{0,8},{8,0},{16,24},{24,16},{1,9},{9,1},{17,25},{25,17},{2,10},{10... | collective-permute-start | bytes 1572872 | tf_op jit(solution)/shard_map/ppermute | solution.py:23
  41.1 2.2 %collective-permute-start.9 = (f32[64,64]{1,0:T(8,128)S(1)}, f32[64,64]{1,0:T(8,128)S(1)}, u32[]{:S(2)}, u32[]{:S(2)}) collective-permute-start(f32[64,64]{1,0:T(8,128)S(1)} %get-tuple-element.32), channel_id=1, source_target_pairs={{0,8},{1,9},{2,10},{3,11},{4,12},{5,13},{6,14},{7,15},{8,0},{9,1},... | collective-permute-start | bytes 49160 | tf_op jit(solution)/shard_map/ppermute | solution.py:295
  43.4 4.5 %collective-permute-start.10 = (f32[64,64]{1,0:T(8,128)S(1)}, f32[64,64]{1,0:T(8,128)S(1)}, u32[]{:S(2)}, u32[]{:S(2)}) collective-permute-start(f32[64,64]{1,0:T(8,128)S(1)} %add.21), channel_id=1, source_target_pairs={{0,16},{1,17},{2,18},{3,19},{4,20},{5,21},{6,22},{7,23},{8,24},{9,... | collective-permute-start | bytes 49160 | tf_op jit(solution)/shard_map/ppermute | solution.py:295
  43.8 5.7 %collective-permute-start.11 = (f32[64,64]{1,0:T(8,128)S(1)}, f32[64,64]{1,0:T(8,128)S(1)}, u32[]{:S(2)}, u32[]{:S(2)}) collective-permute-start(f32[64,64]{1,0:T(8,128)S(1)} %add.21), channel_id=1, source_target_pairs={{0,1},{1,0},{2,3},{3,2},{4,5},{5,4},{6,7},{7,6},{8,9},{9,8},{10,11... | collective-permute-start | bytes 49160 | tf_op jit(solution)/shard_map/ppermute | solution.py:295
  47.6 4.8 %collective-permute-start.12 = (f32[64,64]{1,0:T(8,128)S(1)}, f32[64,64]{1,0:T(8,128)S(1)}, u32[]{:S(2)}, u32[]{:S(2)}) collective-permute-start(f32[64,64]{1,0:T(8,128)S(1)} %add.21), channel_id=1, source_target_pairs={{0,17},{1,16},{2,19},{3,18},{4,21},{5,20},{6,23},{7,22},{8,25},{9,... | collective-permute-start | bytes 49160 | tf_op jit(solution)/shard_map/ppermute | solution.py:295
  52.4 4.5 %collective-permute-start.13 = (f32[64,64]{1,0:T(8,128)S(1)}, f32[64,64]{1,0:T(8,128)S(1)}, u32[]{:S(2)}, u32[]{:S(2)}) collective-permute-start(f32[64,64]{1,0:T(8,128)S(1)} %add_add_fusion.1), channel_id=1, source_target_pairs={{0,2},{1,3},{2,0},{3,1},{4,6},{5,7},{6,4},{7,5},{8,10},{9,11},{10,... | collective-permute-start | bytes 49160 | tf_op jit(solution)/shard_map/ppermute | solution.py:295
  54.0 5.1 %collective-permute-start.14 = (f32[64,64]{1,0:T(8,128)S(1)}, f32[64,64]{1,0:T(8,128)S(1)}, u32[]{:S(2)}, u32[]{:S(2)}) collective-permute-start(f32[64,64]{1,0:T(8,128)S(1)} %add_add_fusion.1), channel_id=1, source_target_pairs={{0,4},{1,5},{2,6},{3,7},{4,0},{5,1},{6,2},{7,3},{8,12},{9,13},{10,... | collective-permute-start | bytes 49160 | tf_op jit(solution)/shard_map/ppermute | solution.py:295
  54.0 5.8 %collective-permute-start.15 = (f32[64,64]{1,0:T(8,128)S(1)}, f32[64,64]{1,0:T(8,128)S(1)}, u32[]{:S(2)}, u32[]{:S(2)}) collective-permute-start(f32[64,64]{1,0:T(8,128)S(1)} %add_add_fusion.1), channel_id=1, source_target_pairs={{0,6},{1,7},{2,4},{3,5},{4,2},{5,3},{6,0},{7,1},{8,14},{9,15},{10,... | collective-permute-start | bytes 49160 | tf_op jit(solution)/shard_map/ppermute | solution.py:295

commit v4 on v3

v4 whole, which is shorter than its diff:
```python
import functools

import jax
import jax.numpy as jnp
from jax import lax
from jax.experimental import pallas as pl
from jax.experimental.pallas import tpu as pltpu
from jax.sharding import PartitionSpec as P

UNROLL = 32
PARTS = 3
HALVES = 2
CHUNKS = 4
LIST_ROWS = 3
LINES = PARTS * HALVES * LIST_ROWS + 6
PART_OF = (0, 0, 0, 0, 0, 2, 1, 2, 1)
SLOT_OF = (0, 1, 2, 3, 4, 0, 0, 1, 1)
ROW_BY_ROW = (((1,), (1,)), ((), ()))
VMEM_LIMIT = 8 * 2**20


def pair_swap(value, axis):
    size = lax.axis_size(axis)
    return lax.ppermute(value, axis, [(i, i ^ 1) for i in range(size)])


def between_pairs(value, axis):
    return lax.ppermute(value, axis, outside(lax.axis_size(axis)))


def outside(size):
    return [(i, i + 1) for i in range(1, size - 1, 2)] + [(i + 1, i) for i in range(1, size - 1, 2)]


def across_both(value):
    gx_count, gy_count = lax.axis_size("gx"), lax.axis_size("gy")
    pairs = [
        (from_x * gy_count + (from_y ^ 1), to_x * gy_count + to_y)
        for from_x, to_x in outside(gx_count)
        for from_y, to_y in outside(gy_count)
    ]
    return lax.ppermute(value, ("gx", "gy"), pairs)


def two_back(value, axis):
    size = lax.axis_size(axis)
    pairs = [(i, i - 2) for i in range(2, size, 2)]
    pairs += [(i, i + 2) for i in range(1, size - 2, 2)]
    return lax.ppermute(value, axis, pairs)


def exact_log2(value):
    assert value & (value - 1) == 0
    return value.bit_length() - 1


def look_up(table, index):
    packed = sum(value << (3 * place) for place, value in enumerate(table))
    return lax.shift_right_logical(jnp.full(index.shape, packed, jnp.int32), 3 * index) & 7


def build_lists(links, work, tiles_dev, blocks, gy_count):
    own_x, own_y = lax.axis_index("gx"), lax.axis_index("gy")
    count = links.shape[0] * links.shape[2]
    tile_bits, gy_bits = exact_log2(tiles_dev), exact_log2(gy_count)
    link = jnp.concatenate([links[block] for block in range(blocks)], axis=1)
    order = lax.broadcasted_iota(jnp.int32, link.shape, 1)
    tile = order & (tiles_dev - 1)
    place = tile * blocks + lax.shift_right_logical(order, tile_bits)
    owner = lax.shift_right_logical(link, tile_bits)
    owner_x, owner_y = lax.shift_right_logical(owner, gy_bits), owner & (gy_count - 1)
    across = jnp.where(owner_x == own_x, 0, jnp.where(owner_x == (own_x ^ 1), 1, 2))
    own_row, beside = owner_y == own_y, owner_y == (own_y ^ 1)
    kind = across + jnp.where(own_row, 0, jnp.where(beside, 3, 6))
    part, slot = look_up(PART_OF, kind), look_up(SLOT_OF, kind)
    half = lax.shift_right_logical(tile, tile_bits - 1)
    code = (place - half * (count // HALVES)) * 512 + slot * tiles_dev + (link & (tiles_dev - 1)) + 1

    def ones_where(hit):
        return jnp.where(hit, 1.0, 0.0).astype(jnp.bfloat16)

    def iota(shape, dim):
        return lax.broadcasted_iota(jnp.int32, shape, dim)

    def dot(left, right):
        return jnp.dot(left, right, preferred_element_type=jnp.float32)

    def row_dot(left, right):
        return lax.dot_general(left, right, ROW_BY_ROW, preferred_element_type=jnp.float32)

    def to_even(length):
        return ((length.astype(jnp.int32) + 1) & -2).astype(jnp.float32).astype(jnp.bfloat16)

    groups, lines = PARTS * tiles_dev, LINES
    group = part * tiles_dev + tile
    in_group = iota((groups, count), 0) == group
    members = ones_where(in_group)
    before = dot(members, ones_where(iota((count, count), 0) < iota((count, count), 1)))
    lengths = dot(members, jnp.ones((count, 128), jnp.bfloat16))
    first, second = iota((groups, groups), 0), iota((groups, groups), 1)
    half_bits = tile_bits - 1
    same_list = lax.shift_right_logical(first, half_bits) == lax.shift_right_logical(second, half_bits)
    starts = dot(ones_where(same_list & (second < first)), to_even(lengths))
    rank = jnp.sum(jnp.where(in_group, before + starts[:, :1], 0.0), axis=0, keepdims=True).astype(jnp.int32)
    row = (part * HALVES + half) * LIST_ROWS + lax.shift_right_logical(rank, 7)
    column_hits = ones_where(iota((128, count), 0) == (rank & 127))
    row_hits = iota((lines, count), 0) == row
    listed = jnp.zeros((lines, 128), jnp.float32)
    for shift in (16, 8, 0):
        digit = (lax.shift_right_logical(code, shift) & 255).astype(jnp.float32)
        listed = listed * 256.0 + row_dot(jnp.where(row_hits, digit, 0.0).astype(jnp.bfloat16), column_hits)
    by_group = to_even(row_dot(jnp.ones((lines, count), jnp.bfloat16), members))
    of_list = iota((128, groups), 0) == lax.shift_right_logical(iota((128, groups), 1), half_bits)
    totals = row_dot(by_group, ones_where(of_list))
    work[...] = jnp.where(iota((lines, 128), 0) == lines - 1, totals, listed).astype(jnp.int32)


def lay_out(sources, rows, tiles_dev):
    width = rows.shape[-1]
    rows[0] = jnp.zeros(rows.shape[1:], rows.dtype)
    for slot, source in enumerate(sources):
        for tile in range(tiles_dev):
            rows[1 + slot * tiles_dev + tile] = source[:, tile * width:(tile + 1) * width]


def batches(part, half, work):
    return lax.div(work[LINES - 1, part * HALVES + half] + (UNROLL - 1), UNROLL)


def products_of(part, half, work, index, near, acc, rows):
    tiles_half = acc.shape[0] // HALVES
    blocks = near.shape[0] // tiles_half
    groups = 128 // UNROLL
    line = (part * HALVES + half) * LIST_ROWS + lax.div(index, groups)
    begin = lax.rem(index, groups) * UNROLL
    products = []
    for lane in range(0, UNROLL, 2):
        codes = [work[line, begin + lane + i] for i in range(2)]
        entries = [lax.shift_right_logical(code, 9) for code in codes]
        left = jnp.concatenate([near[entry] for entry in entries], axis=1)
        right = jnp.concatenate([rows[code & 511] for code in codes], axis=1)
        product = lax.dot_general(left, right, ROW_BY_ROW, preferred_element_type=jnp.float32)
        products.append((lax.div(entries[0], blocks) + half * tiles_half, product))
    return products


def add_all(products, acc):
    for target, product in products:
        acc[target] += product


def add_both(part, work, nears, acc, rows):
    def step(index, carry):
        products = []
        for half, near in enumerate(nears):
            products += products_of(part, half, work, index, near, acc, rows)
        add_all(products, acc)
        return carry

    longest = jnp.maximum(*(batches(part, half, work) for half in range(HALVES)))
    lax.fori_loop(0, longest, step, 0)


def loads_of(half, near_hbm, near, sems):
    chunks = sems.shape[1]
    length = near.shape[0] // chunks
    return [
        pltpu.make_async_copy(
            near_hbm.at[pl.ds(half * near.shape[0] + chunk * length, length)],
            near.at[pl.ds(chunk * length, length)],
            sems.at[half, chunk],
        )
        for chunk in range(chunks)
    ]


def load_kernel(tiles_dev, gy_count, links, near_hbm, near_0, near_1, work, sems):
    loads = [load for half, near in enumerate((near_0, near_1)) for load in loads_of(half, near_hbm, near, sems)]
    for load in loads:
        load.start()
    build_lists(links, work, tiles_dev, near_hbm.shape[0] // tiles_dev, gy_count)
    for load in loads:
        load.wait()


def early_kernel(work_in, near_0, near_1, *refs):
    acc, rows, work, sem = refs[-4:]
    copy = pltpu.make_async_copy(work_in, work, sem)
    copy.start()
    lay_out(refs[:-4], rows, acc.shape[0])
    acc[...] = jnp.zeros(acc.shape, acc.dtype)
    copy.wait()
    add_both(0, work, (near_0, near_1), acc, rows)


def next_kernel(work_in, near_0, near_1, *refs):
    acc, rows, work, sem = refs[-4:]
    copy = pltpu.make_async_copy(work_in, work, sem)
    copy.start()
    lay_out(refs[:-5], rows, acc.shape[0])
    copy.wait()
    add_both(1, work, (near_0, near_1), acc, rows)


def last_kernel(work_in, near_0, near_1, outer, core, acc_in, split, gram, acc, rows, work, sem):
    tiles_dev, width, columns = acc.shape
    copy = pltpu.make_async_copy(work_in, work, sem)
    copy.start()
    lay_out((outer, core), rows, tiles_dev)
    copy.wait()
    add_both(2, work, (near_0, near_1), acc, rows)
    for tile in range(tiles_dev):
        image = acc[tile].T
        high = image.astype(jnp.bfloat16)
        low = (image - high.astype(jnp.float32)).astype(jnp.bfloat16)
        split[:, tile * width:(tile + 1) * width] = jnp.concatenate([high, low], axis=0)
    both = split[...]
    full = lax.dot_general(both, both, ROW_BY_ROW, preferred_element_type=jnp.float32)
    top = full[:columns, :columns] + full[columns:, columns:]
    side = full[:columns, columns:] + full[columns:, :columns]
    total = top + side
    gram[...] = jnp.concatenate([total[:columns // 2], total[columns // 2:]], axis=1)


def finish_kernel(scale, gram, split, basis, factor):
    columns = 2 * gram.shape[0]
    shape = (8, 2 * columns)
    row = lax.broadcasted_iota(jnp.int32, shape, 0)
    lane = lax.broadcasted_iota(jnp.int32, shape, 1)
    groups = columns // 8
    live = []
    for g in range(groups):
        unit = jnp.where(lane == row + (columns + 8 * g), 1.0, 0.0)
        begin, side = 8 * g % (columns // 2), 8 * g // (columns // 2) * columns
        live.append(jnp.concatenate([gram[begin:begin + 8, side:side + columns], unit[:, columns:]], axis=1))
    done = []
    for g in range(groups):
        cols = [[jnp.broadcast_to(part[:, 8 * g + j:8 * g + j + 1], shape) for part in live] for j in range(8)]
        pivots = jnp.ones(shape, jnp.float32)
        for j in range(8):
            pivot = jnp.broadcast_to(cols[j][0][j:j+1], shape)
            pivots = jnp.where(row == j, pivot, pivots)
            inverse = 1.0 / pivot
            ratios = [part * inverse for part in cols[j]]
            ratios[0] = jnp.where(row > j, ratios[0], 0.0)
            for i in range(j + 1, 8):
                pick = jnp.broadcast_to(cols[i][0][j:j+1], shape)
                cols[i] = [part - ratio * pick for part, ratio in zip(cols[i], ratios)]
            pick = jnp.broadcast_to(live[0][j:j+1], shape)
            live = [part - ratio * pick for part, ratio in zip(live, ratios)]
        done.append(live[0] * lax.rsqrt(pivots))
        live = live[1:]
    whole = jnp.concatenate(done, axis=0)
    left, right = whole[:, :columns], whole[:, columns:]
    on_or_above = lax.broadcasted_iota(jnp.int32, left.shape, 0) <= lax.broadcasted_iota(jnp.int32, left.shape, 1)
    factor[...] = jnp.where(on_or_above, left, 0.0) * (1.0 / scale)
    weight = right * scale
    high = weight.astype(jnp.bfloat16)
    low = (weight - high.astype(jnp.float32)).astype(jnp.bfloat16)
    stacked = jnp.concatenate([high, high, low], axis=1)
    values = jnp.concatenate([split[...], split[:columns]], axis=0)
    basis[...] = jnp.dot(stacked, values, preferred_element_type=jnp.float32)


def in_vmem():
    return pl.BlockSpec(memory_space=pltpu.VMEM)


def sum_over_all(value):
    gx_count, gy_count = lax.axis_size("gx"), lax.axis_size("gy")
    total = gx_count * gy_count
    bits = [gy_count * 2**i for i in range(1, gx_count.bit_length() - 1)]
    bits = bits[:1] + [2**i for i in range(gy_count.bit_length() - 1)] + bits[1:]

    def from_other(mask):
        return lax.ppermute(value, ("gx", "gy"), [(i, i ^ mask) for i in range(total)])

    value = value + from_other(gy_count)
    while bits:
        taken, bits = bits[:2], bits[2:]
        near = value + from_other(taken[0])
        if len(taken) == 2:
            near = near + (from_other(taken[1]) + from_other(taken[0] ^ taken[1]))
        value = near
    return value


def shards(near_tiles, block, adjacency):
    tiles_dev, blocks = adjacency.shape[2:]
    width = near_tiles.shape[4]
    rows, columns = block.shape[2:]
    gx_count, gy_count = lax.axis_size("gx"), lax.axis_size("gy")
    scale = float(rows * gx_count * gy_count) ** 0.5

    beside = pair_swap(block, "gy")
    two_off = two_back(block, "gy")
    outer = between_pairs(block, "gx")
    core = pair_swap(block, "gx")

    count = tiles_dev * blocks
    links = adjacency[0, 0].T.reshape(blocks, 1, tiles_dev)
    near = near_tiles.reshape(count, width, width)
    acc_shape = jax.ShapeDtypeStruct((tiles_dev, width, columns), jnp.float32)
    flat = lambda value: value[0, 0].T

    def tile_rows(sources):
        return pltpu.VMEM((sources * tiles_dev + 1, columns, width), jnp.bfloat16)

    def params(limit=VMEM_LIMIT):
        return dict(
            compiler_params=pltpu.CompilerParams(vmem_limit_bytes=limit),
        )

    work_scratch = [pltpu.SMEM((LINES, 128), jnp.int32), pltpu.SemaphoreType.DMA]
    near_half = pltpu.VMEM((count // HALVES, width, width), near.dtype)
    near_0, near_1, work = pl.pallas_call(
        functools.partial(load_kernel, tiles_dev, gy_count),
        out_shape=(near_half, near_half, jax.ShapeDtypeStruct((LINES, 128), jnp.int32)),
        in_specs=[in_vmem(), pl.BlockSpec(memory_space=pltpu.HBM)], out_specs=(in_vmem(),) * 3,
        scratch_shapes=[pltpu.SemaphoreType.DMA((HALVES, CHUNKS))], name="load", **params(24 * 2**20),
    )(links, near)

    beside, two_off, work = lax.optimization_barrier((beside, two_off, work))
    beyond = pair_swap(two_off, "gy")
    beside_outer = between_pairs(beside, "gx")
    beyond_outer = across_both(beside)
    beside_core = pair_swap(beside, "gx")
    sources = (block, core, outer, beside, beside_core)
    acc = pl.pallas_call(
        early_kernel, out_shape=acc_shape, in_specs=[in_vmem()] * 8, out_specs=in_vmem(),
        scratch_shapes=[tile_rows(5)] + work_scratch, name="early_rows", **params(),
    )(work, near_0, near_1, *(flat(source) for source in sources))

    beyond, beyond_outer, acc = lax.optimization_barrier((beyond, beyond_outer, acc))
    beyond_core = pair_swap(beyond, "gx")
    acc = pl.pallas_call(
        next_kernel, out_shape=acc_shape, in_specs=[in_vmem()] * 6, out_specs=in_vmem(),
        scratch_shapes=[tile_rows(2)] + work_scratch, name="next_rows", input_output_aliases={5: 0}, **params(),
    )(work, near_0, near_1, flat(beyond), flat(beyond_outer), acc)

    beside_outer, beyond_core, acc = lax.optimization_barrier((beside_outer, beyond_core, acc))
    split, gram, _ = pl.pallas_call(
        last_kernel,
        out_shape=(
            jax.ShapeDtypeStruct((2 * columns, rows), jnp.bfloat16),
            jax.ShapeDtypeStruct((columns // 2, 2 * columns), jnp.float32),
            acc_shape,
        ),
        in_specs=[in_vmem()] * 6, out_specs=(in_vmem(),) * 3,
        scratch_shapes=[tile_rows(2)] + work_scratch, name="last_rows_and_gram", input_output_aliases={5: 2}, **params(),
    )(work, near_0, near_1, flat(beside_outer), flat(beyond_core), acc)

    gram = sum_over_all(gram)
    basis, factor = pl.pallas_call(
        functools.partial(finish_kernel, scale),
        out_shape=(
            jax.ShapeDtypeStruct((columns, rows), jnp.float32),
            jax.ShapeDtypeStruct((columns, columns), jnp.float32),
        ),
        in_specs=[in_vmem()] * 2, out_specs=(in_vmem(), in_vmem()), name="orthonormalize", **params(),
    )(gram, split)
    return basis.T.reshape(1, 1, rows, columns), factor


def solution(mesh):
    in_specs = (
        P("gx", "gy", None, None, None, None),
        P("gx", "gy", None, None),
        P("gx", "gy", None, None),
    )
    out_specs = (P("gx", "gy", None, None), P())
    return jax.shard_map(shards, mesh=mesh, in_specs=in_specs, out_specs=out_specs, check_vma=False)
```

time: 63.6 us -> 60.2 us (0.947)
  Pallas kernels: 22.6 us -> 21 us
  waiting for transfers between devices: 13.5 us -> 12.1 us
  local copies, waits for them, and re-layouts: 1.92 us -> 0.72 us
  starting transfers between devices: 24.2 us -> 25.4 us
    ppermute x1, waiting for transfers between devices: 3.34 us -> 0.01 us  [two_back(): return lax.ppermute(value, axis, pairs)]
    ppermute x5, waiting for transfers between devices: 1.79 us -> 4.22 us  [pair_swap(): return lax.ppermute(value, axis, [(i, i ^ 1) for i in range(size)])]
    ppermute x5, starting transfers between devices: 10.5 us -> 12.2 us  [pair_swap(): return lax.ppermute(value, axis, [(i, i ^ 1) for i in range(size)])]
    pallas_call x3, Pallas kernels: 17.4 us -> 16 us  [the longest x1 8.01 us: shards(): pl.pallas_call(early_kernel, out_shape=acc_shape, in_specs=[in_vmem()] *...]
    unnamed x5 -> x3, local copies, waits for them, and re-layouts: 1.82 us -> 0.71 us
  transfers between devices with their start and end apart: 16 -> 16, of which waited for: 9 -> 9; matrix products, arithmetic and copies ran while one was open for 1% -> 1% of each run, Pallas kernels for 28% -> 27%
where the time goes in v4:
time: 60.2 us; the launch traced here: 59.9 us
  starting transfers between devices  25.4 us (42%)
  Pallas kernels  21 us (35%)
  waiting for transfers between devices  12.1 us (20%)
  between operations  0.77 us (1%)
  local copies, waits for them, and re-layouts  0.72 us (1%)
    ppermute x5, starting transfers between devices, pair_swap(): return lax.ppermute(value, axis, [(i, i ^ 1) for i in range(size)])  12.2 us
    ppermute x7, starting transfers between devices, from_other(): lax.ppermute(value, ('gx', 'gy'), [(i, i ^ mask) for i in range(total)])  9.83 us
    pallas_call x1, Pallas kernels, shards(): pl.pallas_call(early_kernel, out_shape=acc_shape, in_specs=[in_vmem()] *...  8.01 us
    ppermute x7, waiting for transfers between devices, from_other(): lax.ppermute(value, ('gx', 'gy'), [(i, i ^ mask) for i in range(total)])  7.83 us
    pallas_call x1, Pallas kernels, shards(): pl.pallas_call(functools.partial(load_kernel, tiles_dev, gy_count), out_s...  7.19 us
    ppermute x5, waiting for transfers between devices, pair_swap(): return lax.ppermute(value, axis, [(i, i ^ 1) for i in range(size)])  4.22 us
    pallas_call x1, Pallas kernels, shards(): pl.pallas_call(functools.partial(finish_kernel, scale), out_shape=(jax.Sh...  3.15 us
    pallas_call x1, Pallas kernels, shards(): pl.pallas_call(last_kernel, out_shape=(jax.ShapeDtypeStruct((2 * columns,...  1.85 us
  transfers between devices with their start and end apart: 16, of which 9 were waited for; matrix products, arithmetic and copies ran while one was open for 1% of the time, Pallas kernels for 27%

profile of v4, /device:TPU:0, one launch (start us, length us, event | category | flops | bytes accessed | tf_op | source)
XLA Modules:
  0.0 59.9 jit_solution(13444029759350764025)
XLA Ops:
  0.6 1.3 %collective-permute-start.1 = (bf16[1,1,4096,64]{2,3,1,0:T(8,128)(2,1)}, bf16[1,1,4096,64]{2,3,1,0:T(8,128)(2,1)S(1)}, u32[]{:S(2)}, u32[]{:S(2)}) collective-permute-start(bf16[1,1,4096,64]{2,3,1,0:T(8,128)(2,1)} %param.4), channel_id=1, source_target_pairs={{2,0},{4,2},{6,4},{1,3},{3,5},{5,7},{10,8},{12,10},{14,12},{9,11},... | collective-permute-start | bytes 1572872 | tf_op jit(solution)/shard_map/ppermute | solution.py:49
  1.9 5.2 %collective-permute-start = (bf16[1,1,4096,64]{2,3,1,0:T(8,128)(2,1)}, bf16[1,1,4096,64]{2,3,1,0:T(8,128)(2,1)S(1)}, u32[]{:S(2)}, u32[]{:S(2)}) collective-permute-start(bf16[1,1,4096,64]{2,3,1,0:T(8,128)(2,1)} %param.4), channel_id=1, source_target_pairs={{0,1},{1,0},{2,3},{3,2},{4,5},{5,4},{6,7},{7,6},{8,9},{9,8},{10,11... | collective-permute-start | bytes 1572872 | tf_op jit(solution)/shard_map/ppermute | solution.py:24
  7.2 0.7 %collective-permute-start.6 = (bf16[1,1,4096,64]{2,3,1,0:T(8,128)(2,1)}, bf16[1,1,4096,64]{2,3,1,0:T(8,128)(2,1)S(1)}, u32[]{:S(2)}, u32[]{:S(2)}) collective-permute-start(bf16[1,1,4096,64]{2,3,1,0:T(8,128)(2,1)} %param.4), channel_id=1, source_target_pairs={{8,16},{16,8},{9,17},{17,9},{10,18},{18,10},{11,19},{19,11},{12,20... | collective-permute-start | bytes 1572872 | tf_op jit(solution)/shard_map/ppermute | solution.py:28
  7.8 2.9 %collective-permute-start.5 = (bf16[1,1,4096,64]{2,3,1,0:T(8,128)(2,1)}, bf16[1,1,4096,64]{2,3,1,0:T(8,128)(2,1)S(1)}, u32[]{:S(2)}, u32[]{:S(2)}) collective-permute-start(bf16[1,1,4096,64]{2,3,1,0:T(8,128)(2,1)} %param.4), channel_id=1, source_target_pairs={{0,8},{8,0},{16,24},{24,16},{1,9},{9,1},{17,25},{25,17},{2,10},{10... | collective-permute-start | bytes 1572872 | tf_op jit(solution)/shard_map/ppermute | solution.py:24
  10.8 0.7 %copy.9 = s32[1,1,32,20]{2,3,1,0:T(8,128)S(1)} copy(s32[1,1,32,20]{2,1,3,0:T(1,128)} %param.5) | data formatting | bytes 5120
  11.5 0.0 copy-start
  11.5 7.2 %load.1 = (bf16[320,128,128]{2,1,0:T(8,128)(2,1)S(1)}, bf16[320,128,128]{2,1,0:T(8,128)(2,1)S(1)}, s32[24,128]{1,0:T(8,128)S(1)}) custom-call(s32[20,1,32]{2,1,0:T(1,128)S(1)} %reshape.13.links, bf16[640,128,128]{2,1,0:T(8,128)(2,1)} %bitcast.45), custom_call_target="tpu_custom_call" | custom-call | tf_op jit(solution)/shard_map/load/pallas_call | solution.py:316
  18.7 0.3 collective-permute-done
  19.0 1.7 %collective-permute-start.3 = (bf16[1,1,4096,64]{2,3,1,0:T(8,128)(2,1)S(1)}, bf16[1,1,4096,64]{2,3,1,0:T(8,128)(2,1)S(1)}, u32[]{:S(2)}, u32[]{:S(2)}) collective-permute-start(bf16[1,1,4096,64]{2,3,1,0:T(8,128)(2,1)S(1)} %collective-permute-done.1), channel_id=1, source_target_pairs={{0,1},{1,0},{2,3},{3,2},{4,5},{5,4},{6,7},{7,6},{8,9},{9,8},{10,11... | collective-permute-start | bytes 1572872 | tf_op jit(solution)/shard_map/ppermute | solution.py:24
  20.8 0.7 %collective-permute-start.4 = (bf16[1,1,4096,64]{2,3,1,0:T(8,128)(2,1)S(1)}, bf16[1,1,4096,64]{2,3,1,0:T(8,128)(2,1)S(1)}, u32[]{:S(2)}, u32[]{:S(2)}) collective-permute-start(bf16[1,1,4096,64]{2,3,1,0:T(8,128)(2,1)S(1)} %collective-permute-done), channel_id=1, source_target_pairs={{8,18},{10,20},{12,22},{11,17},{13,19},{15,21},{16,10},{18,12},{20... | collective-permute-start | bytes 1572872 | tf_op jit(solution)/shard_map/ppermute | solution.py:42
  21.4 0.0 collective-permute-done.6
  21.5 0.7 %collective-permute-start.2 = (bf16[1,1,4096,64]{2,3,1,0:T(8,128)(2,1)S(1)}, bf16[1,1,4096,64]{2,3,1,0:T(8,128)(2,1)S(1)}, u32[]{:S(2)}, u32[]{:S(2)}) collective-permute-start(bf16[1,1,4096,64]{2,3,1,0:T(8,128)(2,1)S(1)} %collective-permute-done), channel_id=1, source_target_pairs={{8,16},{16,8},{9,17},{17,9},{10,18},{18,10},{11,19},{19,11},{12,20... | collective-permute-start | bytes 1572872 | tf_op jit(solution)/shard_map/ppermute | solution.py:28
  22.2 8.0 %early_rows.1.refs_2_ = f32[32,128,64]{2,1,0:T(8,128)S(1)} custom-call(s32[24,128]{1,0:T(8,128)S(1)} %get-tuple-element.19.work_in, bf16[320,128,128]{2,1,0:T(8,128)(2,1)S(1)} %get-tuple-element.20.near_0, bf16[320,128,128]{2,1,0:T(8,128)(2,1)S(1)} %get-tuple-element.21.near_1, bf16[64,4096]{1,0:T(8,128)(2,1)S(1)} %bitcast.36, ...), custom_call_target="tpu_custom_call" | custom-call | tf_op jit(solution)/shard_map/early_rows/pallas_call | solution.py:329
  30.2 3.1 %collective-permute-done.3 = bf16[1,1,4096,64]{2,3,1,0:T(8,128)(2,1)S(1)} collective-permute-done((bf16[1,1,4096,64]{2,3,1,0:T(8,128)(2,1)S(1)}, bf16[1,1,4096,64]{2,3,1,0:T(8,128)(2,1)S(1)}, u32[]{:S(2)}, u32[]{:S(2)}) %collective-permute-start.3) | collective-permute-done | bytes 524320 | tf_op jit(solution)/shard_map/ppermute | solution.py:24
  33.4 2.4 %collective-permute-start.8 = (bf16[1,1,4096,64]{2,3,1,0:T(8,128)(2,1)S(1)}, bf16[1,1,4096,64]{2,3,1,0:T(8,128)(2,1)S(1)}, u32[]{:S(2)}, u32[]{:S(2)}) collective-permute-start(bf16[1,1,4096,64]{2,3,1,0:T(8,128)(2,1)S(1)} %collective-permute-done.3), channel_id=1, source_target_pairs={{0,8},{8,0},{16,24},{24,16},{1,9},{9,1},{17,25},{25,17},{2,10},{10... | collective-permute-start | bytes 1572872 | tf_op jit(solution)/shard_map/ppermute | solution.py:24
  35.7 0.8 %next_rows.1.acc_in = f32[32,128,64]{2,1,0:T(8,128)S(1)} custom-call(s32[24,128]{1,0:T(8,128)S(1)} %get-tuple-element.19.work_in, bf16[320,128,128]{2,1,0:T(8,128)(2,1)S(1)} %get-tuple-element.20.near_0, bf16[320,128,128]{2,1,0:T(8,128)(2,1)S(1)} %get-tuple-element.21.near_1, bf16[64,4096]{1,0:T(8,128)(2,1)S(1)} %bitcast.40, ...), custom_call_target="tpu_custom_call", output_to_operand_aliasing={{}: (5, {})} | custom-call | tf_op jit(solution)/shard_map/next_rows/pallas_call | solution.py:336
  36.5 0.8 %collective-permute-done.8 = bf16[1,1,4096,64]{2,3,1,0:T(8,128)(2,1)S(1)} collective-permute-done((bf16[1,1,4096,64]{2,3,1,0:T(8,128)(2,1)S(1)}, bf16[1,1,4096,64]{2,3,1,0:T(8,128)(2,1)S(1)}, u32[]{:S(2)}, u32[]{:S(2)}) %collective-permute-start.8) | collective-permute-done | bytes 524320 | tf_op jit(solution)/shard_map/ppermute | solution.py:24
  37.2 1.9 %last_rows_and_gram.1 = (bf16[128,4096]{1,0:T(8,128)(2,1)S(1)}, f32[32,128]{1,0:T(8,128)S(1)}, f32[32,128,64]{2,1,0:T(8,128)S(1)}) custom-call(s32[24,128]{1,0:T(8,128)S(1)} %get-tuple-element.19.work_in, bf16[320,128,128]{2,1,0:T(8,128)(2,1)S(1)} %get-tuple-element.20.near_0, ...), custom_call_target="tpu_custom_call", output_to_operand_aliasing={{2}: (5, {})} | custom-call | tf_op jit(solution)/shard_map/last_rows_and_gram/pallas_call | solution.py:342
  39.1 1.9 %collective-permute-start.9 = (f32[32,128]{1,0:T(8,128)S(1)}, f32[32,128]{1,0:T(8,128)S(1)}, u32[]{:S(2)}, u32[]{:S(2)}) collective-permute-start(f32[32,128]{1,0:T(8,128)S(1)} %get-tuple-element.30), channel_id=1, source_target_pairs={{0,8},{1,9},{2,10},{3,11},{4,12},{5,13},{6,14},{7,15},{8,0},{9,1},... | collective-permute-start | bytes 49160 | tf_op jit(solution)/shard_map/ppermute | solution.py:276
  41.0 0.8 %collective-permute-done.9 = f32[32,128]{1,0:T(8,128)S(1)} collective-permute-done((f32[32,128]{1,0:T(8,128)S(1)}, f32[32,128]{1,0:T(8,128)S(1)}, u32[]{:S(2)}, u32[]{:S(2)}) %collective-permute-start.9) | collective-permute-done | bytes 16416 | tf_op jit(solution)/shard_map/ppermute | solution.py:276
  41.8 2.5 %collective-permute-start.12 = (f32[32,128]{1,0:T(8,128)S(1)}, f32[32,128]{1,0:T(8,128)S(1)}, u32[]{:S(2)}, u32[]{:S(2)}) collective-permute-start(f32[32,128]{1,0:T(8,128)S(1)} %add.21), channel_id=1, source_target_pairs={{0,17},{1,16},{2,19},{3,18},{4,21},{5,20},{6,23},{7,22},{8,25},{9,... | collective-permute-start | bytes 49160 | tf_op jit(solution)/shard_map/ppermute | solution.py:276
  44.3 0.6 %collective-permute-start.11 = (f32[32,128]{1,0:T(8,128)S(1)}, f32[32,128]{1,0:T(8,128)S(1)}, u32[]{:S(2)}, u32[]{:S(2)}) collective-permute-start(f32[32,128]{1,0:T(8,128)S(1)} %add.21), channel_id=1, source_target_pairs={{0,1},{1,0},{2,3},{3,2},{4,5},{5,4},{6,7},{7,6},{8,9},{9,8},{10,11... | collective-permute-start | bytes 49160 | tf_op jit(solution)/shard_map/ppermute | solution.py:276
  44.9 0.4 collective-permute-start.10
  45.3 1.1 %collective-permute-done.12 = f32[32,128]{1,0:T(8,128)S(1)} collective-permute-done((f32[32,128]{1,0:T(8,128)S(1)}, f32[32,128]{1,0:T(8,128)S(1)}, u32[]{:S(2)}, u32[]{:S(2)}) %collective-permute-start.12) | collective-permute-done | bytes 16416 | tf_op jit(solution)/shard_map/ppermute | solution.py:276
  46.5 1.6 %collective-permute-done.11 = f32[32,128]{1,0:T(8,128)S(1)} collective-permute-done((f32[32,128]{1,0:T(8,128)S(1)}, f32[32,128]{1,0:T(8,128)S(1)}, u32[]{:S(2)}, u32[]{:S(2)}) %collective-permute-start.11) | collective-permute-done | bytes 16416 | tf_op jit(solution)/shard_map/ppermute | solution.py:276
  48.1 0.6 %collective-permute-done.10 = f32[32,128]{1,0:T(8,128)S(1)} collective-permute-done((f32[32,128]{1,0:T(8,128)S(1)}, f32[32,128]{1,0:T(8,128)S(1)}, u32[]{:S(2)}, u32[]{:S(2)}) %collective-permute-start.10) | collective-permute-done | bytes 16416 | tf_op jit(solution)/shard_map/ppermute | solution.py:276
  48.7 3.4 %collective-permute-start.15 = (f32[32,128]{1,0:T(8,128)S(1)}, f32[32,128]{1,0:T(8,128)S(1)}, u32[]{:S(2)}, u32[]{:S(2)}) collective-permute-start(f32[32,128]{1,0:T(8,128)S(1)} %add_add_fusion.1), channel_id=1, source_target_pairs={{0,6},{1,7},{2,4},{3,5},{4,2},{5,3},{6,0},{7,1},{8,14},{9,15},{10,... | collective-permute-start | bytes 49160 | tf_op jit(solution)/shard_map/ppermute | solution.py:276
  52.0 0.8 %collective-permute-start.14 = (f32[32,128]{1,0:T(8,128)S(1)}, f32[32,128]{1,0:T(8,128)S(1)}, u32[]{:S(2)}, u32[]{:S(2)}) collective-permute-start(f32[32,128]{1,0:T(8,128)S(1)} %add_add_fusion.1), channel_id=1, source_target_pairs={{0,4},{1,5},{2,6},{3,7},{4,0},{5,1},{6,2},{7,3},{8,12},{9,13},{10,... | collective-permute-start | bytes 49160 | tf_op jit(solution)/shard_map/ppermute | solution.py:276
  52.9 0.3 collective-permute-start.13
  53.1 1.3 %collective-permute-done.15 = f32[32,128]{1,0:T(8,128)S(1)} collective-permute-done((f32[32,128]{1,0:T(8,128)S(1)}, f32[32,128]{1,0:T(8,128)S(1)}, u32[]{:S(2)}, u32[]{:S(2)}) %collective-permute-start.15) | collective-permute-done | bytes 16416 | tf_op jit(solution)/shard_map/ppermute | solution.py:276
  54.4 2.3 %collective-permute-done.14 = f32[32,128]{1,0:T(8,128)S(1)} collective-permute-done((f32[32,128]{1,0:T(8,128)S(1)}, f32[32,128]{1,0:T(8,128)S(1)}, u32[]{:S(2)}, u32[]{:S(2)}) %collective-permute-start.14) | collective-permute-done | bytes 16416 | tf_op jit(solution)/shard_map/ppermute | solution.py:276
  56.8 3.1 %orthonormalize.1 = (f32[64,4096]{1,0:T(8,128)}, f32[64,64]{1,0:T(8,128)}) custom-call(f32[32,128]{1,0:T(8,128)S(1)} %add_add_fusion.gram, bf16[128,4096]{1,0:T(8,128)(2,1)S(1)} %get-tuple-element.31.split), custom_call_target="tpu_custom_call" | custom-call | tf_op jit(solution)/shard_map/orthonormalize/pallas_call | solution.py:354
  (12 shorter events, 0.0 us)
Async XLA Ops:
  0.6 18.1 %collective-permute-start.1 = (bf16[1,1,4096,64]{2,3,1,0:T(8,128)(2,1)}, bf16[1,1,4096,64]{2,3,1,0:T(8,128)(2,1)S(1)}, u32[]{:S(2)}, u32[]{:S(2)}) collective-permute-start(bf16[1,1,4096,64]{2,3,1,0:T(8,128)(2,1)} %param.4), channel_id=1, source_target_pairs={{2,0},{4,2},{6,4},{1,3},{3,5},{5,7},{10,8},{12,10},{14,12},{9,11},... | collective-permute-start | bytes 1572872 | tf_op jit(solution)/shard_map/ppermute | solution.py:49
  1.9 17.1 %collective-permute-start = (bf16[1,1,4096,64]{2,3,1,0:T(8,128)(2,1)}, bf16[1,1,4096,64]{2,3,1,0:T(8,128)(2,1)S(1)}, u32[]{:S(2)}, u32[]{:S(2)}) collective-permute-start(bf16[1,1,4096,64]{2,3,1,0:T(8,128)(2,1)} %param.4), channel_id=1, source_target_pairs={{0,1},{1,0},{2,3},{3,2},{4,5},{5,4},{6,7},{7,6},{8,9},{9,8},{10,11... | collective-permute-start | bytes 1572872 | tf_op jit(solution)/shard_map/ppermute | solution.py:24
  7.2 14.3 %collective-permute-start.6 = (bf16[1,1,4096,64]{2,3,1,0:T(8,128)(2,1)}, bf16[1,1,4096,64]{2,3,1,0:T(8,128)(2,1)S(1)}, u32[]{:S(2)}, u32[]{:S(2)}) collective-permute-start(bf16[1,1,4096,64]{2,3,1,0:T(8,128)(2,1)} %param.4), channel_id=1, source_target_pairs={{8,16},{16,8},{9,17},{17,9},{10,18},{18,10},{11,19},{19,11},{12,20... | collective-permute-start | bytes 1572872 | tf_op jit(solution)/shard_map/ppermute | solution.py:28
  7.8 14.3 %collective-permute-start.5 = (bf16[1,1,4096,64]{2,3,1,0:T(8,128)(2,1)}, bf16[1,1,4096,64]{2,3,1,0:T(8,128)(2,1)S(1)}, u32[]{:S(2)}, u32[]{:S(2)}) collective-permute-start(bf16[1,1,4096,64]{2,3,1,0:T(8,128)(2,1)} %param.4), channel_id=1, source_target_pairs={{0,8},{8,0},{16,24},{24,16},{1,9},{9,1},{17,25},{25,17},{2,10},{10... | collective-permute-start | bytes 1572872 | tf_op jit(solution)/shard_map/ppermute | solution.py:24
  11.5 10.7 %copy-start = (bf16[1,1,4096,64]{2,3,1,0:T(8,128)(2,1)S(1)}, bf16[1,1,4096,64]{2,3,1,0:T(8,128)(2,1)}, u32[]{:S(2)}) copy-start(bf16[1,1,4096,64]{2,3,1,0:T(8,128)(2,1)} %param.4) | copy-start | bytes 1572868
  19.0 3.2 %collective-permute-start.7 = (bf16[1,1,4096,64]{2,3,1,0:T(8,128)(2,1)S(1)}, bf16[1,1,4096,64]{2,3,1,0:T(8,128)(2,1)S(1)}, u32[]{:S(2)}, u32[]{:S(2)}) collective-permute-start(bf16[1,1,4096,64]{2,3,1,0:T(8,128)(2,1)S(1)} %collective-permute-done), channel_id=1, source_target_pairs={{0,8},{8,0},{16,24},{24,16},{1,9},{9,1},{17,25},{25,17},{2,10},{10... | collective-permute-start | bytes 1572872 | tf_op jit(solution)/shard_map/ppermute | solution.py:24
  19.0 14.3 %collective-permute-start.3 = (bf16[1,1,4096,64]{2,3,1,0:T(8,128)(2,1)S(1)}, bf16[1,1,4096,64]{2,3,1,0:T(8,128)(2,1)S(1)}, u32[]{:S(2)}, u32[]{:S(2)}) collective-permute-start(bf16[1,1,4096,64]{2,3,1,0:T(8,128)(2,1)S(1)} %collective-permute-done.1), channel_id=1, source_target_pairs={{0,1},{1,0},{2,3},{3,2},{4,5},{5,4},{6,7},{7,6},{8,9},{9,8},{10,11... | collective-permute-start | bytes 1572872 | tf_op jit(solution)/shard_map/ppermute | solution.py:24
  20.8 12.6 %collective-permute-start.4 = (bf16[1,1,4096,64]{2,3,1,0:T(8,128)(2,1)S(1)}, bf16[1,1,4096,64]{2,3,1,0:T(8,128)(2,1)S(1)}, u32[]{:S(2)}, u32[]{:S(2)}) collective-permute-start(bf16[1,1,4096,64]{2,3,1,0:T(8,128)(2,1)S(1)} %collective-permute-done), channel_id=1, source_target_pairs={{8,18},{10,20},{12,22},{11,17},{13,19},{15,21},{16,10},{18,12},{20... | collective-permute-start | bytes 1572872 | tf_op jit(solution)/shard_map/ppermute | solution.py:42
  21.5 15.0 %collective-permute-start.2 = (bf16[1,1,4096,64]{2,3,1,0:T(8,128)(2,1)S(1)}, bf16[1,1,4096,64]{2,3,1,0:T(8,128)(2,1)S(1)}, u32[]{:S(2)}, u32[]{:S(2)}) collective-permute-start(bf16[1,1,4096,64]{2,3,1,0:T(8,128)(2,1)S(1)} %collective-permute-done), channel_id=1, source_target_pairs={{8,16},{16,8},{9,17},{17,9},{10,18},{18,10},{11,19},{19,11},{12,20... | collective-permute-start | bytes 1572872 | tf_op jit(solution)/shard_map/ppermute | solution.py:28
  33.4 3.9 %collective-permute-start.8 = (bf16[1,1,4096,64]{2,3,1,0:T(8,128)(2,1)S(1)}, bf16[1,1,4096,64]{2,3,1,0:T(8,128)(2,1)S(1)}, u32[]{:S(2)}, u32[]{:S(2)}) collective-permute-start(bf16[1,1,4096,64]{2,3,1,0:T(8,128)(2,1)S(1)} %collective-permute-done.3), channel_id=1, source_target_pairs={{0,8},{8,0},{16,24},{24,16},{1,9},{9,1},{17,25},{25,17},{2,10},{10... | collective-permute-start | bytes 1572872 | tf_op jit(solution)/shard_map/ppermute | solution.py:24
  39.1 2.7 %collective-permute-start.9 = (f32[32,128]{1,0:T(8,128)S(1)}, f32[32,128]{1,0:T(8,128)S(1)}, u32[]{:S(2)}, u32[]{:S(2)}) collective-permute-start(f32[32,128]{1,0:T(8,128)S(1)} %get-tuple-element.30), channel_id=1, source_target_pairs={{0,8},{1,9},{2,10},{3,11},{4,12},{5,13},{6,14},{7,15},{8,0},{9,1},... | collective-permute-start | bytes 49160 | tf_op jit(solution)/shard_map/ppermute | solution.py:276
  41.8 4.6 %collective-permute-start.12 = (f32[32,128]{1,0:T(8,128)S(1)}, f32[32,128]{1,0:T(8,128)S(1)}, u32[]{:S(2)}, u32[]{:S(2)}) collective-permute-start(f32[32,128]{1,0:T(8,128)S(1)} %add.21), channel_id=1, source_target_pairs={{0,17},{1,16},{2,19},{3,18},{4,21},{5,20},{6,23},{7,22},{8,25},{9,... | collective-permute-start | bytes 49160 | tf_op jit(solution)/shard_map/ppermute | solution.py:276
  44.3 3.7 %collective-permute-start.11 = (f32[32,128]{1,0:T(8,128)S(1)}, f32[32,128]{1,0:T(8,128)S(1)}, u32[]{:S(2)}, u32[]{:S(2)}) collective-permute-start(f32[32,128]{1,0:T(8,128)S(1)} %add.21), channel_id=1, source_target_pairs={{0,1},{1,0},{2,3},{3,2},{4,5},{5,4},{6,7},{7,6},{8,9},{9,8},{10,11... | collective-permute-start | bytes 49160 | tf_op jit(solution)/shard_map/ppermute | solution.py:276
  44.9 3.7 %collective-permute-start.10 = (f32[32,128]{1,0:T(8,128)S(1)}, f32[32,128]{1,0:T(8,128)S(1)}, u32[]{:S(2)}, u32[]{:S(2)}) collective-permute-start(f32[32,128]{1,0:T(8,128)S(1)} %add.21), channel_id=1, source_target_pairs={{0,16},{1,17},{2,18},{3,19},{4,20},{5,21},{6,22},{7,23},{8,24},{9,... | collective-permute-start | bytes 49160 | tf_op jit(solution)/shard_map/ppermute | solution.py:276
  48.7 5.7 %collective-permute-start.15 = (f32[32,128]{1,0:T(8,128)S(1)}, f32[32,128]{1,0:T(8,128)S(1)}, u32[]{:S(2)}, u32[]{:S(2)}) collective-permute-start(f32[32,128]{1,0:T(8,128)S(1)} %add_add_fusion.1), channel_id=1, source_target_pairs={{0,6},{1,7},{2,4},{3,5},{4,2},{5,3},{6,0},{7,1},{8,14},{9,15},{10,... | collective-permute-start | bytes 49160 | tf_op jit(solution)/shard_map/ppermute | solution.py:276
  52.0 4.7 %collective-permute-start.14 = (f32[32,128]{1,0:T(8,128)S(1)}, f32[32,128]{1,0:T(8,128)S(1)}, u32[]{:S(2)}, u32[]{:S(2)}) collective-permute-start(f32[32,128]{1,0:T(8,128)S(1)} %add_add_fusion.1), channel_id=1, source_target_pairs={{0,4},{1,5},{2,6},{3,7},{4,0},{5,1},{6,2},{7,3},{8,12},{9,13},{10,... | collective-permute-start | bytes 49160 | tf_op jit(solution)/shard_map/ppermute | solution.py:276
  52.9 3.9 %collective-permute-start.13 = (f32[32,128]{1,0:T(8,128)S(1)}, f32[32,128]{1,0:T(8,128)S(1)}, u32[]{:S(2)}, u32[]{:S(2)}) collective-permute-start(f32[32,128]{1,0:T(8,128)S(1)} %add_add_fusion.1), channel_id=1, source_target_pairs={{0,2},{1,3},{2,0},{3,1},{4,6},{5,7},{6,4},{7,5},{8,10},{9,11},{10,... | collective-permute-start | bytes 49160 | tf_op jit(solution)/shard_map/ppermute | solution.py:276

commit v5 on v4

--- a/solution.py
+++ b/solution.py
@@ -11,6 +11,7 @@
 PARTS = 3
 HALVES = 2
 CHUNKS = 4
+AHEAD = 2
 LIST_ROWS = 3
 LINES = PARTS * HALVES * LIST_ROWS + 6
 PART_OF = (0, 0, 0, 0, 0, 2, 1, 2, 1)
@@ -32,21 +33,35 @@
     return [(i, i + 1) for i in range(1, size - 1, 2)] + [(i + 1, i) for i in range(1, size - 1, 2)]
 
 
-def across_both(value):
+def pass_on(value, axis):
+    pairs = [(sender ^ 1, receiver) for sender, receiver in outside(lax.axis_size(axis))]
+    return lax.ppermute(value, axis, pairs)
+
+
+def swap_of_outer(value):
+    gx_count, gy_count = lax.axis_size("gx"), lax.axis_size("gy")
+    pairs = [(x * gy_count + y, x * gy_count + (y ^ 1)) for x, _ in outside(gx_count) for y in range(gy_count)]
+    return lax.ppermute(value, ("gx", "gy"), pairs)
+
+
+def to_mate_of_outside(value):
     gx_count, gy_count = lax.axis_size("gx"), lax.axis_size("gy")
     pairs = [
-        (from_x * gy_count + (from_y ^ 1), to_x * gy_count + to_y)
-        for from_x, to_x in outside(gx_count)
-        for from_y, to_y in outside(gy_count)
+        (x * gy_count + sender, x * gy_count + (receiver ^ 1))
+        for x, _ in outside(gx_count)
+        for sender, receiver in outside(gy_count)
     ]
     return lax.ppermute(value, ("gx", "gy"), pairs)
 
 
-def two_back(value, axis):
-    size = lax.axis_size(axis)
-    pairs = [(i, i - 2) for i in range(2, size, 2)]
-    pairs += [(i, i + 2) for i in range(1, size - 2, 2)]
-    return lax.ppermute(value, axis, pairs)
+def from_mate_across(value):
+    gx_count, gy_count = lax.axis_size("gx"), lax.axis_size("gy")
+    pairs = [
+        (from_x * gy_count + (receiver ^ 1), to_x * gy_count + receiver)
+        for from_x, to_x in outside(gx_count)
+        for _, receiver in outside(gy_count)
+    ]
+    return lax.ppermute(value, ("gx", "gy"), pairs)
 
 
 def exact_log2(value):
@@ -162,20 +177,19 @@
 
 
 def loads_of(half, near_hbm, near, sems):
-    chunks = sems.shape[1]
-    length = near.shape[0] // chunks
+    length = near.shape[0] // CHUNKS
     return [
         pltpu.make_async_copy(
             near_hbm.at[pl.ds(half * near.shape[0] + chunk * length, length)],
             near.at[pl.ds(chunk * length, length)],
-            sems.at[half, chunk],
+            sems.at[chunk],
         )
-        for chunk in range(chunks)
+        for chunk in range(CHUNKS)
     ]
 
 
 def load_kernel(tiles_dev, gy_count, links, near_hbm, near_0, near_1, work, sems):
-    loads = [load for half, near in enumerate((near_0, near_1)) for load in loads_of(half, near_hbm, near, sems)]
+    loads = loads_of(0, near_hbm, near_0, sems.at[0]) + loads_of(1, near_hbm, near_1, sems.at[1])[:AHEAD]
     for load in loads:
         load.start()
     build_lists(links, work, tiles_dev, near_hbm.shape[0] // tiles_dev, gy_count)
@@ -183,14 +197,37 @@
         load.wait()
 
 
-def early_kernel(work_in, near_0, near_1, *refs):
-    acc, rows, work, sem = refs[-4:]
+def early_kernel(work_in, near_hbm, near_0, near_in, *refs):
+    near_1, acc, rows, work, sem, sems = refs[-6:]
+    loads = loads_of(1, near_hbm, near_1, sems)
+    for load in loads[AHEAD:]:
+        load.start()
     copy = pltpu.make_async_copy(work_in, work, sem)
     copy.start()
-    lay_out(refs[:-4], rows, acc.shape[0])
+    lay_out(refs[:-6], rows, acc.shape[0])
     acc[...] = jnp.zeros(acc.shape, acc.dtype)
     copy.wait()
-    add_both(0, work, (near_0, near_1), acc, rows)
+    length = near_1.shape[0] // CHUNKS
+    count = batches(0, 1, work)
+
+    def wait(chunk, carry):
+        held = near_1.at[pl.ds(chunk * length, length)]
+        pltpu.make_async_copy(near_hbm.at[pl.ds(chunk * length, length)], held, sems.at[chunk]).wait()
+        return carry
+
+    def step(index, there):
+        groups = 128 // UNROLL
+        last = work[LIST_ROWS + lax.div(index, groups), lax.rem(index, groups) * UNROLL + UNROLL - 2]
+        needed = jnp.where(index >= count - 1, CHUNKS, lax.div(lax.shift_right_logical(last, 9), length) + 1)
+        lax.fori_loop(there, needed, wait, 0)
+        products = []
+        for half, near in enumerate((near_0, near_1)):
+            products += products_of(0, half, work, index, near, acc, rows)
+        add_all(products, acc)
+        return jnp.maximum(there, needed)
+
+    there = lax.fori_loop(0, jnp.maximum(batches(0, 0, work), count), step, jnp.int32(AHEAD))
+    lax.fori_loop(there, CHUNKS, wait, 0)
 
 
 def next_kernel(work_in, near_0, near_1, *refs):
@@ -293,7 +330,7 @@
     scale = float(rows * gx_count * gy_count) ** 0.5
 
     beside = pair_swap(block, "gy")
-    two_off = two_back(block, "gy")
+    two_off = to_mate_of_outside(block)
     outer = between_pairs(block, "gx")
     core = pair_swap(block, "gx")
 
@@ -321,15 +358,17 @@
     )(links, near)
 
     beside, two_off, work = lax.optimization_barrier((beside, two_off, work))
-    beyond = pair_swap(two_off, "gy")
-    beside_outer = between_pairs(beside, "gx")
-    beyond_outer = across_both(beside)
+    beyond = pass_on(beside, "gy")
+    beside_outer = swap_of_outer(outer)
+    beyond_outer = from_mate_across(two_off)
     beside_core = pair_swap(beside, "gx")
     sources = (block, core, outer, beside, beside_core)
-    acc = pl.pallas_call(
-        early_kernel, out_shape=acc_shape, in_specs=[in_vmem()] * 8, out_specs=in_vmem(),
-        scratch_shapes=[tile_rows(5)] + work_scratch, name="early_rows", **params(),
-    )(work, near_0, near_1, *(flat(source) for source in sources))
+    near_1, acc = pl.pallas_call(
+        early_kernel, out_shape=(near_half, acc_shape),
+        in_specs=[in_vmem(), pl.BlockSpec(memory_space=pltpu.HBM)] + [in_vmem()] * 7, out_specs=(in_vmem(),) * 2,
+        scratch_shapes=[tile_rows(5)] + work_scratch + [pltpu.SemaphoreType.DMA((CHUNKS,))],
+        name="early_rows", input_output_aliases={3: 0}, **params(24 * 2**20),
+    )(work, near, near_0, near_1, *(flat(source) for source in sources))
 
     beyond, beyond_outer, acc = lax.optimization_barrier((beyond, beyond_outer, acc))
     beyond_core = pair_swap(beyond, "gx")

time: 60.2 us -> 60.3 us (level)
  Pallas kernels: 21 us -> 19.7 us
    ppermute x5 -> x4, starting transfers between devices: 12.2 us -> 7.22 us  [pair_swap(): return lax.ppermute(value, axis, [(i, i ^ 1) for i in range(size)])]
    ppermute x2 -> x4, starting transfers between devices: 1.97 us -> 5.94 us  [the longest x1 3.87 us: pass_on(): return lax.ppermute(value, axis, pairs)]
    ppermute x5 -> x4, waiting for transfers between devices: 4.22 us -> 1.57 us  [pair_swap(): return lax.ppermute(value, axis, [(i, i ^ 1) for i in range(size)])]
    ppermute x7, starting transfers between devices: 9.83 us -> 12 us  [from_other(): lax.ppermute(value, ('gx', 'gy'), [(i, i ^ mask) for i in range(total)])]
    ppermute x2 -> x4, waiting for transfers between devices: 0.01 us -> 2.08 us  [the longest x1 2.08 us: pass_on(): return lax.ppermute(value, axis, pairs)]
    pallas_call x1, Pallas kernels: 7.19 us -> 5.69 us  [shards(): pl.pallas_call(functools.partial(load_kernel, tiles_dev, gy_count), out_s...]
    ppermute x7, waiting for transfers between devices: 7.83 us -> 8.9 us  [from_other(): lax.ppermute(value, ('gx', 'gy'), [(i, i ^ mask) for i in range(total)])]
    ppermute x2 -> x1, starting transfers between devices: 1.38 us -> 0.69 us  [between_pairs(): return lax.ppermute(value, axis, outside(lax.axis_size(axis)))]
  transfers between devices with their start and end apart: 16 -> 16, of which waited for: 9 -> 8; matrix products, arithmetic and copies ran while one was open for 1% -> 1% of each run, Pallas kernels for 27% -> 25%
where the time goes in v5:
time: 60.3 us; the launch traced here: 59.6 us
  starting transfers between devices  25.9 us (43%)
  Pallas kernels  19.7 us (33%)
  waiting for transfers between devices  12.6 us (21%)
  between operations  0.76 us (1%)
  local copies, waits for them, and re-layouts  0.72 us (1%)
    ppermute x7, starting transfers between devices, from_other(): lax.ppermute(value, ('gx', 'gy'), [(i, i ^ mask) for i in range(total)])  12 us
    ppermute x7, waiting for transfers between devices, from_other(): lax.ppermute(value, ('gx', 'gy'), [(i, i ^ mask) for i in range(total)])  8.9 us
    pallas_call x1, Pallas kernels, shards(): pl.pallas_call(early_kernel, out_shape=(near_half, acc_shape), in_specs=[...  8.25 us
    ppermute x4, starting transfers between devices, pair_swap(): return lax.ppermute(value, axis, [(i, i ^ 1) for i in range(size)])  7.22 us
    pallas_call x1, Pallas kernels, shards(): pl.pallas_call(functools.partial(load_kernel, tiles_dev, gy_count), out_s...  5.69 us
    ppermute x1, starting transfers between devices, pass_on(): return lax.ppermute(value, axis, pairs)  3.87 us
    pallas_call x1, Pallas kernels, shards(): pl.pallas_call(functools.partial(finish_kernel, scale), out_shape=(jax.Sh...  3.14 us
    ppermute x1, waiting for transfers between devices, pass_on(): return lax.ppermute(value, axis, pairs)  2.08 us
  transfers between devices with their start and end apart: 16, of which 8 were waited for; matrix products, arithmetic and copies ran while one was open for 1% of the time, Pallas kernels for 25%

profile of v5, /device:TPU:0, one launch (start us, length us, event | category | flops | bytes accessed | tf_op | source)
XLA Modules:
  0.0 59.6 jit_solution(17713404828720854078)
XLA Ops:
  0.6 3.0 %collective-permute-start = (bf16[1,1,4096,64]{2,3,1,0:T(8,128)(2,1)}, bf16[1,1,4096,64]{2,3,1,0:T(8,128)(2,1)S(1)}, u32[]{:S(2)}, u32[]{:S(2)}) collective-permute-start(bf16[1,1,4096,64]{2,3,1,0:T(8,128)(2,1)} %param.4), channel_id=1, source_target_pairs={{0,1},{1,0},{2,3},{3,2},{4,5},{5,4},{6,7},{7,6},{8,9},{9,8},{10,11... | collective-permute-start | bytes 1572872 | tf_op jit(solution)/shard_map/ppermute | solution.py:25
  3.6 0.7 %collective-permute-start.1 = (bf16[1,1,4096,64]{2,3,1,0:T(8,128)(2,1)}, bf16[1,1,4096,64]{2,3,1,0:T(8,128)(2,1)S(1)}, u32[]{:S(2)}, u32[]{:S(2)}) collective-permute-start(bf16[1,1,4096,64]{2,3,1,0:T(8,128)(2,1)} %param.4), channel_id=1, source_target_pairs={{9,11},{11,13},{13,15},{10,8},{12,10},{14,12},{17,19},{19,21},{21,... | collective-permute-start | bytes 1572872 | tf_op jit(solution)/shard_map/ppermute | solution.py:54
  4.3 0.7 %collective-permute-start.3 = (bf16[1,1,4096,64]{2,3,1,0:T(8,128)(2,1)}, bf16[1,1,4096,64]{2,3,1,0:T(8,128)(2,1)S(1)}, u32[]{:S(2)}, u32[]{:S(2)}) collective-permute-start(bf16[1,1,4096,64]{2,3,1,0:T(8,128)(2,1)} %param.4), channel_id=1, source_target_pairs={{8,16},{16,8},{9,17},{17,9},{10,18},{18,10},{11,19},{19,11},{12,20... | collective-permute-start | bytes 1572872 | tf_op jit(solution)/shard_map/ppermute | solution.py:29
  5.0 3.5 %collective-permute-start.2 = (bf16[1,1,4096,64]{2,3,1,0:T(8,128)(2,1)}, bf16[1,1,4096,64]{2,3,1,0:T(8,128)(2,1)S(1)}, u32[]{:S(2)}, u32[]{:S(2)}) collective-permute-start(bf16[1,1,4096,64]{2,3,1,0:T(8,128)(2,1)} %param.4), channel_id=1, source_target_pairs={{0,8},{8,0},{16,24},{24,16},{1,9},{9,1},{17,25},{25,17},{2,10},{10... | collective-permute-start | bytes 1572872 | tf_op jit(solution)/shard_map/ppermute | solution.py:25
  8.5 0.7 %copy.10 = s32[1,1,32,20]{2,3,1,0:T(8,128)S(1)} copy(s32[1,1,32,20]{2,1,3,0:T(1,128)} %param.5) | data formatting | bytes 5120
  9.3 0.0 copy-start
  9.3 5.7 %load.1 = (bf16[320,128,128]{2,1,0:T(8,128)(2,1)S(1)}, bf16[320,128,128]{2,1,0:T(8,128)(2,1)S(1)}, s32[24,128]{1,0:T(8,128)S(1)}) custom-call(s32[20,1,32]{2,1,0:T(1,128)S(1)} %reshape.13.links, bf16[640,128,128]{2,1,0:T(8,128)(2,1)} %bitcast.45), custom_call_target="tpu_custom_call" | custom-call | tf_op jit(solution)/shard_map/load/pallas_call | solution.py:353
  15.0 0.8 %collective-permute-done = bf16[1,1,4096,64]{2,3,1,0:T(8,128)(2,1)S(1)} collective-permute-done((bf16[1,1,4096,64]{2,3,1,0:T(8,128)(2,1)}, bf16[1,1,4096,64]{2,3,1,0:T(8,128)(2,1)S(1)}, u32[]{:S(2)}, u32[]{:S(2)}) %collective-permute-start) | collective-permute-done | bytes 524320 | tf_op jit(solution)/shard_map/ppermute | solution.py:25
  15.8 3.9 %collective-permute-start.6 = (bf16[1,1,4096,64]{2,3,1,0:T(8,128)(2,1)S(1)}, bf16[1,1,4096,64]{2,3,1,0:T(8,128)(2,1)S(1)}, u32[]{:S(2)}, u32[]{:S(2)}) collective-permute-start(bf16[1,1,4096,64]{2,3,1,0:T(8,128)(2,1)S(1)} %collective-permute-done), channel_id=1, source_target_pairs={{0,2},{2,4},{4,6},{3,1},{5,3},{7,5},{8,10},{10,12},{12,14},{11,9},... | collective-permute-start | bytes 1572872 | tf_op jit(solution)/shard_map/ppermute | solution.py:38
  19.7 0.7 %collective-permute-start.7 = (bf16[1,1,4096,64]{2,3,1,0:T(8,128)(2,1)S(1)}, bf16[1,1,4096,64]{2,3,1,0:T(8,128)(2,1)S(1)}, u32[]{:S(2)}, u32[]{:S(2)}) collective-permute-start(bf16[1,1,4096,64]{2,3,1,0:T(8,128)(2,1)S(1)} %collective-permute-done.1), channel_id=1, source_target_pairs={{11,18},{13,20},{15,22},{8,17},{10,19},{12,21},{19,10},{21,12},{23... | collective-permute-start | bytes 1572872 | tf_op jit(solution)/shard_map/ppermute | solution.py:64
  20.4 0.0 collective-permute-done.3
  20.4 0.7 %collective-permute-start.5 = (bf16[1,1,4096,64]{2,3,1,0:T(8,128)(2,1)S(1)}, bf16[1,1,4096,64]{2,3,1,0:T(8,128)(2,1)S(1)}, u32[]{:S(2)}, u32[]{:S(2)}) collective-permute-start(bf16[1,1,4096,64]{2,3,1,0:T(8,128)(2,1)S(1)} %collective-permute-done.3), channel_id=1, source_target_pairs={{8,9},{9,8},{10,11},{11,10},{12,13},{13,12},{14,15},{15,14},{16,17... | collective-permute-start | bytes 1572872 | tf_op jit(solution)/shard_map/ppermute | solution.py:44
  21.1 8.3 %early_rows.1 = (bf16[320,128,128]{2,1,0:T(8,128)(2,1)S(1)}, f32[32,128,64]{2,1,0:T(8,128)S(1)}) custom-call(s32[24,128]{1,0:T(8,128)S(1)} %get-tuple-element.21.work_in, bf16[640,128,128]{2,1,0:T(8,128)(2,1)} %bitcast.46, bf16[320,128,128]{2,1,0:T(8,128)(2,1)S(1)} %get-tuple-element.22.near_0, ...), custom_call_target="tpu_custom_call", output_to_operand_aliasing={{0}: (3, {})} | custom-call | tf_op jit(solution)/shard_map/early_rows/pallas_call | solution.py:366
  29.4 2.1 %collective-permute-done.6 = bf16[1,1,4096,64]{2,3,1,0:T(8,128)(2,1)S(1)} collective-permute-done((bf16[1,1,4096,64]{2,3,1,0:T(8,128)(2,1)S(1)}, bf16[1,1,4096,64]{2,3,1,0:T(8,128)(2,1)S(1)}, u32[]{:S(2)}, u32[]{:S(2)}) %collective-permute-start.6) | collective-permute-done | bytes 524320 | tf_op jit(solution)/shard_map/ppermute | solution.py:38
  31.4 0.0 collective-permute-done.7
  31.4 0.7 %collective-permute-start.8 = (bf16[1,1,4096,64]{2,3,1,0:T(8,128)(2,1)S(1)}, bf16[1,1,4096,64]{2,3,1,0:T(8,128)(2,1)S(1)}, u32[]{:S(2)}, u32[]{:S(2)}) collective-permute-start(bf16[1,1,4096,64]{2,3,1,0:T(8,128)(2,1)S(1)} %collective-permute-done.6), channel_id=1, source_target_pairs={{0,8},{8,0},{16,24},{24,16},{1,9},{9,1},{17,25},{25,17},{2,10},{10... | collective-permute-start | bytes 1572872 | tf_op jit(solution)/shard_map/ppermute | solution.py:25
  32.1 0.8 %next_rows.1.acc_in = f32[32,128,64]{2,1,0:T(8,128)S(1)} custom-call(s32[24,128]{1,0:T(8,128)S(1)} %get-tuple-element.21.work_in, bf16[320,128,128]{2,1,0:T(8,128)(2,1)S(1)} %get-tuple-element.22.near_0, bf16[320,128,128]{2,1,0:T(8,128)(2,1)S(1)} %get-tuple-element.25.near_1, bf16[64,4096]{1,0:T(8,128)(2,1)S(1)} %bitcast.41, ...), custom_call_target="tpu_custom_call", output_to_operand_aliasing={{}: (5, {})} | custom-call | tf_op jit(solution)/shard_map/next_rows/pallas_call | solution.py:375
  32.9 0.8 %collective-permute-done.8 = bf16[1,1,4096,64]{2,3,1,0:T(8,128)(2,1)S(1)} collective-permute-done((bf16[1,1,4096,64]{2,3,1,0:T(8,128)(2,1)S(1)}, bf16[1,1,4096,64]{2,3,1,0:T(8,128)(2,1)S(1)}, u32[]{:S(2)}, u32[]{:S(2)}) %collective-permute-start.8) | collective-permute-done | bytes 524320 | tf_op jit(solution)/shard_map/ppermute | solution.py:25
  33.7 1.8 %last_rows_and_gram.1 = (bf16[128,4096]{1,0:T(8,128)(2,1)S(1)}, f32[32,128]{1,0:T(8,128)S(1)}, f32[32,128,64]{2,1,0:T(8,128)S(1)}) custom-call(s32[24,128]{1,0:T(8,128)S(1)} %get-tuple-element.21.work_in, bf16[320,128,128]{2,1,0:T(8,128)(2,1)S(1)} %get-tuple-element.22.near_0, ...), custom_call_target="tpu_custom_call", output_to_operand_aliasing={{2}: (5, {})} | custom-call | tf_op jit(solution)/shard_map/last_rows_and_gram/pallas_call | solution.py:381
  35.5 1.9 %collective-permute-start.9 = (f32[32,128]{1,0:T(8,128)S(1)}, f32[32,128]{1,0:T(8,128)S(1)}, u32[]{:S(2)}, u32[]{:S(2)}) collective-permute-start(f32[32,128]{1,0:T(8,128)S(1)} %get-tuple-element.34), channel_id=1, source_target_pairs={{0,8},{1,9},{2,10},{3,11},{4,12},{5,13},{6,14},{7,15},{8,0},{9,1},... | collective-permute-start | bytes 49160 | tf_op jit(solution)/shard_map/ppermute | solution.py:313
  37.4 0.8 %collective-permute-done.9 = f32[32,128]{1,0:T(8,128)S(1)} collective-permute-done((f32[32,128]{1,0:T(8,128)S(1)}, f32[32,128]{1,0:T(8,128)S(1)}, u32[]{:S(2)}, u32[]{:S(2)}) %collective-permute-start.9) | collective-permute-done | bytes 16416 | tf_op jit(solution)/shard_map/ppermute | solution.py:313
  38.3 0.5 collective-permute-start.10
  38.7 4.8 %collective-permute-start.11 = (f32[32,128]{1,0:T(8,128)S(1)}, f32[32,128]{1,0:T(8,128)S(1)}, u32[]{:S(2)}, u32[]{:S(2)}) collective-permute-start(f32[32,128]{1,0:T(8,128)S(1)} %add.21), channel_id=1, source_target_pairs={{0,1},{1,0},{2,3},{3,2},{4,5},{5,4},{6,7},{7,6},{8,9},{9,8},{10,11... | collective-permute-start | bytes 49160 | tf_op jit(solution)/shard_map/ppermute | solution.py:313
  43.5 0.4 collective-permute-start.12
  43.9 1.3 %collective-permute-done.11 = f32[32,128]{1,0:T(8,128)S(1)} collective-permute-done((f32[32,128]{1,0:T(8,128)S(1)}, f32[32,128]{1,0:T(8,128)S(1)}, u32[]{:S(2)}, u32[]{:S(2)}) %collective-permute-start.11) | collective-permute-done | bytes 16416 | tf_op jit(solution)/shard_map/ppermute | solution.py:313
  45.2 2.9 %collective-permute-done.12 = f32[32,128]{1,0:T(8,128)S(1)} collective-permute-done((f32[32,128]{1,0:T(8,128)S(1)}, f32[32,128]{1,0:T(8,128)S(1)}, u32[]{:S(2)}, u32[]{:S(2)}) %collective-permute-start.12) | collective-permute-done | bytes 16416 | tf_op jit(solution)/shard_map/ppermute | solution.py:313
  48.2 1.6 %collective-permute-start.13 = (f32[32,128]{1,0:T(8,128)S(1)}, f32[32,128]{1,0:T(8,128)S(1)}, u32[]{:S(2)}, u32[]{:S(2)}) collective-permute-start(f32[32,128]{1,0:T(8,128)S(1)} %add_add_fusion.1), channel_id=1, source_target_pairs={{0,2},{1,3},{2,0},{3,1},{4,6},{5,7},{6,4},{7,5},{8,10},{9,11},{10,... | collective-permute-start | bytes 49160 | tf_op jit(solution)/shard_map/ppermute | solution.py:313
  49.8 1.1 %collective-permute-start.14 = (f32[32,128]{1,0:T(8,128)S(1)}, f32[32,128]{1,0:T(8,128)S(1)}, u32[]{:S(2)}, u32[]{:S(2)}) collective-permute-start(f32[32,128]{1,0:T(8,128)S(1)} %add_add_fusion.1), channel_id=1, source_target_pairs={{0,4},{1,5},{2,6},{3,7},{4,0},{5,1},{6,2},{7,3},{8,12},{9,13},{10,... | collective-permute-start | bytes 49160 | tf_op jit(solution)/shard_map/ppermute | solution.py:313
  50.9 1.7 %collective-permute-start.15 = (f32[32,128]{1,0:T(8,128)S(1)}, f32[32,128]{1,0:T(8,128)S(1)}, u32[]{:S(2)}, u32[]{:S(2)}) collective-permute-start(f32[32,128]{1,0:T(8,128)S(1)} %add_add_fusion.1), channel_id=1, source_target_pairs={{0,6},{1,7},{2,4},{3,5},{4,2},{5,3},{6,0},{7,1},{8,14},{9,15},{10,... | collective-permute-start | bytes 49160 | tf_op jit(solution)/shard_map/ppermute | solution.py:313
  52.6 1.9 %collective-permute-done.14 = f32[32,128]{1,0:T(8,128)S(1)} collective-permute-done((f32[32,128]{1,0:T(8,128)S(1)}, f32[32,128]{1,0:T(8,128)S(1)}, u32[]{:S(2)}, u32[]{:S(2)}) %collective-permute-start.14) | collective-permute-done | bytes 16416 | tf_op jit(solution)/shard_map/ppermute | solution.py:313
  54.5 1.9 %collective-permute-done.15 = f32[32,128]{1,0:T(8,128)S(1)} collective-permute-done((f32[32,128]{1,0:T(8,128)S(1)}, f32[32,128]{1,0:T(8,128)S(1)}, u32[]{:S(2)}, u32[]{:S(2)}) %collective-permute-start.15) | collective-permute-done | bytes 16416 | tf_op jit(solution)/shard_map/ppermute | solution.py:313
  56.5 3.1 %orthonormalize.1 = (f32[64,4096]{1,0:T(8,128)}, f32[64,64]{1,0:T(8,128)}) custom-call(f32[32,128]{1,0:T(8,128)S(1)} %add_add_fusion.gram, bf16[128,4096]{1,0:T(8,128)(2,1)S(1)} %get-tuple-element.35.split), custom_call_target="tpu_custom_call" | custom-call | tf_op jit(solution)/shard_map/orthonormalize/pallas_call | solution.py:393
  (12 shorter events, 0.0 us)
Async XLA Ops:
  0.6 15.1 %collective-permute-start = (bf16[1,1,4096,64]{2,3,1,0:T(8,128)(2,1)}, bf16[1,1,4096,64]{2,3,1,0:T(8,128)(2,1)S(1)}, u32[]{:S(2)}, u32[]{:S(2)}) collective-permute-start(bf16[1,1,4096,64]{2,3,1,0:T(8,128)(2,1)} %param.4), channel_id=1, source_target_pairs={{0,1},{1,0},{2,3},{3,2},{4,5},{5,4},{6,7},{7,6},{8,9},{9,8},{10,11... | collective-permute-start | bytes 1572872 | tf_op jit(solution)/shard_map/ppermute | solution.py:25
  3.6 12.1 %collective-permute-start.1 = (bf16[1,1,4096,64]{2,3,1,0:T(8,128)(2,1)}, bf16[1,1,4096,64]{2,3,1,0:T(8,128)(2,1)S(1)}, u32[]{:S(2)}, u32[]{:S(2)}) collective-permute-start(bf16[1,1,4096,64]{2,3,1,0:T(8,128)(2,1)} %param.4), channel_id=1, source_target_pairs={{9,11},{11,13},{13,15},{10,8},{12,10},{14,12},{17,19},{19,21},{21,... | collective-permute-start | bytes 1572872 | tf_op jit(solution)/shard_map/ppermute | solution.py:54
  4.3 16.0 %collective-permute-start.3 = (bf16[1,1,4096,64]{2,3,1,0:T(8,128)(2,1)}, bf16[1,1,4096,64]{2,3,1,0:T(8,128)(2,1)S(1)}, u32[]{:S(2)}, u32[]{:S(2)}) collective-permute-start(bf16[1,1,4096,64]{2,3,1,0:T(8,128)(2,1)} %param.4), channel_id=1, source_target_pairs={{8,16},{16,8},{9,17},{17,9},{10,18},{18,10},{11,19},{19,11},{12,20... | collective-permute-start | bytes 1572872 | tf_op jit(solution)/shard_map/ppermute | solution.py:29
  5.0 16.0 %collective-permute-start.2 = (bf16[1,1,4096,64]{2,3,1,0:T(8,128)(2,1)}, bf16[1,1,4096,64]{2,3,1,0:T(8,128)(2,1)S(1)}, u32[]{:S(2)}, u32[]{:S(2)}) collective-permute-start(bf16[1,1,4096,64]{2,3,1,0:T(8,128)(2,1)} %param.4), channel_id=1, source_target_pairs={{0,8},{8,0},{16,24},{24,16},{1,9},{9,1},{17,25},{25,17},{2,10},{10... | collective-permute-start | bytes 1572872 | tf_op jit(solution)/shard_map/ppermute | solution.py:25
  9.3 11.8 %copy-start = (bf16[1,1,4096,64]{2,3,1,0:T(8,128)(2,1)S(1)}, bf16[1,1,4096,64]{2,3,1,0:T(8,128)(2,1)}, u32[]{:S(2)}) copy-start(bf16[1,1,4096,64]{2,3,1,0:T(8,128)(2,1)} %param.4) | copy-start | bytes 1572868
  15.8 5.3 %collective-permute-start.4 = (bf16[1,1,4096,64]{2,3,1,0:T(8,128)(2,1)S(1)}, bf16[1,1,4096,64]{2,3,1,0:T(8,128)(2,1)S(1)}, u32[]{:S(2)}, u32[]{:S(2)}) collective-permute-start(bf16[1,1,4096,64]{2,3,1,0:T(8,128)(2,1)S(1)} %collective-permute-done), channel_id=1, source_target_pairs={{0,8},{8,0},{16,24},{24,16},{1,9},{9,1},{17,25},{25,17},{2,10},{10... | collective-permute-start | bytes 1572872 | tf_op jit(solution)/shard_map/ppermute | solution.py:25
  15.8 15.7 %collective-permute-start.6 = (bf16[1,1,4096,64]{2,3,1,0:T(8,128)(2,1)S(1)}, bf16[1,1,4096,64]{2,3,1,0:T(8,128)(2,1)S(1)}, u32[]{:S(2)}, u32[]{:S(2)}) collective-permute-start(bf16[1,1,4096,64]{2,3,1,0:T(8,128)(2,1)S(1)} %collective-permute-done), channel_id=1, source_target_pairs={{0,2},{2,4},{4,6},{3,1},{5,3},{7,5},{8,10},{10,12},{12,14},{11,9},... | collective-permute-start | bytes 1572872 | tf_op jit(solution)/shard_map/ppermute | solution.py:38
  19.7 11.8 %collective-permute-start.7 = (bf16[1,1,4096,64]{2,3,1,0:T(8,128)(2,1)S(1)}, bf16[1,1,4096,64]{2,3,1,0:T(8,128)(2,1)S(1)}, u32[]{:S(2)}, u32[]{:S(2)}) collective-permute-start(bf16[1,1,4096,64]{2,3,1,0:T(8,128)(2,1)S(1)} %collective-permute-done.1), channel_id=1, source_target_pairs={{11,18},{13,20},{15,22},{8,17},{10,19},{12,21},{19,10},{21,12},{23... | collective-permute-start | bytes 1572872 | tf_op jit(solution)/shard_map/ppermute | solution.py:64
  20.4 12.5 %collective-permute-start.5 = (bf16[1,1,4096,64]{2,3,1,0:T(8,128)(2,1)S(1)}, bf16[1,1,4096,64]{2,3,1,0:T(8,128)(2,1)S(1)}, u32[]{:S(2)}, u32[]{:S(2)}) collective-permute-start(bf16[1,1,4096,64]{2,3,1,0:T(8,128)(2,1)S(1)} %collective-permute-done.3), channel_id=1, source_target_pairs={{8,9},{9,8},{10,11},{11,10},{12,13},{13,12},{14,15},{15,14},{16,17... | collective-permute-start | bytes 1572872 | tf_op jit(solution)/shard_map/ppermute | solution.py:44
  31.4 2.2 %collective-permute-start.8 = (bf16[1,1,4096,64]{2,3,1,0:T(8,128)(2,1)S(1)}, bf16[1,1,4096,64]{2,3,1,0:T(8,128)(2,1)S(1)}, u32[]{:S(2)}, u32[]{:S(2)}) collective-permute-start(bf16[1,1,4096,64]{2,3,1,0:T(8,128)(2,1)S(1)} %collective-permute-done.6), channel_id=1, source_target_pairs={{0,8},{8,0},{16,24},{24,16},{1,9},{9,1},{17,25},{25,17},{2,10},{10... | collective-permute-start | bytes 1572872 | tf_op jit(solution)/shard_map/ppermute | solution.py:25
  35.5 2.7 %collective-permute-start.9 = (f32[32,128]{1,0:T(8,128)S(1)}, f32[32,128]{1,0:T(8,128)S(1)}, u32[]{:S(2)}, u32[]{:S(2)}) collective-permute-start(f32[32,128]{1,0:T(8,128)S(1)} %get-tuple-element.34), channel_id=1, source_target_pairs={{0,8},{1,9},{2,10},{3,11},{4,12},{5,13},{6,14},{7,15},{8,0},{9,1},... | collective-permute-start | bytes 49160 | tf_op jit(solution)/shard_map/ppermute | solution.py:313
  38.3 5.7 %collective-permute-start.10 = (f32[32,128]{1,0:T(8,128)S(1)}, f32[32,128]{1,0:T(8,128)S(1)}, u32[]{:S(2)}, u32[]{:S(2)}) collective-permute-start(f32[32,128]{1,0:T(8,128)S(1)} %add.21), channel_id=1, source_target_pairs={{0,16},{1,17},{2,18},{3,19},{4,20},{5,21},{6,22},{7,23},{8,24},{9,... | collective-permute-start | bytes 49160 | tf_op jit(solution)/shard_map/ppermute | solution.py:313
  38.7 6.5 %collective-permute-start.11 = (f32[32,128]{1,0:T(8,128)S(1)}, f32[32,128]{1,0:T(8,128)S(1)}, u32[]{:S(2)}, u32[]{:S(2)}) collective-permute-start(f32[32,128]{1,0:T(8,128)S(1)} %add.21), channel_id=1, source_target_pairs={{0,1},{1,0},{2,3},{3,2},{4,5},{5,4},{6,7},{7,6},{8,9},{9,8},{10,11... | collective-permute-start | bytes 49160 | tf_op jit(solution)/shard_map/ppermute | solution.py:313
  43.5 4.6 %collective-permute-start.12 = (f32[32,128]{1,0:T(8,128)S(1)}, f32[32,128]{1,0:T(8,128)S(1)}, u32[]{:S(2)}, u32[]{:S(2)}) collective-permute-start(f32[32,128]{1,0:T(8,128)S(1)} %add.21), channel_id=1, source_target_pairs={{0,17},{1,16},{2,19},{3,18},{4,21},{5,20},{6,23},{7,22},{8,25},{9,... | collective-permute-start | bytes 49160 | tf_op jit(solution)/shard_map/ppermute | solution.py:313
  48.2 4.5 %collective-permute-start.13 = (f32[32,128]{1,0:T(8,128)S(1)}, f32[32,128]{1,0:T(8,128)S(1)}, u32[]{:S(2)}, u32[]{:S(2)}) collective-permute-start(f32[32,128]{1,0:T(8,128)S(1)} %add_add_fusion.1), channel_id=1, source_target_pairs={{0,2},{1,3},{2,0},{3,1},{4,6},{5,7},{6,4},{7,5},{8,10},{9,11},{10,... | collective-permute-start | bytes 49160 | tf_op jit(solution)/shard_map/ppermute | solution.py:313
  49.8 4.7 %collective-permute-start.14 = (f32[32,128]{1,0:T(8,128)S(1)}, f32[32,128]{1,0:T(8,128)S(1)}, u32[]{:S(2)}, u32[]{:S(2)}) collective-permute-start(f32[32,128]{1,0:T(8,128)S(1)} %add_add_fusion.1), channel_id=1, source_target_pairs={{0,4},{1,5},{2,6},{3,7},{4,0},{5,1},{6,2},{7,3},{8,12},{9,13},{10,... | collective-permute-start | bytes 49160 | tf_op jit(solution)/shard_map/ppermute | solution.py:313
  50.9 5.5 %collective-permute-start.15 = (f32[32,128]{1,0:T(8,128)S(1)}, f32[32,128]{1,0:T(8,128)S(1)}, u32[]{:S(2)}, u32[]{:S(2)}) collective-permute-start(f32[32,128]{1,0:T(8,128)S(1)} %add_add_fusion.1), channel_id=1, source_target_pairs={{0,6},{1,7},{2,4},{3,5},{4,2},{5,3},{6,0},{7,1},{8,14},{9,15},{10,... | collective-permute-start | bytes 49160 | tf_op jit(solution)/shard_map/ppermute | solution.py:313

commit v6 on v5

--- a/solution.py
+++ b/solution.py
@@ -215,18 +215,21 @@
         pltpu.make_async_copy(near_hbm.at[pl.ds(chunk * length, length)], held, sems.at[chunk]).wait()
         return carry
 
-    def step(index, there):
+    def step(pair, there):
         groups = 128 // UNROLL
+        index = 2 * pair + 1
         last = work[LIST_ROWS + lax.div(index, groups), lax.rem(index, groups) * UNROLL + UNROLL - 2]
         needed = jnp.where(index >= count - 1, CHUNKS, lax.div(lax.shift_right_logical(last, 9), length) + 1)
         lax.fori_loop(there, needed, wait, 0)
         products = []
-        for half, near in enumerate((near_0, near_1)):
-            products += products_of(0, half, work, index, near, acc, rows)
+        for place in (index - 1, index):
+            for half, near in enumerate((near_0, near_1)):
+                products += products_of(0, half, work, place, near, acc, rows)
         add_all(products, acc)
         return jnp.maximum(there, needed)
 
-    there = lax.fori_loop(0, jnp.maximum(batches(0, 0, work), count), step, jnp.int32(AHEAD))
+    pairs = lax.div(jnp.maximum(batches(0, 0, work), count) + 1, 2)
+    there = lax.fori_loop(0, pairs, step, jnp.int32(AHEAD))
     lax.fori_loop(there, CHUNKS, wait, 0)
 
 
@@ -307,7 +310,8 @@
     gx_count, gy_count = lax.axis_size("gx"), lax.axis_size("gy")
     total = gx_count * gy_count
     bits = [gy_count * 2**i for i in range(1, gx_count.bit_length() - 1)]
-    bits = bits[:1] + [2**i for i in range(gy_count.bit_length() - 1)] + bits[1:]
+    along = [2**i for i in range(gy_count.bit_length() - 1)]
+    bits = bits[:1] + along[1:2] + along[:1] + along[2:] + bits[1:]
 
     def from_other(mask):
         return lax.ppermute(value, ("gx", "gy"), [(i, i ^ mask) for i in range(total)])

time: 60.3 us -> 60 us (level)
  Pallas kernels: 19.7 us -> 18.9 us
  waiting for transfers between devices: 12.6 us -> 13.3 us
    ppermute x7, starting transfers between devices: 12 us -> 12.9 us  [from_other(): lax.ppermute(value, ('gx', 'gy'), [(i, i ^ mask) for i in range(total)])]
    ppermute x1, waiting for transfers between devices: 2.08 us -> 2.9 us  [pass_on(): return lax.ppermute(value, axis, pairs)]
    pallas_call x1, Pallas kernels: 8.25 us -> 7.43 us  [shards(): pl.pallas_call(early_kernel, out_shape=(near_half, acc_shape), in_specs=[...]
    ppermute x4, starting transfers between devices: 7.22 us -> 6.52 us  [pair_swap(): return lax.ppermute(value, axis, [(i, i ^ 1) for i in range(size)])]
  transfers between devices with their start and end apart: 16 -> 16, of which waited for: 8 -> 8; matrix products, arithmetic and copies ran while one was open for 1% -> 1% of each run, Pallas kernels for 25% -> 23%
where the time goes in v6:
time: 60 us; the launch traced here: 59.7 us
  starting transfers between devices  26 us (43%)
  Pallas kernels  18.9 us (31%)
  waiting for transfers between devices  13.3 us (22%)
  between operations  0.76 us (1%)
  local copies, waits for them, and re-layouts  0.72 us (1%)
    ppermute x7, starting transfers between devices, from_other(): lax.ppermute(value, ('gx', 'gy'), [(i, i ^ mask) for i in range(total)])  12.9 us
    ppermute x7, waiting for transfers between devices, from_other(): lax.ppermute(value, ('gx', 'gy'), [(i, i ^ mask) for i in range(total)])  8.44 us
    pallas_call x1, Pallas kernels, shards(): pl.pallas_call(early_kernel, out_shape=(near_half, acc_shape), in_specs=[...  7.43 us
    ppermute x4, starting transfers between devices, pair_swap(): return lax.ppermute(value, axis, [(i, i ^ 1) for i in range(size)])  6.52 us
    pallas_call x1, Pallas kernels, shards(): pl.pallas_call(functools.partial(load_kernel, tiles_dev, gy_count), out_s...  5.69 us
    ppermute x1, starting transfers between devices, pass_on(): return lax.ppermute(value, axis, pairs)  3.87 us
    pallas_call x1, Pallas kernels, shards(): pl.pallas_call(functools.partial(finish_kernel, scale), out_shape=(jax.Sh...  3.14 us
    ppermute x1, waiting for transfers between devices, pass_on(): return lax.ppermute(value, axis, pairs)  2.9 us
  transfers between devices with their start and end apart: 16, of which 8 were waited for; matrix products, arithmetic and copies ran while one was open for 1% of the time, Pallas kernels for 23%

profile of v6, /device:TPU:0, one launch (start us, length us, event | category | flops | bytes accessed | tf_op | source)
XLA Modules:
  0.0 59.7 jit_solution(7241612961961596955)
XLA Ops:
  0.6 3.0 %collective-permute-start = (bf16[1,1,4096,64]{2,3,1,0:T(8,128)(2,1)}, bf16[1,1,4096,64]{2,3,1,0:T(8,128)(2,1)S(1)}, u32[]{:S(2)}, u32[]{:S(2)}) collective-permute-start(bf16[1,1,4096,64]{2,3,1,0:T(8,128)(2,1)} %param.4), channel_id=1, source_target_pairs={{0,1},{1,0},{2,3},{3,2},{4,5},{5,4},{6,7},{7,6},{8,9},{9,8},{10,11... | collective-permute-start | bytes 1572872 | tf_op jit(solution)/shard_map/ppermute | solution.py:25
  3.6 0.7 %collective-permute-start.1 = (bf16[1,1,4096,64]{2,3,1,0:T(8,128)(2,1)}, bf16[1,1,4096,64]{2,3,1,0:T(8,128)(2,1)S(1)}, u32[]{:S(2)}, u32[]{:S(2)}) collective-permute-start(bf16[1,1,4096,64]{2,3,1,0:T(8,128)(2,1)} %param.4), channel_id=1, source_target_pairs={{9,11},{11,13},{13,15},{10,8},{12,10},{14,12},{17,19},{19,21},{21,... | collective-permute-start | bytes 1572872 | tf_op jit(solution)/shard_map/ppermute | solution.py:54
  4.3 0.7 %collective-permute-start.3 = (bf16[1,1,4096,64]{2,3,1,0:T(8,128)(2,1)}, bf16[1,1,4096,64]{2,3,1,0:T(8,128)(2,1)S(1)}, u32[]{:S(2)}, u32[]{:S(2)}) collective-permute-start(bf16[1,1,4096,64]{2,3,1,0:T(8,128)(2,1)} %param.4), channel_id=1, source_target_pairs={{8,16},{16,8},{9,17},{17,9},{10,18},{18,10},{11,19},{19,11},{12,20... | collective-permute-start | bytes 1572872 | tf_op jit(solution)/shard_map/ppermute | solution.py:29
  5.0 3.5 %collective-permute-start.2 = (bf16[1,1,4096,64]{2,3,1,0:T(8,128)(2,1)}, bf16[1,1,4096,64]{2,3,1,0:T(8,128)(2,1)S(1)}, u32[]{:S(2)}, u32[]{:S(2)}) collective-permute-start(bf16[1,1,4096,64]{2,3,1,0:T(8,128)(2,1)} %param.4), channel_id=1, source_target_pairs={{0,8},{8,0},{16,24},{24,16},{1,9},{9,1},{17,25},{25,17},{2,10},{10... | collective-permute-start | bytes 1572872 | tf_op jit(solution)/shard_map/ppermute | solution.py:25
  8.5 0.7 %copy.10 = s32[1,1,32,20]{2,3,1,0:T(8,128)S(1)} copy(s32[1,1,32,20]{2,1,3,0:T(1,128)} %param.5) | data formatting | bytes 5120
  9.3 0.0 copy-start
  9.3 5.7 %load.1 = (bf16[320,128,128]{2,1,0:T(8,128)(2,1)S(1)}, bf16[320,128,128]{2,1,0:T(8,128)(2,1)S(1)}, s32[24,128]{1,0:T(8,128)S(1)}) custom-call(s32[20,1,32]{2,1,0:T(1,128)S(1)} %reshape.13.links, bf16[640,128,128]{2,1,0:T(8,128)(2,1)} %bitcast.45), custom_call_target="tpu_custom_call" | custom-call | tf_op jit(solution)/shard_map/load/pallas_call | solution.py:357
  15.0 0.8 %collective-permute-done = bf16[1,1,4096,64]{2,3,1,0:T(8,128)(2,1)S(1)} collective-permute-done((bf16[1,1,4096,64]{2,3,1,0:T(8,128)(2,1)}, bf16[1,1,4096,64]{2,3,1,0:T(8,128)(2,1)S(1)}, u32[]{:S(2)}, u32[]{:S(2)}) %collective-permute-start) | collective-permute-done | bytes 524320 | tf_op jit(solution)/shard_map/ppermute | solution.py:25
  15.8 0.0 collective-permute-done.1
  15.8 3.9 %collective-permute-start.6 = (bf16[1,1,4096,64]{2,3,1,0:T(8,128)(2,1)S(1)}, bf16[1,1,4096,64]{2,3,1,0:T(8,128)(2,1)S(1)}, u32[]{:S(2)}, u32[]{:S(2)}) collective-permute-start(bf16[1,1,4096,64]{2,3,1,0:T(8,128)(2,1)S(1)} %collective-permute-done), channel_id=1, source_target_pairs={{0,2},{2,4},{4,6},{3,1},{5,3},{7,5},{8,10},{10,12},{12,14},{11,9},... | collective-permute-start | bytes 1572872 | tf_op jit(solution)/shard_map/ppermute | solution.py:38
  19.7 0.7 %collective-permute-start.7 = (bf16[1,1,4096,64]{2,3,1,0:T(8,128)(2,1)S(1)}, bf16[1,1,4096,64]{2,3,1,0:T(8,128)(2,1)S(1)}, u32[]{:S(2)}, u32[]{:S(2)}) collective-permute-start(bf16[1,1,4096,64]{2,3,1,0:T(8,128)(2,1)S(1)} %collective-permute-done.1), channel_id=1, source_target_pairs={{11,18},{13,20},{15,22},{8,17},{10,19},{12,21},{19,10},{21,12},{23... | collective-permute-start | bytes 1572872 | tf_op jit(solution)/shard_map/ppermute | solution.py:64
  20.4 0.0 collective-permute-done.3
  20.4 0.7 %collective-permute-start.5 = (bf16[1,1,4096,64]{2,3,1,0:T(8,128)(2,1)S(1)}, bf16[1,1,4096,64]{2,3,1,0:T(8,128)(2,1)S(1)}, u32[]{:S(2)}, u32[]{:S(2)}) collective-permute-start(bf16[1,1,4096,64]{2,3,1,0:T(8,128)(2,1)S(1)} %collective-permute-done.3), channel_id=1, source_target_pairs={{8,9},{9,8},{10,11},{11,10},{12,13},{13,12},{14,15},{15,14},{16,17... | collective-permute-start | bytes 1572872 | tf_op jit(solution)/shard_map/ppermute | solution.py:44
  21.1 0.0 collective-permute-done.4
  21.1 7.4 %early_rows.1 = (bf16[320,128,128]{2,1,0:T(8,128)(2,1)S(1)}, f32[32,128,64]{2,1,0:T(8,128)S(1)}) custom-call(s32[24,128]{1,0:T(8,128)S(1)} %get-tuple-element.21.work_in, bf16[640,128,128]{2,1,0:T(8,128)(2,1)} %bitcast.46, bf16[320,128,128]{2,1,0:T(8,128)(2,1)S(1)} %get-tuple-element.22.near_0, ...), custom_call_target="tpu_custom_call", output_to_operand_aliasing={{0}: (3, {})} | custom-call | tf_op jit(solution)/shard_map/early_rows/pallas_call | solution.py:370
  28.5 2.9 %collective-permute-done.6 = bf16[1,1,4096,64]{2,3,1,0:T(8,128)(2,1)S(1)} collective-permute-done((bf16[1,1,4096,64]{2,3,1,0:T(8,128)(2,1)S(1)}, bf16[1,1,4096,64]{2,3,1,0:T(8,128)(2,1)S(1)}, u32[]{:S(2)}, u32[]{:S(2)}) %collective-permute-start.6) | collective-permute-done | bytes 524320 | tf_op jit(solution)/shard_map/ppermute | solution.py:38
  31.4 0.0 collective-permute-done.7
  31.4 0.8 %next_rows.1.acc_in = f32[32,128,64]{2,1,0:T(8,128)S(1)} custom-call(s32[24,128]{1,0:T(8,128)S(1)} %get-tuple-element.21.work_in, bf16[320,128,128]{2,1,0:T(8,128)(2,1)S(1)} %get-tuple-element.22.near_0, bf16[320,128,128]{2,1,0:T(8,128)(2,1)S(1)} %get-tuple-element.25.near_1, bf16[64,4096]{1,0:T(8,128)(2,1)S(1)} %bitcast.41, ...), custom_call_target="tpu_custom_call", output_to_operand_aliasing={{}: (5, {})} | custom-call | tf_op jit(solution)/shard_map/next_rows/pallas_call | solution.py:379
  32.2 1.1 %collective-permute-done.8 = bf16[1,1,4096,64]{2,3,1,0:T(8,128)(2,1)S(1)} collective-permute-done((bf16[1,1,4096,64]{2,3,1,0:T(8,128)(2,1)S(1)}, bf16[1,1,4096,64]{2,3,1,0:T(8,128)(2,1)S(1)}, u32[]{:S(2)}, u32[]{:S(2)}) %collective-permute-start.8) | collective-permute-done | bytes 524320 | tf_op jit(solution)/shard_map/ppermute | solution.py:25
  33.3 1.9 %last_rows_and_gram.1 = (bf16[128,4096]{1,0:T(8,128)(2,1)S(1)}, f32[32,128]{1,0:T(8,128)S(1)}, f32[32,128,64]{2,1,0:T(8,128)S(1)}) custom-call(s32[24,128]{1,0:T(8,128)S(1)} %get-tuple-element.21.work_in, bf16[320,128,128]{2,1,0:T(8,128)(2,1)S(1)} %get-tuple-element.22.near_0, ...), custom_call_target="tpu_custom_call", output_to_operand_aliasing={{2}: (5, {})} | custom-call | tf_op jit(solution)/shard_map/last_rows_and_gram/pallas_call | solution.py:385
  35.2 1.7 %collective-permute-start.9 = (f32[32,128]{1,0:T(8,128)S(1)}, f32[32,128]{1,0:T(8,128)S(1)}, u32[]{:S(2)}, u32[]{:S(2)}) collective-permute-start(f32[32,128]{1,0:T(8,128)S(1)} %get-tuple-element.34), channel_id=1, source_target_pairs={{0,8},{1,9},{2,10},{3,11},{4,12},{5,13},{6,14},{7,15},{8,0},{9,1},... | collective-permute-start | bytes 49160 | tf_op jit(solution)/shard_map/ppermute | solution.py:317
  36.9 0.8 %collective-permute-done.9 = f32[32,128]{1,0:T(8,128)S(1)} collective-permute-done((f32[32,128]{1,0:T(8,128)S(1)}, f32[32,128]{1,0:T(8,128)S(1)}, u32[]{:S(2)}, u32[]{:S(2)}) %collective-permute-start.9) | collective-permute-done | bytes 16416 | tf_op jit(solution)/shard_map/ppermute | solution.py:317
  37.7 1.7 %collective-permute-start.10 = (f32[32,128]{1,0:T(8,128)S(1)}, f32[32,128]{1,0:T(8,128)S(1)}, u32[]{:S(2)}, u32[]{:S(2)}) collective-permute-start(f32[32,128]{1,0:T(8,128)S(1)} %add.21), channel_id=1, source_target_pairs={{0,16},{1,17},{2,18},{3,19},{4,20},{5,21},{6,22},{7,23},{8,24},{9,... | collective-permute-start | bytes 49160 | tf_op jit(solution)/shard_map/ppermute | solution.py:317
  39.5 5.0 %collective-permute-start.11 = (f32[32,128]{1,0:T(8,128)S(1)}, f32[32,128]{1,0:T(8,128)S(1)}, u32[]{:S(2)}, u32[]{:S(2)}) collective-permute-start(f32[32,128]{1,0:T(8,128)S(1)} %add.21), channel_id=1, source_target_pairs={{0,2},{1,3},{2,0},{3,1},{4,6},{5,7},{6,4},{7,5},{8,10},{9,11},{10,... | collective-permute-start | bytes 49160 | tf_op jit(solution)/shard_map/ppermute | solution.py:317
  44.5 1.7 %collective-permute-done.11 = f32[32,128]{1,0:T(8,128)S(1)} collective-permute-done((f32[32,128]{1,0:T(8,128)S(1)}, f32[32,128]{1,0:T(8,128)S(1)}, u32[]{:S(2)}, u32[]{:S(2)}) %collective-permute-start.11) | collective-permute-done | bytes 16416 | tf_op jit(solution)/shard_map/ppermute | solution.py:317
  46.2 2.9 %collective-permute-done.12 = f32[32,128]{1,0:T(8,128)S(1)} collective-permute-done((f32[32,128]{1,0:T(8,128)S(1)}, f32[32,128]{1,0:T(8,128)S(1)}, u32[]{:S(2)}, u32[]{:S(2)}) %collective-permute-start.12) | collective-permute-done | bytes 16416 | tf_op jit(solution)/shard_map/ppermute | solution.py:317
  49.1 0.7 %collective-permute-start.13 = (f32[32,128]{1,0:T(8,128)S(1)}, f32[32,128]{1,0:T(8,128)S(1)}, u32[]{:S(2)}, u32[]{:S(2)}) collective-permute-start(f32[32,128]{1,0:T(8,128)S(1)} %add_add_fusion.1), channel_id=1, source_target_pairs={{0,1},{1,0},{2,3},{3,2},{4,5},{5,4},{6,7},{7,6},{8,9},{9,8},{10,11... | collective-permute-start | bytes 49160 | tf_op jit(solution)/shard_map/ppermute | solution.py:317
  49.8 1.2 %collective-permute-start.14 = (f32[32,128]{1,0:T(8,128)S(1)}, f32[32,128]{1,0:T(8,128)S(1)}, u32[]{:S(2)}, u32[]{:S(2)}) collective-permute-start(f32[32,128]{1,0:T(8,128)S(1)} %add_add_fusion.1), channel_id=1, source_target_pairs={{0,4},{1,5},{2,6},{3,7},{4,0},{5,1},{6,2},{7,3},{8,12},{9,13},{10,... | collective-permute-start | bytes 49160 | tf_op jit(solution)/shard_map/ppermute | solution.py:317
  51.0 2.6 %collective-permute-start.15 = (f32[32,128]{1,0:T(8,128)S(1)}, f32[32,128]{1,0:T(8,128)S(1)}, u32[]{:S(2)}, u32[]{:S(2)}) collective-permute-start(f32[32,128]{1,0:T(8,128)S(1)} %add_add_fusion.1), channel_id=1, source_target_pairs={{0,5},{1,4},{2,7},{3,6},{4,1},{5,0},{6,3},{7,2},{8,13},{9,12},{10,... | collective-permute-start | bytes 49160 | tf_op jit(solution)/shard_map/ppermute | solution.py:317
  53.6 1.0 %collective-permute-done.14 = f32[32,128]{1,0:T(8,128)S(1)} collective-permute-done((f32[32,128]{1,0:T(8,128)S(1)}, f32[32,128]{1,0:T(8,128)S(1)}, u32[]{:S(2)}, u32[]{:S(2)}) %collective-permute-start.14) | collective-permute-done | bytes 16416 | tf_op jit(solution)/shard_map/ppermute | solution.py:317
  54.5 2.0 %collective-permute-done.15 = f32[32,128]{1,0:T(8,128)S(1)} collective-permute-done((f32[32,128]{1,0:T(8,128)S(1)}, f32[32,128]{1,0:T(8,128)S(1)}, u32[]{:S(2)}, u32[]{:S(2)}) %collective-permute-start.15) | collective-permute-done | bytes 16416 | tf_op jit(solution)/shard_map/ppermute | solution.py:317
  56.5 3.1 %orthonormalize.1 = (f32[64,4096]{1,0:T(8,128)}, f32[64,64]{1,0:T(8,128)}) custom-call(f32[32,128]{1,0:T(8,128)S(1)} %add_add_fusion.gram, bf16[128,4096]{1,0:T(8,128)(2,1)S(1)} %get-tuple-element.35.split), custom_call_target="tpu_custom_call" | custom-call | tf_op jit(solution)/shard_map/orthonormalize/pallas_call | solution.py:397
  (12 shorter events, 0.1 us)
Async XLA Ops:
  0.6 15.1 %collective-permute-start = (bf16[1,1,4096,64]{2,3,1,0:T(8,128)(2,1)}, bf16[1,1,4096,64]{2,3,1,0:T(8,128)(2,1)S(1)}, u32[]{:S(2)}, u32[]{:S(2)}) collective-permute-start(bf16[1,1,4096,64]{2,3,1,0:T(8,128)(2,1)} %param.4), channel_id=1, source_target_pairs={{0,1},{1,0},{2,3},{3,2},{4,5},{5,4},{6,7},{7,6},{8,9},{9,8},{10,11... | collective-permute-start | bytes 1572872 | tf_op jit(solution)/shard_map/ppermute | solution.py:25
  3.6 12.1 %collective-permute-start.1 = (bf16[1,1,4096,64]{2,3,1,0:T(8,128)(2,1)}, bf16[1,1,4096,64]{2,3,1,0:T(8,128)(2,1)S(1)}, u32[]{:S(2)}, u32[]{:S(2)}) collective-permute-start(bf16[1,1,4096,64]{2,3,1,0:T(8,128)(2,1)} %param.4), channel_id=1, source_target_pairs={{9,11},{11,13},{13,15},{10,8},{12,10},{14,12},{17,19},{19,21},{21,... | collective-permute-start | bytes 1572872 | tf_op jit(solution)/shard_map/ppermute | solution.py:54
  4.3 16.0 %collective-permute-start.3 = (bf16[1,1,4096,64]{2,3,1,0:T(8,128)(2,1)}, bf16[1,1,4096,64]{2,3,1,0:T(8,128)(2,1)S(1)}, u32[]{:S(2)}, u32[]{:S(2)}) collective-permute-start(bf16[1,1,4096,64]{2,3,1,0:T(8,128)(2,1)} %param.4), channel_id=1, source_target_pairs={{8,16},{16,8},{9,17},{17,9},{10,18},{18,10},{11,19},{19,11},{12,20... | collective-permute-start | bytes 1572872 | tf_op jit(solution)/shard_map/ppermute | solution.py:29
  5.0 16.0 %collective-permute-start.2 = (bf16[1,1,4096,64]{2,3,1,0:T(8,128)(2,1)}, bf16[1,1,4096,64]{2,3,1,0:T(8,128)(2,1)S(1)}, u32[]{:S(2)}, u32[]{:S(2)}) collective-permute-start(bf16[1,1,4096,64]{2,3,1,0:T(8,128)(2,1)} %param.4), channel_id=1, source_target_pairs={{0,8},{8,0},{16,24},{24,16},{1,9},{9,1},{17,25},{25,17},{2,10},{10... | collective-permute-start | bytes 1572872 | tf_op jit(solution)/shard_map/ppermute | solution.py:25
  9.3 11.8 %copy-start = (bf16[1,1,4096,64]{2,3,1,0:T(8,128)(2,1)S(1)}, bf16[1,1,4096,64]{2,3,1,0:T(8,128)(2,1)}, u32[]{:S(2)}) copy-start(bf16[1,1,4096,64]{2,3,1,0:T(8,128)(2,1)} %param.4) | copy-start | bytes 1572868
  15.8 5.3 %collective-permute-start.4 = (bf16[1,1,4096,64]{2,3,1,0:T(8,128)(2,1)S(1)}, bf16[1,1,4096,64]{2,3,1,0:T(8,128)(2,1)S(1)}, u32[]{:S(2)}, u32[]{:S(2)}) collective-permute-start(bf16[1,1,4096,64]{2,3,1,0:T(8,128)(2,1)S(1)} %collective-permute-done), channel_id=1, source_target_pairs={{0,8},{8,0},{16,24},{24,16},{1,9},{9,1},{17,25},{25,17},{2,10},{10... | collective-permute-start | bytes 1572872 | tf_op jit(solution)/shard_map/ppermute | solution.py:25
  15.8 15.7 %collective-permute-start.6 = (bf16[1,1,4096,64]{2,3,1,0:T(8,128)(2,1)S(1)}, bf16[1,1,4096,64]{2,3,1,0:T(8,128)(2,1)S(1)}, u32[]{:S(2)}, u32[]{:S(2)}) collective-permute-start(bf16[1,1,4096,64]{2,3,1,0:T(8,128)(2,1)S(1)} %collective-permute-done), channel_id=1, source_target_pairs={{0,2},{2,4},{4,6},{3,1},{5,3},{7,5},{8,10},{10,12},{12,14},{11,9},... | collective-permute-start | bytes 1572872 | tf_op jit(solution)/shard_map/ppermute | solution.py:38
  19.7 11.8 %collective-permute-start.7 = (bf16[1,1,4096,64]{2,3,1,0:T(8,128)(2,1)S(1)}, bf16[1,1,4096,64]{2,3,1,0:T(8,128)(2,1)S(1)}, u32[]{:S(2)}, u32[]{:S(2)}) collective-permute-start(bf16[1,1,4096,64]{2,3,1,0:T(8,128)(2,1)S(1)} %collective-permute-done.1), channel_id=1, source_target_pairs={{11,18},{13,20},{15,22},{8,17},{10,19},{12,21},{19,10},{21,12},{23... | collective-permute-start | bytes 1572872 | tf_op jit(solution)/shard_map/ppermute | solution.py:64
  20.4 11.8 %collective-permute-start.5 = (bf16[1,1,4096,64]{2,3,1,0:T(8,128)(2,1)S(1)}, bf16[1,1,4096,64]{2,3,1,0:T(8,128)(2,1)S(1)}, u32[]{:S(2)}, u32[]{:S(2)}) collective-permute-start(bf16[1,1,4096,64]{2,3,1,0:T(8,128)(2,1)S(1)} %collective-permute-done.3), channel_id=1, source_target_pairs={{8,9},{9,8},{10,11},{11,10},{12,13},{13,12},{14,15},{15,14},{16,17... | collective-permute-start | bytes 1572872 | tf_op jit(solution)/shard_map/ppermute | solution.py:44
  31.4 1.9 %collective-permute-start.8 = (bf16[1,1,4096,64]{2,3,1,0:T(8,128)(2,1)S(1)}, bf16[1,1,4096,64]{2,3,1,0:T(8,128)(2,1)S(1)}, u32[]{:S(2)}, u32[]{:S(2)}) collective-permute-start(bf16[1,1,4096,64]{2,3,1,0:T(8,128)(2,1)S(1)} %collective-permute-done.6), channel_id=1, source_target_pairs={{0,8},{8,0},{16,24},{24,16},{1,9},{9,1},{17,25},{25,17},{2,10},{10... | collective-permute-start | bytes 1572872 | tf_op jit(solution)/shard_map/ppermute | solution.py:25
  35.2 2.5 %collective-permute-start.9 = (f32[32,128]{1,0:T(8,128)S(1)}, f32[32,128]{1,0:T(8,128)S(1)}, u32[]{:S(2)}, u32[]{:S(2)}) collective-permute-start(f32[32,128]{1,0:T(8,128)S(1)} %get-tuple-element.34), channel_id=1, source_target_pairs={{0,8},{1,9},{2,10},{3,11},{4,12},{5,13},{6,14},{7,15},{8,0},{9,1},... | collective-permute-start | bytes 49160 | tf_op jit(solution)/shard_map/ppermute | solution.py:317
  37.7 6.7 %collective-permute-start.10 = (f32[32,128]{1,0:T(8,128)S(1)}, f32[32,128]{1,0:T(8,128)S(1)}, u32[]{:S(2)}, u32[]{:S(2)}) collective-permute-start(f32[32,128]{1,0:T(8,128)S(1)} %add.21), channel_id=1, source_target_pairs={{0,16},{1,17},{2,18},{3,19},{4,20},{5,21},{6,22},{7,23},{8,24},{9,... | collective-permute-start | bytes 49160 | tf_op jit(solution)/shard_map/ppermute | solution.py:317
  39.5 6.7 %collective-permute-start.11 = (f32[32,128]{1,0:T(8,128)S(1)}, f32[32,128]{1,0:T(8,128)S(1)}, u32[]{:S(2)}, u32[]{:S(2)}) collective-permute-start(f32[32,128]{1,0:T(8,128)S(1)} %add.21), channel_id=1, source_target_pairs={{0,2},{1,3},{2,0},{3,1},{4,6},{5,7},{6,4},{7,5},{8,10},{9,11},{10,... | collective-permute-start | bytes 49160 | tf_op jit(solution)/shard_map/ppermute | solution.py:317
  44.5 4.6 %collective-permute-start.12 = (f32[32,128]{1,0:T(8,128)S(1)}, f32[32,128]{1,0:T(8,128)S(1)}, u32[]{:S(2)}, u32[]{:S(2)}) collective-permute-start(f32[32,128]{1,0:T(8,128)S(1)} %add.21), channel_id=1, source_target_pairs={{0,18},{1,19},{2,16},{3,17},{4,22},{5,23},{6,20},{7,21},{8,26},{9,... | collective-permute-start | bytes 49160 | tf_op jit(solution)/shard_map/ppermute | solution.py:317
  49.1 4.5 %collective-permute-start.13 = (f32[32,128]{1,0:T(8,128)S(1)}, f32[32,128]{1,0:T(8,128)S(1)}, u32[]{:S(2)}, u32[]{:S(2)}) collective-permute-start(f32[32,128]{1,0:T(8,128)S(1)} %add_add_fusion.1), channel_id=1, source_target_pairs={{0,1},{1,0},{2,3},{3,2},{4,5},{5,4},{6,7},{7,6},{8,9},{9,8},{10,11... | collective-permute-start | bytes 49160 | tf_op jit(solution)/shard_map/ppermute | solution.py:317
  49.8 4.7 %collective-permute-start.14 = (f32[32,128]{1,0:T(8,128)S(1)}, f32[32,128]{1,0:T(8,128)S(1)}, u32[]{:S(2)}, u32[]{:S(2)}) collective-permute-start(f32[32,128]{1,0:T(8,128)S(1)} %add_add_fusion.1), channel_id=1, source_target_pairs={{0,4},{1,5},{2,6},{3,7},{4,0},{5,1},{6,2},{7,3},{8,12},{9,13},{10,... | collective-permute-start | bytes 49160 | tf_op jit(solution)/shard_map/ppermute | solution.py:317
  51.0 5.5 %collective-permute-start.15 = (f32[32,128]{1,0:T(8,128)S(1)}, f32[32,128]{1,0:T(8,128)S(1)}, u32[]{:S(2)}, u32[]{:S(2)}) collective-permute-start(f32[32,128]{1,0:T(8,128)S(1)} %add_add_fusion.1), channel_id=1, source_target_pairs={{0,5},{1,4},{2,7},{3,6},{4,1},{5,0},{6,3},{7,2},{8,13},{9,12},{10,... | collective-permute-start | bytes 49160 | tf_op jit(solution)/shard_map/ppermute | solution.py:317

commit v7 on v5

--- a/solution.py
+++ b/solution.py
@@ -11,7 +11,7 @@
 PARTS = 3
 HALVES = 2
 CHUNKS = 4
-AHEAD = 2
+AHEAD = 1
 LIST_ROWS = 3
 LINES = PARTS * HALVES * LIST_ROWS + 6
 PART_OF = (0, 0, 0, 0, 0, 2, 1, 2, 1)

time: 60.3 us -> 59.9 us (level)
  waiting for transfers between devices: 12.6 us -> 13.6 us
  Pallas kernels: 19.7 us -> 19 us
    ppermute x4, waiting for transfers between devices: 1.57 us -> 2.32 us  [pair_swap(): return lax.ppermute(value, axis, [(i, i ^ 1) for i in range(size)])]
    pallas_call x1, Pallas kernels: 5.69 us -> 4.94 us  [shards(): pl.pallas_call(functools.partial(load_kernel, tiles_dev, gy_count), out_s...]
  transfers between devices with their start and end apart: 16 -> 16, of which waited for: 8 -> 8; matrix products, arithmetic and copies ran while one was open for 1% -> 1% of each run, Pallas kernels for 25% -> 23%
where the time goes in v7:
time: 59.9 us; the launch traced here: 59.6 us
  starting transfers between devices  25.5 us (43%)
  Pallas kernels  19 us (32%)
  waiting for transfers between devices  13.6 us (23%)
  between operations  0.76 us (1%)
  local copies, waits for them, and re-layouts  0.72 us (1%)
    ppermute x7, starting transfers between devices, from_other(): lax.ppermute(value, ('gx', 'gy'), [(i, i ^ mask) for i in range(total)])  11.7 us
    ppermute x7, waiting for transfers between devices, from_other(): lax.ppermute(value, ('gx', 'gy'), [(i, i ^ mask) for i in range(total)])  9.19 us
    pallas_call x1, Pallas kernels, shards(): pl.pallas_call(early_kernel, out_shape=(near_half, acc_shape), in_specs=[...  8.26 us
    ppermute x4, starting transfers between devices, pair_swap(): return lax.ppermute(value, axis, [(i, i ^ 1) for i in range(size)])  7.32 us
    pallas_call x1, Pallas kernels, shards(): pl.pallas_call(functools.partial(load_kernel, tiles_dev, gy_count), out_s...  4.94 us
    ppermute x1, starting transfers between devices, pass_on(): return lax.ppermute(value, axis, pairs)  3.75 us
    pallas_call x1, Pallas kernels, shards(): pl.pallas_call(functools.partial(finish_kernel, scale), out_shape=(jax.Sh...  3.14 us
    ppermute x4, waiting for transfers between devices, pair_swap(): return lax.ppermute(value, axis, [(i, i ^ 1) for i in range(size)])  2.32 us
  transfers between devices with their start and end apart: 16, of which 8 were waited for; matrix products, arithmetic and copies ran while one was open for 1% of the time, Pallas kernels for 23%

profile of v7, /device:TPU:0, one launch (start us, length us, event | category | flops | bytes accessed | tf_op | source)
XLA Modules:
  0.0 59.6 jit_solution(9741884895166156969)
XLA Ops:
  0.6 3.0 %collective-permute-start = (bf16[1,1,4096,64]{2,3,1,0:T(8,128)(2,1)}, bf16[1,1,4096,64]{2,3,1,0:T(8,128)(2,1)S(1)}, u32[]{:S(2)}, u32[]{:S(2)}) collective-permute-start(bf16[1,1,4096,64]{2,3,1,0:T(8,128)(2,1)} %param.4), channel_id=1, source_target_pairs={{0,1},{1,0},{2,3},{3,2},{4,5},{5,4},{6,7},{7,6},{8,9},{9,8},{10,11... | collective-permute-start | bytes 1572872 | tf_op jit(solution)/shard_map/ppermute | solution.py:25
  3.6 0.7 %collective-permute-start.1 = (bf16[1,1,4096,64]{2,3,1,0:T(8,128)(2,1)}, bf16[1,1,4096,64]{2,3,1,0:T(8,128)(2,1)S(1)}, u32[]{:S(2)}, u32[]{:S(2)}) collective-permute-start(bf16[1,1,4096,64]{2,3,1,0:T(8,128)(2,1)} %param.4), channel_id=1, source_target_pairs={{9,11},{11,13},{13,15},{10,8},{12,10},{14,12},{17,19},{19,21},{21,... | collective-permute-start | bytes 1572872 | tf_op jit(solution)/shard_map/ppermute | solution.py:54
  4.3 0.7 %collective-permute-start.3 = (bf16[1,1,4096,64]{2,3,1,0:T(8,128)(2,1)}, bf16[1,1,4096,64]{2,3,1,0:T(8,128)(2,1)S(1)}, u32[]{:S(2)}, u32[]{:S(2)}) collective-permute-start(bf16[1,1,4096,64]{2,3,1,0:T(8,128)(2,1)} %param.4), channel_id=1, source_target_pairs={{8,16},{16,8},{9,17},{17,9},{10,18},{18,10},{11,19},{19,11},{12,20... | collective-permute-start | bytes 1572872 | tf_op jit(solution)/shard_map/ppermute | solution.py:29
  5.0 3.5 %collective-permute-start.2 = (bf16[1,1,4096,64]{2,3,1,0:T(8,128)(2,1)}, bf16[1,1,4096,64]{2,3,1,0:T(8,128)(2,1)S(1)}, u32[]{:S(2)}, u32[]{:S(2)}) collective-permute-start(bf16[1,1,4096,64]{2,3,1,0:T(8,128)(2,1)} %param.4), channel_id=1, source_target_pairs={{0,8},{8,0},{16,24},{24,16},{1,9},{9,1},{17,25},{25,17},{2,10},{10... | collective-permute-start | bytes 1572872 | tf_op jit(solution)/shard_map/ppermute | solution.py:25
  8.5 0.7 %copy.10 = s32[1,1,32,20]{2,3,1,0:T(8,128)S(1)} copy(s32[1,1,32,20]{2,1,3,0:T(1,128)} %param.5) | data formatting | bytes 5120
  9.3 0.0 copy-start
  9.3 4.9 %load.1 = (bf16[320,128,128]{2,1,0:T(8,128)(2,1)S(1)}, bf16[320,128,128]{2,1,0:T(8,128)(2,1)S(1)}, s32[24,128]{1,0:T(8,128)S(1)}) custom-call(s32[20,1,32]{2,1,0:T(1,128)S(1)} %reshape.13.links, bf16[640,128,128]{2,1,0:T(8,128)(2,1)} %bitcast.45), custom_call_target="tpu_custom_call" | custom-call | tf_op jit(solution)/shard_map/load/pallas_call | solution.py:353
  14.2 1.6 %collective-permute-done = bf16[1,1,4096,64]{2,3,1,0:T(8,128)(2,1)S(1)} collective-permute-done((bf16[1,1,4096,64]{2,3,1,0:T(8,128)(2,1)}, bf16[1,1,4096,64]{2,3,1,0:T(8,128)(2,1)S(1)}, u32[]{:S(2)}, u32[]{:S(2)}) %collective-permute-start) | collective-permute-done | bytes 524320 | tf_op jit(solution)/shard_map/ppermute | solution.py:25
  15.8 3.8 %collective-permute-start.6 = (bf16[1,1,4096,64]{2,3,1,0:T(8,128)(2,1)S(1)}, bf16[1,1,4096,64]{2,3,1,0:T(8,128)(2,1)S(1)}, u32[]{:S(2)}, u32[]{:S(2)}) collective-permute-start(bf16[1,1,4096,64]{2,3,1,0:T(8,128)(2,1)S(1)} %collective-permute-done), channel_id=1, source_target_pairs={{0,2},{2,4},{4,6},{3,1},{5,3},{7,5},{8,10},{10,12},{12,14},{11,9},... | collective-permute-start | bytes 1572872 | tf_op jit(solution)/shard_map/ppermute | solution.py:38
  19.5 0.7 %collective-permute-start.7 = (bf16[1,1,4096,64]{2,3,1,0:T(8,128)(2,1)S(1)}, bf16[1,1,4096,64]{2,3,1,0:T(8,128)(2,1)S(1)}, u32[]{:S(2)}, u32[]{:S(2)}) collective-permute-start(bf16[1,1,4096,64]{2,3,1,0:T(8,128)(2,1)S(1)} %collective-permute-done.1), channel_id=1, source_target_pairs={{11,18},{13,20},{15,22},{8,17},{10,19},{12,21},{19,10},{21,12},{23... | collective-permute-start | bytes 1572872 | tf_op jit(solution)/shard_map/ppermute | solution.py:64
  20.2 0.7 %collective-permute-start.5 = (bf16[1,1,4096,64]{2,3,1,0:T(8,128)(2,1)S(1)}, bf16[1,1,4096,64]{2,3,1,0:T(8,128)(2,1)S(1)}, u32[]{:S(2)}, u32[]{:S(2)}) collective-permute-start(bf16[1,1,4096,64]{2,3,1,0:T(8,128)(2,1)S(1)} %collective-permute-done.3), channel_id=1, source_target_pairs={{8,9},{9,8},{10,11},{11,10},{12,13},{13,12},{14,15},{15,14},{16,17... | collective-permute-start | bytes 1572872 | tf_op jit(solution)/shard_map/ppermute | solution.py:44
  20.9 0.0 collective-permute-done.2
  21.0 0.0 collective-permute-done.4
  21.0 8.3 %early_rows.1 = (bf16[320,128,128]{2,1,0:T(8,128)(2,1)S(1)}, f32[32,128,64]{2,1,0:T(8,128)S(1)}) custom-call(s32[24,128]{1,0:T(8,128)S(1)} %get-tuple-element.21.work_in, bf16[640,128,128]{2,1,0:T(8,128)(2,1)} %bitcast.46, bf16[320,128,128]{2,1,0:T(8,128)(2,1)S(1)} %get-tuple-element.22.near_0, ...), custom_call_target="tpu_custom_call", output_to_operand_aliasing={{0}: (3, {})} | custom-call | tf_op jit(solution)/shard_map/early_rows/pallas_call | solution.py:366
  29.2 2.1 %collective-permute-done.6 = bf16[1,1,4096,64]{2,3,1,0:T(8,128)(2,1)S(1)} collective-permute-done((bf16[1,1,4096,64]{2,3,1,0:T(8,128)(2,1)S(1)}, bf16[1,1,4096,64]{2,3,1,0:T(8,128)(2,1)S(1)}, u32[]{:S(2)}, u32[]{:S(2)}) %collective-permute-start.6) | collective-permute-done | bytes 524320 | tf_op jit(solution)/shard_map/ppermute | solution.py:38
  31.3 0.8 %collective-permute-start.8 = (bf16[1,1,4096,64]{2,3,1,0:T(8,128)(2,1)S(1)}, bf16[1,1,4096,64]{2,3,1,0:T(8,128)(2,1)S(1)}, u32[]{:S(2)}, u32[]{:S(2)}) collective-permute-start(bf16[1,1,4096,64]{2,3,1,0:T(8,128)(2,1)S(1)} %collective-permute-done.6), channel_id=1, source_target_pairs={{0,8},{8,0},{16,24},{24,16},{1,9},{9,1},{17,25},{25,17},{2,10},{10... | collective-permute-start | bytes 1572872 | tf_op jit(solution)/shard_map/ppermute | solution.py:25
  32.1 0.8 %next_rows.1.acc_in = f32[32,128,64]{2,1,0:T(8,128)S(1)} custom-call(s32[24,128]{1,0:T(8,128)S(1)} %get-tuple-element.21.work_in, bf16[320,128,128]{2,1,0:T(8,128)(2,1)S(1)} %get-tuple-element.22.near_0, bf16[320,128,128]{2,1,0:T(8,128)(2,1)S(1)} %get-tuple-element.25.near_1, bf16[64,4096]{1,0:T(8,128)(2,1)S(1)} %bitcast.41, ...), custom_call_target="tpu_custom_call", output_to_operand_aliasing={{}: (5, {})} | custom-call | tf_op jit(solution)/shard_map/next_rows/pallas_call | solution.py:375
  32.9 0.8 %collective-permute-done.8 = bf16[1,1,4096,64]{2,3,1,0:T(8,128)(2,1)S(1)} collective-permute-done((bf16[1,1,4096,64]{2,3,1,0:T(8,128)(2,1)S(1)}, bf16[1,1,4096,64]{2,3,1,0:T(8,128)(2,1)S(1)}, u32[]{:S(2)}, u32[]{:S(2)}) %collective-permute-start.8) | collective-permute-done | bytes 524320 | tf_op jit(solution)/shard_map/ppermute | solution.py:25
  33.7 1.8 %last_rows_and_gram.1 = (bf16[128,4096]{1,0:T(8,128)(2,1)S(1)}, f32[32,128]{1,0:T(8,128)S(1)}, f32[32,128,64]{2,1,0:T(8,128)S(1)}) custom-call(s32[24,128]{1,0:T(8,128)S(1)} %get-tuple-element.21.work_in, bf16[320,128,128]{2,1,0:T(8,128)(2,1)S(1)} %get-tuple-element.22.near_0, ...), custom_call_target="tpu_custom_call", output_to_operand_aliasing={{2}: (5, {})} | custom-call | tf_op jit(solution)/shard_map/last_rows_and_gram/pallas_call | solution.py:381
  35.5 1.9 %collective-permute-start.9 = (f32[32,128]{1,0:T(8,128)S(1)}, f32[32,128]{1,0:T(8,128)S(1)}, u32[]{:S(2)}, u32[]{:S(2)}) collective-permute-start(f32[32,128]{1,0:T(8,128)S(1)} %get-tuple-element.34), channel_id=1, source_target_pairs={{0,8},{1,9},{2,10},{3,11},{4,12},{5,13},{6,14},{7,15},{8,0},{9,1},... | collective-permute-start | bytes 49160 | tf_op jit(solution)/shard_map/ppermute | solution.py:313
  37.4 0.8 %collective-permute-done.9 = f32[32,128]{1,0:T(8,128)S(1)} collective-permute-done((f32[32,128]{1,0:T(8,128)S(1)}, f32[32,128]{1,0:T(8,128)S(1)}, u32[]{:S(2)}, u32[]{:S(2)}) %collective-permute-start.9) | collective-permute-done | bytes 16416 | tf_op jit(solution)/shard_map/ppermute | solution.py:313
  38.3 1.1 %collective-permute-start.10 = (f32[32,128]{1,0:T(8,128)S(1)}, f32[32,128]{1,0:T(8,128)S(1)}, u32[]{:S(2)}, u32[]{:S(2)}) collective-permute-start(f32[32,128]{1,0:T(8,128)S(1)} %add.21), channel_id=1, source_target_pairs={{0,16},{1,17},{2,18},{3,19},{4,20},{5,21},{6,22},{7,23},{8,24},{9,... | collective-permute-start | bytes 49160 | tf_op jit(solution)/shard_map/ppermute | solution.py:313
  39.3 4.2 %collective-permute-start.11 = (f32[32,128]{1,0:T(8,128)S(1)}, f32[32,128]{1,0:T(8,128)S(1)}, u32[]{:S(2)}, u32[]{:S(2)}) collective-permute-start(f32[32,128]{1,0:T(8,128)S(1)} %add.21), channel_id=1, source_target_pairs={{0,1},{1,0},{2,3},{3,2},{4,5},{5,4},{6,7},{7,6},{8,9},{9,8},{10,11... | collective-permute-start | bytes 49160 | tf_op jit(solution)/shard_map/ppermute | solution.py:313
  43.5 0.1 collective-permute-start.12
  43.6 1.6 %collective-permute-done.11 = f32[32,128]{1,0:T(8,128)S(1)} collective-permute-done((f32[32,128]{1,0:T(8,128)S(1)}, f32[32,128]{1,0:T(8,128)S(1)}, u32[]{:S(2)}, u32[]{:S(2)}) %collective-permute-start.11) | collective-permute-done | bytes 16416 | tf_op jit(solution)/shard_map/ppermute | solution.py:313
  45.2 2.9 %collective-permute-done.12 = f32[32,128]{1,0:T(8,128)S(1)} collective-permute-done((f32[32,128]{1,0:T(8,128)S(1)}, f32[32,128]{1,0:T(8,128)S(1)}, u32[]{:S(2)}, u32[]{:S(2)}) %collective-permute-start.12) | collective-permute-done | bytes 16416 | tf_op jit(solution)/shard_map/ppermute | solution.py:313
  48.2 1.6 %collective-permute-start.13 = (f32[32,128]{1,0:T(8,128)S(1)}, f32[32,128]{1,0:T(8,128)S(1)}, u32[]{:S(2)}, u32[]{:S(2)}) collective-permute-start(f32[32,128]{1,0:T(8,128)S(1)} %add_add_fusion.1), channel_id=1, source_target_pairs={{0,2},{1,3},{2,0},{3,1},{4,6},{5,7},{6,4},{7,5},{8,10},{9,11},{10,... | collective-permute-start | bytes 49160 | tf_op jit(solution)/shard_map/ppermute | solution.py:313
  49.8 1.1 %collective-permute-start.14 = (f32[32,128]{1,0:T(8,128)S(1)}, f32[32,128]{1,0:T(8,128)S(1)}, u32[]{:S(2)}, u32[]{:S(2)}) collective-permute-start(f32[32,128]{1,0:T(8,128)S(1)} %add_add_fusion.1), channel_id=1, source_target_pairs={{0,4},{1,5},{2,6},{3,7},{4,0},{5,1},{6,2},{7,3},{8,12},{9,13},{10,... | collective-permute-start | bytes 49160 | tf_op jit(solution)/shard_map/ppermute | solution.py:313
  50.9 1.7 %collective-permute-start.15 = (f32[32,128]{1,0:T(8,128)S(1)}, f32[32,128]{1,0:T(8,128)S(1)}, u32[]{:S(2)}, u32[]{:S(2)}) collective-permute-start(f32[32,128]{1,0:T(8,128)S(1)} %add_add_fusion.1), channel_id=1, source_target_pairs={{0,6},{1,7},{2,4},{3,5},{4,2},{5,3},{6,0},{7,1},{8,14},{9,15},{10,... | collective-permute-start | bytes 49160 | tf_op jit(solution)/shard_map/ppermute | solution.py:313
  52.6 1.9 %collective-permute-done.14 = f32[32,128]{1,0:T(8,128)S(1)} collective-permute-done((f32[32,128]{1,0:T(8,128)S(1)}, f32[32,128]{1,0:T(8,128)S(1)}, u32[]{:S(2)}, u32[]{:S(2)}) %collective-permute-start.14) | collective-permute-done | bytes 16416 | tf_op jit(solution)/shard_map/ppermute | solution.py:313
  54.5 1.9 %collective-permute-done.15 = f32[32,128]{1,0:T(8,128)S(1)} collective-permute-done((f32[32,128]{1,0:T(8,128)S(1)}, f32[32,128]{1,0:T(8,128)S(1)}, u32[]{:S(2)}, u32[]{:S(2)}) %collective-permute-start.15) | collective-permute-done | bytes 16416 | tf_op jit(solution)/shard_map/ppermute | solution.py:313
  56.5 3.1 %orthonormalize.1 = (f32[64,4096]{1,0:T(8,128)}, f32[64,64]{1,0:T(8,128)}) custom-call(f32[32,128]{1,0:T(8,128)S(1)} %add_add_fusion.gram, bf16[128,4096]{1,0:T(8,128)(2,1)S(1)} %get-tuple-element.35.split), custom_call_target="tpu_custom_call" | custom-call | tf_op jit(solution)/shard_map/orthonormalize/pallas_call | solution.py:393
  (12 shorter events, 0.0 us)
Async XLA Ops:
  0.6 15.1 %collective-permute-start = (bf16[1,1,4096,64]{2,3,1,0:T(8,128)(2,1)}, bf16[1,1,4096,64]{2,3,1,0:T(8,128)(2,1)S(1)}, u32[]{:S(2)}, u32[]{:S(2)}) collective-permute-start(bf16[1,1,4096,64]{2,3,1,0:T(8,128)(2,1)} %param.4), channel_id=1, source_target_pairs={{0,1},{1,0},{2,3},{3,2},{4,5},{5,4},{6,7},{7,6},{8,9},{9,8},{10,11... | collective-permute-start | bytes 1572872 | tf_op jit(solution)/shard_map/ppermute | solution.py:25
  3.6 12.1 %collective-permute-start.1 = (bf16[1,1,4096,64]{2,3,1,0:T(8,128)(2,1)}, bf16[1,1,4096,64]{2,3,1,0:T(8,128)(2,1)S(1)}, u32[]{:S(2)}, u32[]{:S(2)}) collective-permute-start(bf16[1,1,4096,64]{2,3,1,0:T(8,128)(2,1)} %param.4), channel_id=1, source_target_pairs={{9,11},{11,13},{13,15},{10,8},{12,10},{14,12},{17,19},{19,21},{21,... | collective-permute-start | bytes 1572872 | tf_op jit(solution)/shard_map/ppermute | solution.py:54
  4.3 15.9 %collective-permute-start.3 = (bf16[1,1,4096,64]{2,3,1,0:T(8,128)(2,1)}, bf16[1,1,4096,64]{2,3,1,0:T(8,128)(2,1)S(1)}, u32[]{:S(2)}, u32[]{:S(2)}) collective-permute-start(bf16[1,1,4096,64]{2,3,1,0:T(8,128)(2,1)} %param.4), channel_id=1, source_target_pairs={{8,16},{16,8},{9,17},{17,9},{10,18},{18,10},{11,19},{19,11},{12,20... | collective-permute-start | bytes 1572872 | tf_op jit(solution)/shard_map/ppermute | solution.py:29
  5.0 15.9 %collective-permute-start.2 = (bf16[1,1,4096,64]{2,3,1,0:T(8,128)(2,1)}, bf16[1,1,4096,64]{2,3,1,0:T(8,128)(2,1)S(1)}, u32[]{:S(2)}, u32[]{:S(2)}) collective-permute-start(bf16[1,1,4096,64]{2,3,1,0:T(8,128)(2,1)} %param.4), channel_id=1, source_target_pairs={{0,8},{8,0},{16,24},{24,16},{1,9},{9,1},{17,25},{25,17},{2,10},{10... | collective-permute-start | bytes 1572872 | tf_op jit(solution)/shard_map/ppermute | solution.py:25
  9.3 11.7 %copy-start = (bf16[1,1,4096,64]{2,3,1,0:T(8,128)(2,1)S(1)}, bf16[1,1,4096,64]{2,3,1,0:T(8,128)(2,1)}, u32[]{:S(2)}) copy-start(bf16[1,1,4096,64]{2,3,1,0:T(8,128)(2,1)} %param.4) | copy-start | bytes 1572868
  15.8 5.2 %collective-permute-start.4 = (bf16[1,1,4096,64]{2,3,1,0:T(8,128)(2,1)S(1)}, bf16[1,1,4096,64]{2,3,1,0:T(8,128)(2,1)S(1)}, u32[]{:S(2)}, u32[]{:S(2)}) collective-permute-start(bf16[1,1,4096,64]{2,3,1,0:T(8,128)(2,1)S(1)} %collective-permute-done), channel_id=1, source_target_pairs={{0,8},{8,0},{16,24},{24,16},{1,9},{9,1},{17,25},{25,17},{2,10},{10... | collective-permute-start | bytes 1572872 | tf_op jit(solution)/shard_map/ppermute | solution.py:25
  15.8 15.6 %collective-permute-start.6 = (bf16[1,1,4096,64]{2,3,1,0:T(8,128)(2,1)S(1)}, bf16[1,1,4096,64]{2,3,1,0:T(8,128)(2,1)S(1)}, u32[]{:S(2)}, u32[]{:S(2)}) collective-permute-start(bf16[1,1,4096,64]{2,3,1,0:T(8,128)(2,1)S(1)} %collective-permute-done), channel_id=1, source_target_pairs={{0,2},{2,4},{4,6},{3,1},{5,3},{7,5},{8,10},{10,12},{12,14},{11,9},... | collective-permute-start | bytes 1572872 | tf_op jit(solution)/shard_map/ppermute | solution.py:38
  19.5 11.8 %collective-permute-start.7 = (bf16[1,1,4096,64]{2,3,1,0:T(8,128)(2,1)S(1)}, bf16[1,1,4096,64]{2,3,1,0:T(8,128)(2,1)S(1)}, u32[]{:S(2)}, u32[]{:S(2)}) collective-permute-start(bf16[1,1,4096,64]{2,3,1,0:T(8,128)(2,1)S(1)} %collective-permute-done.1), channel_id=1, source_target_pairs={{11,18},{13,20},{15,22},{8,17},{10,19},{12,21},{19,10},{21,12},{23... | collective-permute-start | bytes 1572872 | tf_op jit(solution)/shard_map/ppermute | solution.py:64
  20.2 12.7 %collective-permute-start.5 = (bf16[1,1,4096,64]{2,3,1,0:T(8,128)(2,1)S(1)}, bf16[1,1,4096,64]{2,3,1,0:T(8,128)(2,1)S(1)}, u32[]{:S(2)}, u32[]{:S(2)}) collective-permute-start(bf16[1,1,4096,64]{2,3,1,0:T(8,128)(2,1)S(1)} %collective-permute-done.3), channel_id=1, source_target_pairs={{8,9},{9,8},{10,11},{11,10},{12,13},{13,12},{14,15},{15,14},{16,17... | collective-permute-start | bytes 1572872 | tf_op jit(solution)/shard_map/ppermute | solution.py:44
  31.3 2.3 %collective-permute-start.8 = (bf16[1,1,4096,64]{2,3,1,0:T(8,128)(2,1)S(1)}, bf16[1,1,4096,64]{2,3,1,0:T(8,128)(2,1)S(1)}, u32[]{:S(2)}, u32[]{:S(2)}) collective-permute-start(bf16[1,1,4096,64]{2,3,1,0:T(8,128)(2,1)S(1)} %collective-permute-done.6), channel_id=1, source_target_pairs={{0,8},{8,0},{16,24},{24,16},{1,9},{9,1},{17,25},{25,17},{2,10},{10... | collective-permute-start | bytes 1572872 | tf_op jit(solution)/shard_map/ppermute | solution.py:25
  35.5 2.7 %collective-permute-start.9 = (f32[32,128]{1,0:T(8,128)S(1)}, f32[32,128]{1,0:T(8,128)S(1)}, u32[]{:S(2)}, u32[]{:S(2)}) collective-permute-start(f32[32,128]{1,0:T(8,128)S(1)} %get-tuple-element.34), channel_id=1, source_target_pairs={{0,8},{1,9},{2,10},{3,11},{4,12},{5,13},{6,14},{7,15},{8,0},{9,1},... | collective-permute-start | bytes 49160 | tf_op jit(solution)/shard_map/ppermute | solution.py:313
  38.3 5.4 %collective-permute-start.10 = (f32[32,128]{1,0:T(8,128)S(1)}, f32[32,128]{1,0:T(8,128)S(1)}, u32[]{:S(2)}, u32[]{:S(2)}) collective-permute-start(f32[32,128]{1,0:T(8,128)S(1)} %add.21), channel_id=1, source_target_pairs={{0,16},{1,17},{2,18},{3,19},{4,20},{5,21},{6,22},{7,23},{8,24},{9,... | collective-permute-start | bytes 49160 | tf_op jit(solution)/shard_map/ppermute | solution.py:313
  39.3 5.9 %collective-permute-start.11 = (f32[32,128]{1,0:T(8,128)S(1)}, f32[32,128]{1,0:T(8,128)S(1)}, u32[]{:S(2)}, u32[]{:S(2)}) collective-permute-start(f32[32,128]{1,0:T(8,128)S(1)} %add.21), channel_id=1, source_target_pairs={{0,1},{1,0},{2,3},{3,2},{4,5},{5,4},{6,7},{7,6},{8,9},{9,8},{10,11... | collective-permute-start | bytes 49160 | tf_op jit(solution)/shard_map/ppermute | solution.py:313
  43.5 4.6 %collective-permute-start.12 = (f32[32,128]{1,0:T(8,128)S(1)}, f32[32,128]{1,0:T(8,128)S(1)}, u32[]{:S(2)}, u32[]{:S(2)}) collective-permute-start(f32[32,128]{1,0:T(8,128)S(1)} %add.21), channel_id=1, source_target_pairs={{0,17},{1,16},{2,19},{3,18},{4,21},{5,20},{6,23},{7,22},{8,25},{9,... | collective-permute-start | bytes 49160 | tf_op jit(solution)/shard_map/ppermute | solution.py:313
  48.2 4.5 %collective-permute-start.13 = (f32[32,128]{1,0:T(8,128)S(1)}, f32[32,128]{1,0:T(8,128)S(1)}, u32[]{:S(2)}, u32[]{:S(2)}) collective-permute-start(f32[32,128]{1,0:T(8,128)S(1)} %add_add_fusion.1), channel_id=1, source_target_pairs={{0,2},{1,3},{2,0},{3,1},{4,6},{5,7},{6,4},{7,5},{8,10},{9,11},{10,... | collective-permute-start | bytes 49160 | tf_op jit(solution)/shard_map/ppermute | solution.py:313
  49.8 4.7 %collective-permute-start.14 = (f32[32,128]{1,0:T(8,128)S(1)}, f32[32,128]{1,0:T(8,128)S(1)}, u32[]{:S(2)}, u32[]{:S(2)}) collective-permute-start(f32[32,128]{1,0:T(8,128)S(1)} %add_add_fusion.1), channel_id=1, source_target_pairs={{0,4},{1,5},{2,6},{3,7},{4,0},{5,1},{6,2},{7,3},{8,12},{9,13},{10,... | collective-permute-start | bytes 49160 | tf_op jit(solution)/shard_map/ppermute | solution.py:313
  50.9 5.5 %collective-permute-start.15 = (f32[32,128]{1,0:T(8,128)S(1)}, f32[32,128]{1,0:T(8,128)S(1)}, u32[]{:S(2)}, u32[]{:S(2)}) collective-permute-start(f32[32,128]{1,0:T(8,128)S(1)} %add_add_fusion.1), channel_id=1, source_target_pairs={{0,6},{1,7},{2,4},{3,5},{4,2},{5,3},{6,0},{7,1},{8,14},{9,15},{10,... | collective-permute-start | bytes 49160 | tf_op jit(solution)/shard_map/ppermute | solution.py:313
